TPU v7x, 768 devices: a whole 4x8x12 slice. The times are simulated.
768 devices in a mesh: band: 12 (over z), feat: 64 (over x, y, core).
Axes of the slice: x: 4, y: 8, z: 12, core: 2. Of those that a mesh axis runs over, the one named last changes fastest.
Arguments:
- grid_latent: bfloat16 [196608, 512], P(('band', 'feat')), may hold values from -6 to 6
- mesh_latent: bfloat16 [6144, 512], P(('band', 'feat')), may hold values from -6 to 6
- g2m_src: int32 [393216], P(('band', 'feat')), may hold values from 0 to 255
- g2m_peer: int32 [393216, 1], P(('band', 'feat')), may hold values from 0 to 63; in each aligned block of 512 rows (0 to 511, 512 to 1023, ...) at most 16 rows name the same one
- g2m_slot: int32 [393216], P(('band', 'feat')), may hold values from 0 to 7
- proc_src: int32 [196608], P(('band', 'feat')), may hold values from 0 to 23
- proc_dst: int32 [196608], P(('band', 'feat')), may hold values from 0 to 7
- enc_src_w: bfloat16 [512, 512], replicated, may hold values from -0.25 to 0.25
- enc_dst_w: bfloat16 [512, 512], replicated, may hold values from -0.25 to 0.25
- enc_out_w: bfloat16 [512, 512], replicated, may hold values from -0.25 to 0.25
- enc_bias: float32 [512], replicated, may hold values from -3 to 3
- enc_gain: float32 [512], replicated, may hold values from 0.25 to 1.75
- proc_src_w: bfloat16 [512, 512], replicated, may hold values from -0.25 to 0.25
- proc_dst_w: bfloat16 [512, 512], replicated, may hold values from -0.25 to 0.25
- proc_out_w: bfloat16 [512, 512], replicated, may hold values from -0.25 to 0.25
- proc_bias: float32 [512], replicated, may hold values from -3 to 3
- proc_gain: float32 [512], replicated, may hold values from 0.25 to 1.75
- cotangent: bfloat16 [6144, 512], P(('band', 'feat')), may hold values from -6 to 6
Outputs:
- mesh_out: bfloat16 [6144, 512], P(('band', 'feat'))
- grad_grid: bfloat16 [196608, 512], P(('band', 'feat'))
- grad_mesh: bfloat16 [6144, 512], P(('band', 'feat'))
Inputs may be any that keep to these rules, and one draw needn't show every extreme that they name: `g2m_peer`: among the edges of one device at most 16 name the same peer, a bound that some block reaches.
All inputs are finite; a program needn't handle non-finite values.
Results may differ from a plain program's by a relative error of at most 0.015.
Values may be sent and summed in bfloat16 or wider, within the bound.
No kernel may reach another device: no remote copies, remote signals or barrier semaphores. Data moves between devices by JAX's collectives and lax.ppermute only.
A program may use at most 32 MiB of HBM per device.

v0:
```python
import jax
import jax.numpy as jnp
from jax import lax
from jax.sharding import PartitionSpec as P


def with_halo(block, sides, width):
    for axis, dim in sides:
        count = lax.axis_size(axis)
        forward = [(i, i + 1) for i in range(count - 1)]
        backward = [(target, source) for source, target in forward]
        low = lax.ppermute(
            lax.slice_in_dim(block, block.shape[dim] - width, None, axis=dim), axis, forward
        )
        high = lax.ppermute(lax.slice_in_dim(block, 0, width, axis=dim), axis, backward)
        block = jnp.concatenate([low, block, high], axis=dim)
    return block


def layer_norm(values, gain):
    average = jnp.mean(values, axis=-1, keepdims=True)
    centred = values - average
    spread = jnp.mean(centred * centred, axis=-1, keepdims=True)
    inv_std = lax.rsqrt(spread + 1e-05)
    normed = centred * inv_std
    return (normed * gain, normed, inv_std)


def norm_back(normed, inv_std, gain, upstream):
    scaled = upstream * gain
    return inv_std * (
        scaled
        - jnp.mean(scaled, axis=-1, keepdims=True)
        - normed * jnp.mean(scaled * normed, axis=-1, keepdims=True)
    )


def silu_grad(values):
    sigma = jax.nn.sigmoid(values)
    return sigma * (1.0 + values * (1.0 - sigma))


def times_transpose(left, weight):
    return lax.dot_general(
        left, weight, (((1,), (1,)), ((), ())), preferred_element_type=jnp.float32
    )


def node_sum(member, values):
    return jnp.dot(
        member, values, precision=lax.Precision.HIGHEST, preferred_element_type=jnp.float32
    )


def per_device(
    grid_latent,
    mesh_latent,
    g2m_src,
    g2m_peer,
    g2m_slot,
    proc_src,
    proc_dst,
    enc_src_w,
    enc_dst_w,
    enc_out_w,
    enc_bias,
    enc_gain,
    proc_src_w,
    proc_dst_w,
    proc_out_w,
    proc_bias,
    proc_gain,
    cotangent,
):
    peer_count = lax.axis_size("feat")
    edge_count = g2m_src.shape[0]
    node_count = mesh_latent.shape[0]
    latent = grid_latent.shape[1]
    capacity = 2 * edge_count // peer_count
    slot_count = peer_count * capacity
    target = g2m_peer[:, 0]
    choose = (target[:, None] == jnp.arange(peer_count, dtype=jnp.int32)[None, :]).astype(jnp.int32)
    ranked = jnp.sum((jnp.cumsum(choose, axis=0) - 1) * choose, axis=1)
    position = target * capacity + ranked
    out_rows = jnp.zeros((slot_count, latent), jnp.bfloat16).at[position].set(grid_latent[g2m_src])
    out_slot = jnp.full((slot_count,), node_count, jnp.int32).at[position].set(g2m_slot)
    in_rows, in_slot = (
        lax.all_to_all(out_rows, "feat", split_axis=0, concat_axis=0, tiled=True),
        lax.all_to_all(out_slot, "feat", split_axis=0, concat_axis=0, tiled=True),
    )
    filled = in_slot < node_count
    node_ids = jnp.arange(node_count, dtype=jnp.int32)
    member = (in_slot[None, :] == node_ids[:, None]).astype(jnp.float32)
    picked = jnp.minimum(in_slot, node_count - 1)
    dst_proj = jnp.dot(mesh_latent, enc_dst_w, preferred_element_type=jnp.float32)
    enc_pre = (
        jnp.dot(in_rows, enc_src_w, preferred_element_type=jnp.float32)
        + dst_proj[picked]
        + enc_bias
    )
    enc_hid = jax.nn.silu(enc_pre).astype(jnp.bfloat16)
    enc_msg = jnp.dot(enc_hid, enc_out_w, preferred_element_type=jnp.float32)
    enc_agg = node_sum(member, enc_msg)
    enc_norm, enc_hat, enc_inv = layer_norm(enc_agg, enc_gain)
    mesh_mid = (mesh_latent.astype(jnp.float32) + enc_norm).astype(jnp.bfloat16)
    extended = with_halo(mesh_mid, (("band", 0),), node_count)
    src_rows = extended[proc_src]
    pdst_proj = jnp.dot(mesh_mid, proc_dst_w, preferred_element_type=jnp.float32)
    proc_pre = (
        jnp.dot(src_rows, proc_src_w, preferred_element_type=jnp.float32)
        + pdst_proj[proc_dst]
        + proc_bias
    )
    proc_hid = jax.nn.silu(proc_pre).astype(jnp.bfloat16)
    proc_msg = jnp.dot(proc_hid, proc_out_w, preferred_element_type=jnp.float32)
    proc_member = (proc_dst[None, :] == node_ids[:, None]).astype(jnp.float32)
    proc_agg = node_sum(proc_member, proc_msg)
    proc_norm, proc_hat, proc_inv = layer_norm(proc_agg, proc_gain)
    mesh_out = (mesh_mid.astype(jnp.float32) + proc_norm).astype(jnp.bfloat16)
    upstream = cotangent.astype(jnp.float32)
    grad_proc_agg = norm_back(proc_hat, proc_inv, proc_gain, upstream)
    proc_msg_grad = grad_proc_agg[proc_dst].astype(jnp.bfloat16)
    proc_pre_grad = (times_transpose(proc_msg_grad, proc_out_w) * silu_grad(proc_pre)).astype(
        jnp.bfloat16
    )
    sender_grad = times_transpose(proc_pre_grad, proc_src_w)
    receiver_grad = times_transpose(proc_pre_grad, proc_dst_w)
    rim_grad = jnp.zeros((3 * node_count, latent), jnp.float32).at[proc_src].add(sender_grad)
    outer_rims = jnp.concatenate([rim_grad[:node_count], rim_grad[2 * node_count :]], axis=0)
    arrived = with_halo(outer_rims.astype(jnp.bfloat16), (("band", 0),), node_count).astype(
        outer_rims.dtype
    )
    own_rows = (
        rim_grad[node_count : 2 * node_count] + arrived[:node_count] + arrived[3 * node_count :]
    )
    grad_mid = upstream + node_sum(proc_member, receiver_grad) + own_rows
    grad_enc_agg = norm_back(enc_hat, enc_inv, enc_gain, grad_mid)
    enc_msg_grad = (grad_enc_agg[picked] * filled[:, None].astype(jnp.float32)).astype(jnp.bfloat16)
    silu_slope = silu_grad(enc_pre)
    enc_pre_grad = (times_transpose(enc_msg_grad, enc_out_w) * silu_slope).astype(jnp.bfloat16)
    node_grad = times_transpose(enc_pre_grad, enc_dst_w)
    grad_mesh = (grad_mid + node_sum(member, node_grad)).astype(jnp.bfloat16)
    slot_grad = times_transpose(enc_pre_grad, enc_src_w)
    returned = lax.all_to_all(
        slot_grad.astype(jnp.bfloat16), "feat", split_axis=0, concat_axis=0, tiled=True
    ).astype(slot_grad.dtype)
    edge_grad = returned[position]
    grad_grid = (
        jnp.zeros((grid_latent.shape[0], latent), jnp.float32)
        .at[g2m_src]
        .add(edge_grad)
        .astype(jnp.bfloat16)
    )
    return (mesh_out, grad_grid, grad_mesh)


def solution(mesh):
    placed = (
        P(("band", "feat"), None),
        P(("band", "feat"), None),
        P(("band", "feat")),
        P(("band", "feat"), None),
        P(("band", "feat")),
        P(("band", "feat")),
        P(("band", "feat")),
        P(),
        P(),
        P(),
        P(),
        P(),
        P(),
        P(),
        P(),
        P(),
        P(),
        P(("band", "feat"), None),
    )
    return jax.shard_map(
        per_device,
        mesh=mesh,
        in_specs=placed,
        out_specs=(P(("band", "feat"), None), P(("band", "feat"), None), P(("band", "feat"), None)),
        check_vma=False,
    )
```

profile of v0, /device:TPU:517, one launch (start us, length us, event | category | flops | bytes accessed | tf_op | source)
XLA Modules:
  0.0 153.0 jit_solution(17477906873423108696)
XLA Ops:
  0.7 0.8 fusion.16
  1.5 1.2 reduce-window.6
  2.7 0.2 slice_reduce_fusion
  2.9 0.8 fusion.15
  3.7 0.7 compare_select_fusion.1
  4.4 2.6 %scatter_custom_fusion = s32[1024]{0:T(1024)S(1)} fusion(s32[512]{0:T(512)S(1)} %bitcast.58, s32[512]{0:T(512)} %param.22, s32[]{:T(128)} %constant.14.clone.1), kind=kCustom, calls=%fused_computation.91 | custom fusion | bytes 4608 | tf_op jit(solution)/shard_map/scatter | solution.py:86
  7.0 0.7 all_to_all.20
  7.7 11.0 %all-to-all-start = ((s32[64,16,1]{1,2,0:T(1,128)}), s32[64,16,1]{1,2,0:T(1,128)S(1)}, u32[]{:S(2)}, u32[]{:S(2)}) async-start(s32[64,16,1]{1,2,0:T(1,128)} %bitcast.5), calls=%async_computation | async-start | bytes 65536 | tf_op jit(solution)/shard_map/all_to_all | solution.py:89
  18.8 0.7 compare_select_fusion.2
  19.5 7.2 %scatter_custom_fusion.1 = bf16[1024,512]{1,0:T(8,128)(2,1)} fusion(s32[512]{0:T(512)S(1)} %bitcast.59, bf16[256,512]{1,0:T(8,128)(2,1)} %param.18, s32[1024]{0:T(1024)S(1)} %pad_clamp_fusion.3, bf16[]{:T(256)} %constant.19.clone.1), kind=kCustom, calls=%fused_computation.29 | custom fusion | bytes 1049088 | tf_op jit(solution)/shard_map/scatter | solution.py:85
  26.7 10.5 %all-to-all-start.1 = ((bf16[64,16,512]{2,1,0:T(8,128)(2,1)}), bf16[64,16,512]{2,1,0:T(8,128)(2,1)}, u32[]{:S(2)}, u32[]{:S(2)}) async-start(bf16[64,16,512]{2,1,0:T(8,128)(2,1)} %bitcast.6), calls=%async_computation.1 | async-start | bytes 2097152 | tf_op jit(solution)/shard_map/all_to_all | solution.py:88
  37.5 0.5 broadcast.226
  38.0 0.8 fusion.37
  39.0 3.5 %gather_fusion = f32[1024,512]{1,0:T(8,128)S(1)} fusion(f32[8,512]{1,0:T(8,128)S(1)} %fusion.41, s32[1024]{0:T(1024)S(1)} %broadcast_clamp_fusion), kind=kCustom, calls=%fused_computation.1 | custom fusion | bytes 4198400 | tf_op jit(solution)/shard_map/gather | solution.py:98
  42.5 23.0 %all-to-all-done.1 = bf16[64,16,512]{2,1,0:T(8,128)(2,1)} async-done(((bf16[64,16,512]{2,1,0:T(8,128)(2,1)}), bf16[64,16,512]{2,1,0:T(8,128)(2,1)}, u32[]{:S(2)}, u32[]{:S(2)}) %all-to-all-start.1) | async-done | bytes 1048608 | tf_op jit(solution)/shard_map/all_to_all | solution.py:88
  65.5 2.1 %add_add_fusion = f32[1024,512]{1,0:T(8,128)S(1)} fusion(f32[1024,512]{1,0:T(8,128)S(1)} %gather_fusion, bf16[1024,512]{1,0:T(8,128)(2,1)} %bitcast.7, bf16[512,512]{1,0:T(8,128)(2,1)} %param.25, f32[512]{0:T(512)S(1)} %copy-done.13), kind=kOutput, calls=%fused_computation.15 | convolution fusion | flops 537919488 | bytes 5769216 | tf_op jit(solution)/shard_map/dot_general | solution.py:97
  67.6 0.7 fusion.6
  68.3 0.6 copy-done.2
  69.0 0.9 fusion.39
  70.2 3.4 %collective-permute-start.1 = (bf16[8,512]{1,0:T(8,128)(2,1)S(1)}, bf16[8,512]{1,0:T(8,128)(2,1)S(1)}, u32[]{:S(2)}, u32[]{:S(2)}) collective-permute-start(bf16[8,512]{1,0:T(8,128)(2,1)S(1)} %add_convert_fusion.1), channel_id=1, source_target_pairs={{64,0},{128,64},{192,128},{256,192},{320,256},{384,320},{448,384},... | collective-permute-start | bytes 24584 | tf_op jit(solution)/shard_map/ppermute | solution.py:15
  73.5 2.1 %collective-permute-start = (bf16[8,512]{1,0:T(8,128)(2,1)S(1)}, bf16[8,512]{1,0:T(8,128)(2,1)S(1)}, u32[]{:S(2)}, u32[]{:S(2)}) collective-permute-start(bf16[8,512]{1,0:T(8,128)(2,1)S(1)} %add_convert_fusion.1), channel_id=1, source_target_pairs={{0,64},{64,128},{128,192},{192,256},{256,320},{320,384},{384,448},... | collective-permute-start | bytes 24584 | tf_op jit(solution)/shard_map/ppermute | solution.py:12
  75.8 1.0 gather_fusion.2
  76.8 2.3 %collective-permute-done = bf16[8,512]{1,0:T(8,128)(2,1)S(1)} collective-permute-done((bf16[8,512]{1,0:T(8,128)(2,1)S(1)}, bf16[8,512]{1,0:T(8,128)(2,1)S(1)}, u32[]{:S(2)}, u32[]{:S(2)}) %collective-permute-start) | collective-permute-done | bytes 8224 | tf_op jit(solution)/shard_map/ppermute | solution.py:12
  79.1 1.2 gather_fusion.1
  80.3 0.3 fusion
  80.7 1.4 fusion.10
  82.0 0.4 fusion.40
  82.7 0.8 fusion.22
  83.6 1.2 gather_fusion.3
  84.7 1.4 fusion.1
  86.2 0.3 fusion.44
  86.5 2.1 %scatter_custom_fusion.2 = f32[24,512]{1,0:T(8,128)S(1)} fusion(s32[256]{0:T(256)S(1)} %compare_select_fusion.4, f32[256,512]{1,0:T(8,128)S(1)} %fusion.44, f32[]{:T(128)} %constant.46.clone.1), kind=kCustom, calls=%fused_computation.50 | custom fusion | flops 131072 | bytes 49156 | tf_op jit(solution)/shard_map/scatter-add | solution.py:128
  88.6 2.3 %collective-permute-start.3 = (bf16[8,512]{1,0:T(8,128)(2,1)S(1)}, bf16[8,512]{1,0:T(8,128)(2,1)S(1)}, u32[]{:S(2)}, u32[]{:S(2)}) collective-permute-start(bf16[8,512]{1,0:T(8,128)(2,1)S(1)} %get-tuple-element.10), channel_id=1, source_target_pairs={{64,0},{128,64},{192,128},{256,192},{320,256},{384,320},{448,384},... | collective-permute-start | bytes 24584 | tf_op jit(solution)/shard_map/ppermute | solution.py:15
  90.9 3.0 %collective-permute-start.2 = (bf16[8,512]{1,0:T(8,128)(2,1)S(1)}, bf16[8,512]{1,0:T(8,128)(2,1)S(1)}, u32[]{:S(2)}, u32[]{:S(2)}) collective-permute-start(bf16[8,512]{1,0:T(8,128)(2,1)S(1)} %get-tuple-element.9), channel_id=1, source_target_pairs={{0,64},{64,128},{128,192},{192,256},{256,320},{320,384},{384,448},... | collective-permute-start | bytes 24584 | tf_op jit(solution)/shard_map/ppermute | solution.py:12
  93.9 0.3 fusion.43
  94.3 2.3 %collective-permute-done.2 = bf16[8,512]{1,0:T(8,128)(2,1)S(1)} collective-permute-done((bf16[8,512]{1,0:T(8,128)(2,1)S(1)}, bf16[8,512]{1,0:T(8,128)(2,1)S(1)}, u32[]{:S(2)}, u32[]{:S(2)}) %collective-permute-start.2) | collective-permute-done | bytes 8224 | tf_op jit(solution)/shard_map/ppermute | solution.py:12
  96.5 0.4 multiply_reduce_fusion.3
  97.0 3.5 %gather_fusion.4 = f32[1024,512]{1,0:T(8,128)S(1)} fusion(f32[8,512]{1,0:T(8,128)S(1)} %subtract_multiply_fusion, s32[1024]{0:T(1024)S(1)} %broadcast_clamp_fusion), kind=kCustom, calls=%fused_computation.5 | custom fusion | bytes 4198400 | tf_op jit(solution)/shard_map/gather | solution.py:138
  100.6 2.8 %multiply_convert_fusion = bf16[1024,512]{1,0:T(8,128)(2,1)S(1)} fusion(f32[1024,512]{1,0:T(8,128)} %copy-done.2, bf16[512,512]{1,0:T(8,128)(2,1)S(1)} %copy-done, f32[1024,512]{1,0:T(8,128)S(1)} %gather_fusion.4, f32[1024]{0:T(1024)S(1)} %compare_convert_fusion), kind=kOutput, calls=%fused_computation.11 | convolution fusion | flops 542638080 | bytes 5771264 | tf_op jit(solution)/shard_map/dot_general | solution.py:44
  103.4 1.0 copy-done.5
  104.4 1.7 %convolution_convert_fusion = bf16[1024,512]{1,0:T(8,128)(2,1)} fusion(bf16[1024,512]{1,0:T(8,128)(2,1)S(1)} %multiply_convert_fusion, bf16[512,512]{1,0:T(8,128)(2,1)S(1)} %copy-done.7), kind=kOutput, calls=%fused_computation.16 | convolution fusion | flops 537395200 | bytes 2621440 | tf_op jit(solution)/shard_map/dot_general | solution.py:44
  106.2 8.7 %all-to-all-start.2 = ((bf16[64,16,512]{2,1,0:T(8,128)(2,1)}), bf16[64,16,512]{2,1,0:T(8,128)(2,1)S(1)}, u32[]{:S(2)}, u32[]{:S(2)}) async-start(bf16[64,16,512]{2,1,0:T(8,128)(2,1)} %bitcast.53), calls=%async_computation.2 | async-start | bytes 2097152 | tf_op jit(solution)/shard_map/all_to_all | solution.py:144
  114.9 0.7 fusion.45
  115.6 1.4 fusion.2
  117.0 26.2 %all-to-all-done.2 = bf16[64,16,512]{2,1,0:T(8,128)(2,1)S(1)} async-done(((bf16[64,16,512]{2,1,0:T(8,128)(2,1)}), bf16[64,16,512]{2,1,0:T(8,128)(2,1)S(1)}, u32[]{:S(2)}, u32[]{:S(2)}) %all-to-all-start.2) | async-done | bytes 1048608 | tf_op jit(solution)/shard_map/all_to_all | solution.py:144
  143.3 1.7 %bitcast_convert_fusion = f32[1024,512]{1,0:T(8,128)} fusion(bf16[64,16,512]{2,1,0:T(8,128)(2,1)S(1)} %all-to-all-done.2), kind=kLoop, calls=%fused_computation.24 | loop fusion | flops 524288 | bytes 3145728 | tf_op jit(solution)/shard_map/convert_element_type | solution.py:146
  145.0 7.2 %scatter_custom_fusion.3 = f32[256,512]{1,0:T(8,128)S(1)} fusion(s32[512]{0:T(512)S(1)} %compare_select_fusion.2, f32[1024,512]{1,0:T(8,128)} %bitcast_convert_fusion, s32[1024]{0:T(1024)S(1)} %pad_clamp_fusion, f32[]{:T(128)} %constant.46.clone.1), kind=kCustom, calls=%fused_computation.25 | custom fusion | flops 262144 | bytes 524800 | tf_op jit(solution)/shard_map/scatter-add | solution.py:151
  152.2 0.7 convert_element_type.84
  (63 shorter events, 1.3 us)
Async XLA Ops:
  0.6 67.0 %copy-start = (bf16[512,512]{1,0:T(8,128)(2,1)S(1)}, bf16[512,512]{1,0:T(8,128)(2,1)}, u32[]{:S(2)}) copy-start(bf16[512,512]{1,0:T(8,128)(2,1)} %param.27) | copy-start | bytes 1572868
  0.6 36.5 %copy-start.11 = (s32[256]{0:T(256)S(1)}, s32[256]{0:T(256)}, u32[]{:S(2)}) copy-start(s32[256]{0:T(256)} %param.24) | copy-start | bytes 3076
  0.7 36.6 %copy-start.15 = (s32[256]{0:T(256)S(1)}, s32[256]{0:T(256)}, u32[]{:S(2)}) copy-start(s32[256]{0:T(256)} %param.23) | copy-start | bytes 3076
  0.7 36.6 %copy-start.9 = (bf16[8,512]{1,0:T(8,128)(2,1)S(1)}, bf16[8,512]{1,0:T(8,128)(2,1)}, u32[]{:S(2)}) copy-start(bf16[8,512]{1,0:T(8,128)(2,1)} %param.19) | copy-start | bytes 24580
  0.7 36.6 %copy-start.1 = (bf16[512,512]{1,0:T(8,128)(2,1)S(1)}, bf16[512,512]{1,0:T(8,128)(2,1)}, u32[]{:S(2)}) copy-start(bf16[512,512]{1,0:T(8,128)(2,1)} %param.26) | copy-start | bytes 1572868
  7.7 18.9 %all-to-all-start = ((s32[64,16,1]{1,2,0:T(1,128)}), s32[64,16,1]{1,2,0:T(1,128)S(1)}, u32[]{:S(2)}, u32[]{:S(2)}) async-start(s32[64,16,1]{1,2,0:T(1,128)} %bitcast.5), calls=%async_computation | async-start | bytes 65536 | tf_op jit(solution)/shard_map/all_to_all | solution.py:89
  26.7 38.8 %all-to-all-start.1 = ((bf16[64,16,512]{2,1,0:T(8,128)(2,1)}), bf16[64,16,512]{2,1,0:T(8,128)(2,1)}, u32[]{:S(2)}, u32[]{:S(2)}) async-start(bf16[64,16,512]{2,1,0:T(8,128)(2,1)} %bitcast.6), calls=%async_computation.1 | async-start | bytes 2097152 | tf_op jit(solution)/shard_map/all_to_all | solution.py:88
  39.0 26.5 %copy-start.13 = (f32[512]{0:T(512)S(1)}, f32[512]{0:T(512)}, u32[]{:S(2)}) copy-start(f32[512]{0:T(512)} %param.28) | copy-start | bytes 6148
  67.6 1.4 copy-start.2
  69.0 1.1 copy-start.10
  69.0 6.7 %copy-start.3 = (bf16[512,512]{1,0:T(8,128)(2,1)S(1)}, bf16[512,512]{1,0:T(8,128)(2,1)}, u32[]{:S(2)}) copy-start(bf16[512,512]{1,0:T(8,128)(2,1)} %param.31) | copy-start | bytes 1572868
  70.2 6.7 %collective-permute-start.1 = (bf16[8,512]{1,0:T(8,128)(2,1)S(1)}, bf16[8,512]{1,0:T(8,128)(2,1)S(1)}, u32[]{:S(2)}, u32[]{:S(2)}) collective-permute-start(bf16[8,512]{1,0:T(8,128)(2,1)S(1)} %add_convert_fusion.1), channel_id=1, source_target_pairs={{64,0},{128,64},{192,128},{256,192},{320,256},{384,320},{448,384},... | collective-permute-start | bytes 24584 | tf_op jit(solution)/shard_map/ppermute | solution.py:15
  73.5 5.6 %collective-permute-start = (bf16[8,512]{1,0:T(8,128)(2,1)S(1)}, bf16[8,512]{1,0:T(8,128)(2,1)S(1)}, u32[]{:S(2)}, u32[]{:S(2)}) collective-permute-start(bf16[8,512]{1,0:T(8,128)(2,1)S(1)} %add_convert_fusion.1), channel_id=1, source_target_pairs={{0,64},{64,128},{128,192},{192,256},{256,320},{320,384},{384,448},... | collective-permute-start | bytes 24584 | tf_op jit(solution)/shard_map/ppermute | solution.py:12
  76.8 3.5 %copy-start.4 = (bf16[512,512]{1,0:T(8,128)(2,1)S(1)}, bf16[512,512]{1,0:T(8,128)(2,1)}, u32[]{:S(2)}) copy-start(bf16[512,512]{1,0:T(8,128)(2,1)} %param.30) | copy-start | bytes 1572868
  76.8 3.5 %copy-start.14 = (f32[512]{0:T(512)S(1)}, f32[512]{0:T(512)}, u32[]{:S(2)}) copy-start(f32[512]{0:T(512)} %param.33) | copy-start | bytes 6148
  80.6 2.0 %copy-start.8 = (bf16[8,512]{1,0:T(8,128)(2,1)S(1)}, bf16[8,512]{1,0:T(8,128)(2,1)}, u32[]{:S(2)}) copy-start(bf16[8,512]{1,0:T(8,128)(2,1)} %param.35) | copy-start | bytes 24580
  80.6 2.0 %copy-start.12 = (f32[512]{0:T(512)S(1)}, f32[512]{0:T(512)}, u32[]{:S(2)}) copy-start(f32[512]{0:T(512)} %param.34) | copy-start | bytes 6148
  88.6 5.6 %collective-permute-start.3 = (bf16[8,512]{1,0:T(8,128)(2,1)S(1)}, bf16[8,512]{1,0:T(8,128)(2,1)S(1)}, u32[]{:S(2)}, u32[]{:S(2)}) collective-permute-start(bf16[8,512]{1,0:T(8,128)(2,1)S(1)} %get-tuple-element.10), channel_id=1, source_target_pairs={{64,0},{128,64},{192,128},{256,192},{320,256},{384,320},{448,384},... | collective-permute-start | bytes 24584 | tf_op jit(solution)/shard_map/ppermute | solution.py:15
  90.9 5.6 %collective-permute-start.2 = (bf16[8,512]{1,0:T(8,128)(2,1)S(1)}, bf16[8,512]{1,0:T(8,128)(2,1)S(1)}, u32[]{:S(2)}, u32[]{:S(2)}) collective-permute-start(bf16[8,512]{1,0:T(8,128)(2,1)S(1)} %get-tuple-element.9), channel_id=1, source_target_pairs={{0,64},{64,128},{128,192},{192,256},{256,320},{320,384},{384,448},... | collective-permute-start | bytes 24584 | tf_op jit(solution)/shard_map/ppermute | solution.py:12
  100.6 3.9 %copy-start.7 = (bf16[512,512]{1,0:T(8,128)(2,1)S(1)}, bf16[512,512]{1,0:T(8,128)(2,1)}, u32[]{:S(2)}) copy-start(bf16[512,512]{1,0:T(8,128)(2,1)} %param.25) | copy-start | bytes 1572868
  103.4 1.0 copy-start.5
  106.2 8.7 %copy-start.6 = (bf16[1024,512]{1,0:T(8,128)(2,1)S(1)}, bf16[1024,512]{1,0:T(8,128)(2,1)}, u32[]{:S(2)}) copy-start(bf16[1024,512]{1,0:T(8,128)(2,1)} %copy-done.5) | copy-start | bytes 3145732
  106.2 37.1 %all-to-all-start.2 = ((bf16[64,16,512]{2,1,0:T(8,128)(2,1)}), bf16[64,16,512]{2,1,0:T(8,128)(2,1)S(1)}, u32[]{:S(2)}, u32[]{:S(2)}) async-start(bf16[64,16,512]{2,1,0:T(8,128)(2,1)} %bitcast.53), calls=%async_computation.2 | async-start | bytes 2097152 | tf_op jit(solution)/shard_map/all_to_all | solution.py:144
where the time goes:
time: 154 us; the launch traced here: 153 us
  waiting for transfers between devices  53.8 us (35%)
  starting transfers between devices  41 us (27%)
  local copies, waits for them, and re-layouts  23.4 us (15%)
  other arithmetic  18.3 us (12%)
  matrix products  15.3 us (10%)
    all_to_all x1, waiting for transfers between devices, per_device(): lax.all_to_all(slot_grad.astype(jnp.bfloat16), 'feat', split_axis=0, conc...  26.2 us
    all_to_all x1, waiting for transfers between devices, per_device(): lax.all_to_all(out_rows, 'feat', split_axis=0, concat_axis=0, tiled=True)  23 us
    all_to_all x1, starting transfers between devices, per_device(): lax.all_to_all(out_slot, 'feat', split_axis=0, concat_axis=0, tiled=True)  11 us
    all_to_all x1, starting transfers between devices, per_device(): lax.all_to_all(out_rows, 'feat', split_axis=0, concat_axis=0, tiled=True)  10.5 us
    all_to_all x1, starting transfers between devices, per_device(): lax.all_to_all(slot_grad.astype(jnp.bfloat16), 'feat', split_axis=0, conc...  8.68 us
    dot_general x6, matrix products, times_transpose(): lax.dot_general(left, weight, (((1,), (1,)), ((), ())), preferred_element...  7.38 us
    scatter-add x1, other arithmetic, per_device(): grad_grid = jnp.zeros((grid_latent.shape[0], latent), jnp.float32).at[g2m...  7.24 us
    scatter x1, local copies, waits for them, and re-layouts, per_device(): jnp.zeros((slot_count, latent), jnp.bfloat16).at[position]  7.19 us
  transfers between devices with their start and end apart: 7, of which 4 were waited for; matrix products, arithmetic and copies ran while one was open for 11% of the time, Pallas kernels for 0%

commit v1 on v0

v1 whole, which is shorter than its diff:
```python
import functools

import jax
import jax.numpy as jnp
from jax import lax
from jax.experimental import pallas as pl
from jax.experimental.pallas import tpu as pltpu
from jax.sharding import PartitionSpec as P

BF16 = jnp.bfloat16
F32 = jnp.float32


def dot(left, right):
    return jnp.dot(left, right, preferred_element_type=F32)


def dot_t(left, right):
    return lax.dot_general(left, right, (((1,), (1,)), ((), ())), preferred_element_type=F32)


def split(values):
    high = values.astype(BF16)
    return high, (values - high.astype(F32)).astype(BF16)


def wide_dot(values, weight, product):
    rows = values.shape[0]
    high, low = split(values)
    both = product(jnp.concatenate([high.astype(F32), low.astype(F32)], axis=0).astype(BF16), weight)
    return both[:rows] + both[rows:]


def thirds(values):
    high, rest = values.astype(BF16), values
    rest = rest - high.astype(F32)
    mid = rest.astype(BF16).astype(F32)
    low = (rest - mid).astype(BF16).astype(F32)
    return jnp.concatenate([high.astype(F32), mid, low], axis=0).astype(BF16)


def layer_norm(values, gain):
    average = jnp.mean(values, axis=-1, keepdims=True)
    centred = values - average
    spread = jnp.mean(centred * centred, axis=-1, keepdims=True)
    inv_std = lax.rsqrt(spread + 1e-05)
    normed = centred * inv_std
    return normed * gain, normed, inv_std


def norm_back(normed, inv_std, gain, upstream):
    scaled = upstream * gain
    return inv_std * (
        scaled
        - jnp.mean(scaled, axis=-1, keepdims=True)
        - normed * jnp.mean(scaled * normed, axis=-1, keepdims=True)
    )


def call(body, out, *args, scratch=()):
    flops = 4e9
    return pl.pallas_call(
        body,
        out_shape=out,
        in_specs=[pl.BlockSpec(memory_space=pltpu.VMEM)] * len(args),
        out_specs=jax.tree.map(lambda _: pl.BlockSpec(memory_space=pltpu.VMEM), out),
        scratch_shapes=scratch,
        compiler_params=pltpu.CompilerParams(vmem_limit_bytes=40 * 2**20),
        cost_estimate=pl.CostEstimate(flops=int(flops), bytes_accessed=2**22, transcendentals=0),
    )(*args)


def src_kernel(own_ref, mate_ref, pick_ref, weight_ref, bias_ref, pre_ref):
    tile = own_ref.shape[0]
    edges = pick_ref.shape[0]
    for start in range(0, edges, tile):
        grid_ref = own_ref if start < edges // 2 else mate_ref
        rows = dot(pick_ref[start : start + tile, :], grid_ref[...]).astype(BF16)
        pre_ref[start : start + tile, :] = dot(rows, weight_ref[...]) + bias_ref[...]


def enc_kernel(pre_ref, dst_ref, dst_t_ref, mesh_ref, weight_ref, sum_ref, slope_ref):
    tile = 256
    total = None
    for start in range(0, pre_ref.shape[0], tile):
        rows = dot(dst_ref[start : start + tile, :], mesh_ref[...]).astype(BF16)
        pre = pre_ref[start : start + tile, :] + dot(rows, weight_ref[...])
        sigma = jax.nn.sigmoid(pre)
        hidden = (pre * sigma).astype(BF16)
        slope_ref[start : start + tile, :] = sigma * (1.0 + pre * (1.0 - sigma))
        part = dot(dst_t_ref[:, start : start + tile], hidden)
        total = part if total is None else total + part
    sum_ref[...] = total.astype(BF16)


def chunk_sum(ref, count):
    values = ref[...].astype(F32)
    return jnp.sum(values.reshape(values.shape[0] // count, count, values.shape[1]), axis=0)


def mid_kernel(parts_ref, weight_ref, gain_ref, mesh_ref, mid_ref, agg_ref):
    agg = wide_dot(chunk_sum(parts_ref, mesh_ref.shape[0]), weight_ref[...], dot)
    agg_ref[...] = agg
    mid_ref[...] = (mesh_ref[...].astype(F32) + layer_norm(agg, gain_ref[...])[0]).astype(BF16)


def proc_kernel(
    one_ref, mid_ref, two_ref, pick_ref, pick_t_ref, src_w_ref, dst_w_ref, out_w_ref, bias_ref,
    gain_ref, cotangent_ref, out_ref, rim_one_ref, rim_two_ref, grad_ref,
):
    count = mid_ref.shape[0]
    mid = mid_ref[...].astype(F32)
    near = jnp.concatenate([one_ref[...].astype(F32), mid, two_ref[...].astype(F32)], axis=0)
    table = jnp.concatenate(
        [dot(near.astype(BF16), src_w_ref[...]), dot(mid.astype(BF16), dst_w_ref[...]) + bias_ref[...]],
        axis=0,
    )
    pre = dot(pick_ref[...], thirds(table))
    sigma = jax.nn.sigmoid(pre)
    hidden = (pre * sigma).astype(BF16)
    slope = sigma * (1.0 + pre * (1.0 - sigma))
    summed = dot(pick_t_ref[...], hidden)[3 * count :]
    agg = wide_dot(summed, out_w_ref[...], dot)
    shifted, normed, inv_std = layer_norm(agg, gain_ref[...])
    out_ref[...] = (mid + shifted).astype(BF16)
    upstream = cotangent_ref[...].astype(F32)
    grad_agg = norm_back(normed, inv_std, gain_ref[...], upstream).astype(BF16)
    back = dot_t(grad_agg, out_w_ref[...])
    blank = jnp.zeros((3 * count, back.shape[1]), F32)
    spread = dot(pick_ref[...], thirds(jnp.concatenate([blank, back], axis=0)))
    pre_grad = (spread * slope).astype(BF16)
    sums = dot(pick_t_ref[...], pre_grad)
    sender = wide_dot(sums[: 3 * count], src_w_ref[...], dot_t)
    receiver = wide_dot(sums[3 * count :], dst_w_ref[...], dot_t)
    rim_one_ref[...] = sender[:count].astype(BF16)
    rim_two_ref[...] = sender[2 * count :].astype(BF16)
    grad_ref[...] = upstream + receiver + sender[count : 2 * count]


def back_kernel(part_ref, one_ref, two_ref, agg_ref, gain_ref, grad_ref, tiled_ref):
    grad = part_ref[...] + one_ref[...].astype(F32) + two_ref[...].astype(F32)
    grad_ref[...] = grad
    _, normed, inv_std = layer_norm(agg_ref[...], gain_ref[...])
    rows = norm_back(normed, inv_std, gain_ref[...], grad)
    times = tiled_ref.shape[0] // rows.shape[0]
    tiled_ref[...] = jnp.concatenate([rows] * times, axis=0).astype(BF16)


def enc_back_kernel(grad_ref, dst_ref, dst_t_ref, slope_ref, weight_ref, edge_ref, sum_ref):
    tile = 256
    total = None
    for start in range(0, slope_ref.shape[0], tile):
        rows = dot(dst_ref[start : start + tile, :], grad_ref[...]).astype(BF16)
        edge = (dot_t(rows, weight_ref[...]) * slope_ref[start : start + tile, :]).astype(BF16)
        edge_ref[start : start + tile, :] = edge
        part = dot(dst_t_ref[:, start : start + tile], edge)
        total = part if total is None else total + part
    sum_ref[...] = total.astype(BF16)


def grid_kernel(edge_ref, pick_t_ref, weight_ref, own_ref, mate_ref):
    half = edge_ref.shape[0] // 2
    own = dot(pick_t_ref[:, :half], edge_ref[:half, :])
    mate = dot(pick_t_ref[:, half:], edge_ref[half:, :])
    own_ref[...] = wide_dot(own, weight_ref[...], dot_t)
    mate_ref[...] = wide_dot(mate, weight_ref[...], dot_t).astype(BF16)


def mesh_kernel(parts_ref, weight_ref, grad_ref, out_ref):
    summed = chunk_sum(parts_ref, grad_ref.shape[0])
    out_ref[...] = (grad_ref[...] + wide_dot(summed, weight_ref[...], dot_t)).astype(BF16)


def per_device(
    grid_latent,
    mesh_latent,
    g2m_src,
    g2m_peer,
    g2m_slot,
    proc_src,
    proc_dst,
    enc_src_w,
    enc_dst_w,
    enc_out_w,
    enc_bias,
    enc_gain,
    proc_src_w,
    proc_dst_w,
    proc_out_w,
    proc_bias,
    proc_gain,
    cotangent,
):
    feats = lax.axis_size("feat")
    bands = lax.axis_size("band")
    chips = feats // 2
    core = lax.axis_index("feat") % 2
    band = lax.axis_index("band")
    edges = g2m_src.shape[0]
    grids, latent = grid_latent.shape
    nodes = mesh_latent.shape[0]
    plane_nodes = chips * nodes
    plane = [[2 * chip + side for chip in range(chips)] for side in range(2)]
    shape = jax.ShapeDtypeStruct
    row = lambda vector: vector.reshape(1, latent)

    def exchange(values):
        parts = values.reshape(chips, nodes, latent)
        parts = lax.all_to_all(
            parts, "feat", split_axis=0, concat_axis=0, tiled=True, axis_index_groups=plane
        )
        return parts.reshape(plane_nodes, latent)

    def swap(values):
        return lax.ppermute(values, "feat", [(i, i ^ 1) for i in range(feats)])

    first = [(i, i ^ 1) for i in range(bands)]
    second = [(i, j) for i in range(1, bands - 2, 2) for i, j in ((i, i + 1), (i + 1, i))]

    mesh_all = exchange(jnp.tile(mesh_latent, (chips, 1)))

    mate_grid = swap(grid_latent)
    index = jnp.stack([g2m_src, g2m_peer[:, 0], g2m_slot])
    index = jnp.concatenate([index, swap(index)], axis=1)
    source, peer, slot = index[0], index[1], index[2]
    target = jnp.where(peer % 2 == core, peer // 2 * nodes + slot, -1)
    grid_ids = jnp.arange(grids, dtype=jnp.int32)
    node_ids = jnp.arange(plane_nodes, dtype=jnp.int32)
    src_pick = (source[:, None] == grid_ids[None, :]).astype(BF16)
    src_pick_t = (source[None, :] == grid_ids[:, None]).astype(BF16)
    dst_pick = (target[:, None] == node_ids[None, :]).astype(BF16)
    dst_pick_t = (target[None, :] == node_ids[:, None]).astype(BF16)

    side = proc_src // nodes
    sender = jnp.where(band % 2 == 0, 2 - side, side) * nodes + proc_src % nodes
    table_ids = jnp.arange(4 * nodes, dtype=jnp.int32)

    def proc_pick(ids, per_edge):
        return jnp.logical_or(per_edge(sender) == ids, per_edge(proc_dst + 3 * nodes) == ids).astype(BF16)

    pick = proc_pick(jnp.tile(table_ids, 3)[None, :], lambda v: v[:, None])
    pick_t = proc_pick(table_ids[:, None], lambda v: v[None, :])

    pre_src = call(
        src_kernel, shape((2 * edges, latent), F32),
        grid_latent, mate_grid, src_pick, enc_src_w, row(enc_bias),
    )
    partial, slope = call(
        enc_kernel, (shape((plane_nodes, latent), BF16), shape((2 * edges, latent), F32)),
        pre_src, dst_pick, dst_pick_t, mesh_all, enc_dst_w,
    )
    mid, enc_agg = call(
        mid_kernel, (shape((nodes, latent), BF16), shape((nodes, latent), F32)),
        exchange(partial), enc_out_w, row(enc_gain), mesh_latent,
    )
    one = lax.ppermute(mid, "band", first)
    two = lax.ppermute(mid, "band", second)
    mesh_out, rim_one, rim_two, grad_part = call(
        proc_kernel,
        (shape((nodes, latent), BF16),) * 3 + (shape((nodes, latent), F32),),
        one, mid, two, pick, pick_t, proc_src_w, proc_dst_w, proc_out_w, row(proc_bias),
        row(proc_gain), cotangent,
    )
    back_one = lax.ppermute(rim_one, "band", first)
    back_two = lax.ppermute(rim_two, "band", second)
    grad_mid, tiled = call(
        back_kernel, (shape((nodes, latent), F32), shape((plane_nodes, latent), BF16)),
        grad_part, back_one, back_two, enc_agg, row(enc_gain),
    )
    edge_grad, node_part = call(
        enc_back_kernel, (shape((2 * edges, latent), BF16), shape((plane_nodes, latent), BF16)),
        exchange(tiled), dst_pick, dst_pick_t, slope, enc_out_w,
    )
    node_parts = exchange(node_part)
    own_grad, mate_grad = call(
        grid_kernel, (shape((grids, latent), F32), shape((grids, latent), BF16)),
        edge_grad, src_pick_t, enc_src_w,
    )
    grad_grid = (own_grad + swap(mate_grad).astype(F32)).astype(BF16)
    grad_mesh = call(
        mesh_kernel, shape((nodes, latent), BF16), node_parts, enc_dst_w, grad_mid,
    )
    return (mesh_out, grad_grid, grad_mesh)


def solution(mesh):
    shard = ("band", "feat")
    placed = (P(shard, None), P(shard, None), P(shard), P(shard, None), P(shard), P(shard), P(shard))
    placed += (P(),) * 10 + (P(shard, None),)
    return jax.shard_map(
        per_device,
        mesh=mesh,
        in_specs=placed,
        out_specs=(P(shard, None), P(shard, None), P(shard, None)),
        check_vma=False,
    )
```

time: 154 us -> 119 us (0.77)
  the two profiles are of different devices: /device:TPU:517 before, /device:TPU:72 now
where the time goes in v1:
time: 119 us; the launch traced here: 118 us
  starting transfers between devices  47.8 us (40%)
  waiting for transfers between devices  46.4 us (39%)
  Pallas kernels  12 us (10%)
  local copies, waits for them, and re-layouts  7.46 us (6%)
  other arithmetic  3.25 us (3%)
    all_to_all x4, waiting for transfers between devices, exchange(): lax.all_to_all(parts, 'feat', split_axis=0, concat_axis=0, tiled=True, ax...  42.5 us
    all_to_all x4, starting transfers between devices, exchange(): lax.all_to_all(parts, 'feat', split_axis=0, concat_axis=0, tiled=True, ax...  23.8 us
    pallas_call x8, Pallas kernels, call(): pl.pallas_call(body, out_shape=out, in_specs=[pl.BlockSpec(memory_space=p...  12 us
    ppermute x1, starting transfers between devices, per_device(): back_two = lax.ppermute(rim_two, 'band', second)  7.18 us
    ppermute x3, starting transfers between devices, swap(): return lax.ppermute(values, 'feat', [(i, i ^ 1) for i in range(feats)])  6.25 us
    unnamed x38, local copies, waits for them, and re-layouts  5.96 us
    ppermute x1, starting transfers between devices, per_device(): one = lax.ppermute(mid, 'band', first)  5.43 us
    ppermute x1, starting transfers between devices, per_device(): two = lax.ppermute(mid, 'band', second)  3.25 us
  transfers between devices with their start and end apart: 11, of which 6 were waited for; matrix products, arithmetic and copies ran while one was open for 3% of the time, Pallas kernels for 1%

profile of v1, /device:TPU:72, one launch (start us, length us, event | category | flops | bytes accessed | tf_op | source)
XLA Modules:
  0.0 118.0 jit_solution(17345713766554074068)
XLA Ops:
  0.6 0.0 copy-start.7
  0.7 0.8 pad_add_fusion
  1.5 1.9 %collective-permute-start.1 = (s32[3,512]{1,0:T(4,128)S(1)}, s32[3,512]{1,0:T(4,128)S(1)}, u32[]{:S(2)}, u32[]{:S(2)}) collective-permute-start(s32[3,512]{1,0:T(4,128)S(1)} %pad_add_fusion), channel_id=1, source_target_pairs={{0,1},{1,0},{2,3},{3,2},{4,5},{5,4},{6,7},{7,6},{8,9},{9,8},{10,11... | collective-permute-start | bytes 18440 | tf_op jit(solution)/shard_map/ppermute | solution.py:215
  3.4 2.4 %collective-permute-start = (bf16[256,512]{1,0:T(8,128)(2,1)}, bf16[256,512]{1,0:T(8,128)(2,1)S(1)}, u32[]{:S(2)}, u32[]{:S(2)}) collective-permute-start(bf16[256,512]{1,0:T(8,128)(2,1)} %own_ref.1), channel_id=1, source_target_pairs={{0,1},{1,0},{2,3},{3,2},{4,5},{5,4},{6,7},{7,6},{8,9},{9,8},{10,11... | collective-permute-start | bytes 786440 | tf_op jit(solution)/shard_map/ppermute | solution.py:215
  5.8 1.4 %reshape_tile.3 = bf16[32,8,512]{2,1,0:T(8,128)(2,1)} broadcast(bf16[8,512]{1,0:T(8,128)(2,1)} %mesh_ref.1), dimensions={1,2} | broadcast | bytes 270336 | tf_op jit(solution)/shard_map/reshape;tile | solution.py:208
  7.2 10.2 %all-to-all-start = ((bf16[32,8,512]{2,1,0:T(8,128)(2,1)}), bf16[32,8,512]{2,1,0:T(8,128)(2,1)S(1)}, u32[]{:S(2)}, u32[]{:S(2)}) async-start(bf16[32,8,512]{2,1,0:T(8,128)(2,1)} %reshape_tile.3), calls=%async_computation | async-start | bytes 524288 | tf_op jit(solution)/shard_map/all_to_all | solution.py:209
  17.4 0.9 compare_select_fusion
  18.3 0.2 fusion.1.dst_ref
  18.5 0.2 fusion.pick_ref
  18.8 0.1 fusion.2.dst_t_ref
  18.9 0.0 copy-start.6
  18.9 1.3 %shard_map.193.pre_ref = f32[1024,512]{1,0:T(8,128)S(1)} custom-call(bf16[256,512]{1,0:T(8,128)(2,1)S(1)} %copy-done.7, bf16[256,512]{1,0:T(8,128)(2,1)S(1)} %collective-permute-done.mate_ref, bf16[1024,256]{1,0:T(8,128)(2,1)S(1)} %fusion.pick_ref, bf16[512,512]{1,0:T(8,128)(2,1)S(1)} %copy-done.5, f32[1,512]{1,0:T(1,128)S(1)} %bitcast.22), custom_call_target="tpu_custom_call" | custom-call | flops 4000000000 | bytes 4194304 | tf_op jit(solution)/shard_map/pallas_call | solution.py:62
  20.2 1.3 %copy-done.15 = f32[1024,512]{1,0:T(8,128)} copy-done((f32[1024,512]{1,0:T(8,128)}, f32[1024,512]{1,0:T(8,128)S(1)}, u32[]{:S(2)}) %copy-start.15) | copy-done | bytes 2097176
  21.6 8.3 %all-to-all-done = bf16[32,8,512]{2,1,0:T(8,128)(2,1)S(1)} async-done(((bf16[32,8,512]{2,1,0:T(8,128)(2,1)}), bf16[32,8,512]{2,1,0:T(8,128)(2,1)S(1)}, u32[]{:S(2)}, u32[]{:S(2)}) %all-to-all-start) | async-done | bytes 262176 | tf_op jit(solution)/shard_map/all_to_all | solution.py:209
  29.9 1.6 %copy-done.16 = f32[1024,512]{1,0:T(8,128)S(1)} copy-done((f32[1024,512]{1,0:T(8,128)S(1)}, f32[1024,512]{1,0:T(8,128)}, u32[]{:S(2)}) %copy-start.16) | copy-done | bytes 2097176
  31.5 0.0 copy-start.12
  31.5 3.0 %shard_map.194 = (bf16[256,512]{1,0:T(8,128)(2,1)}, f32[1024,512]{1,0:T(8,128)S(1)}) custom-call(f32[1024,512]{1,0:T(8,128)S(1)} %copy-done.16, bf16[1024,256]{1,0:T(8,128)(2,1)S(1)} %fusion.1.dst_ref, bf16[256,1024]{1,0:T(8,128)(2,1)S(1)} %fusion.2.dst_t_ref, bf16[256,512]{1,0:T(8,128)(2,1)S(1)} %bitcast.18, bf16[512,512]{1,0:T(8,128)(2,1)S(1)} %copy-done.6), custom_call_target="tpu_custom_call" | custom-call | flops 4000000000 | bytes 4194304 | tf_op jit(solution)/shard_map/pallas_call | solution.py:62
  34.5 1.4 %copy-done.13 = f32[1024,512]{1,0:T(8,128)} copy-done((f32[1024,512]{1,0:T(8,128)}, f32[1024,512]{1,0:T(8,128)S(1)}, u32[]{:S(2)}) %copy-start.13) | copy-done | bytes 2097176
  35.8 4.6 %all-to-all-start.1 = ((bf16[32,8,512]{2,1,0:T(8,128)(2,1)}), bf16[32,8,512]{2,1,0:T(8,128)(2,1)S(1)}, u32[]{:S(2)}, u32[]{:S(2)}) async-start(bf16[32,8,512]{2,1,0:T(8,128)(2,1)} %bitcast.9), calls=%async_computation.1 | async-start | bytes 524288 | tf_op jit(solution)/shard_map/all_to_all | solution.py:209
  40.4 0.1 eq.154
  40.5 0.1 or_convert_fusion.pick_ref
  40.7 11.2 %all-to-all-done.1 = bf16[32,8,512]{2,1,0:T(8,128)(2,1)S(1)} async-done(((bf16[32,8,512]{2,1,0:T(8,128)(2,1)}), bf16[32,8,512]{2,1,0:T(8,128)(2,1)S(1)}, u32[]{:S(2)}, u32[]{:S(2)}) %all-to-all-start.1) | async-done | bytes 262176 | tf_op jit(solution)/shard_map/all_to_all | solution.py:209
  51.9 0.0 copy-start.1
  51.9 0.0 copy-start.2
  51.9 0.0 copy-start.3
  51.9 0.0 copy-start.8
  51.9 0.0 copy-start.10
  51.9 0.0 copy-start.11
  52.0 0.4 shard_map.195
  52.3 5.4 %collective-permute-start.2 = (bf16[8,512]{1,0:T(8,128)(2,1)S(1)}, bf16[8,512]{1,0:T(8,128)(2,1)S(1)}, u32[]{:S(2)}, u32[]{:S(2)}) collective-permute-start(bf16[8,512]{1,0:T(8,128)(2,1)S(1)} %get-tuple-element.18.mid_ref), channel_id=1, source_target_pairs={{0,64},{64,0},{128,192},{192,128},{256,320},{320,256},{384,448},{4... | collective-permute-start | bytes 24584 | tf_op jit(solution)/shard_map/ppermute | solution.py:256
  57.8 3.3 %collective-permute-start.3 = (bf16[8,512]{1,0:T(8,128)(2,1)S(1)}, bf16[8,512]{1,0:T(8,128)(2,1)S(1)}, u32[]{:S(2)}, u32[]{:S(2)}) collective-permute-start(bf16[8,512]{1,0:T(8,128)(2,1)S(1)} %get-tuple-element.18.mid_ref), channel_id=1, source_target_pairs={{64,128},{128,64},{192,256},{256,192},{320,384},{384,320},{448,512... | collective-permute-start | bytes 24584 | tf_op jit(solution)/shard_map/ppermute | solution.py:257
  61.1 2.3 %collective-permute-done.3.two_ref = bf16[8,512]{1,0:T(8,128)(2,1)S(1)} collective-permute-done((bf16[8,512]{1,0:T(8,128)(2,1)S(1)}, bf16[8,512]{1,0:T(8,128)(2,1)S(1)}, u32[]{:S(2)}, u32[]{:S(2)}) %collective-permute-start.3) | collective-permute-done | bytes 8224 | tf_op jit(solution)/shard_map/ppermute | solution.py:257
  63.4 1.9 %shard_map.196 = (bf16[8,512]{1,0:T(8,128)(2,1)}, bf16[8,512]{1,0:T(8,128)(2,1)S(1)}, bf16[8,512]{1,0:T(8,128)(2,1)S(1)}, f32[8,512]{1,0:T(8,128)S(1)}) custom-call(bf16[8,512]{1,0:T(8,128)(2,1)S(1)} %collective-permute-done.2.one_ref, bf16[8,512]{1,0:T(8,128)(2,1)S(1)} %get-tuple-element.18.mid_ref, bf16[8,512]{1,0:T(8,128)(2,1)S(1)} %collective-permute-done.3.two_ref, ...), custom_call_target="tpu_custom_call" | custom-call | flops 4000000000 | bytes 4194304 | tf_op jit(solution)/shard_map/pallas_call | solution.py:62
  65.3 1.9 %collective-permute-start.4 = (bf16[8,512]{1,0:T(8,128)(2,1)S(1)}, bf16[8,512]{1,0:T(8,128)(2,1)S(1)}, u32[]{:S(2)}, u32[]{:S(2)}) collective-permute-start(bf16[8,512]{1,0:T(8,128)(2,1)S(1)} %get-tuple-element.21), channel_id=1, source_target_pairs={{0,64},{64,0},{128,192},{192,128},{256,320},{320,256},{384,448},{4... | collective-permute-start | bytes 24584 | tf_op jit(solution)/shard_map/ppermute | solution.py:264
  67.2 7.2 %collective-permute-start.5 = (bf16[8,512]{1,0:T(8,128)(2,1)S(1)}, bf16[8,512]{1,0:T(8,128)(2,1)S(1)}, u32[]{:S(2)}, u32[]{:S(2)}) collective-permute-start(bf16[8,512]{1,0:T(8,128)(2,1)S(1)} %get-tuple-element.22), channel_id=1, source_target_pairs={{64,128},{128,64},{192,256},{256,192},{320,384},{384,320},{448,512... | collective-permute-start | bytes 24584 | tf_op jit(solution)/shard_map/ppermute | solution.py:265
  74.4 1.6 %collective-permute-done.5.two_ref = bf16[8,512]{1,0:T(8,128)(2,1)S(1)} collective-permute-done((bf16[8,512]{1,0:T(8,128)(2,1)S(1)}, bf16[8,512]{1,0:T(8,128)(2,1)S(1)}, u32[]{:S(2)}, u32[]{:S(2)}) %collective-permute-start.5) | collective-permute-done | bytes 8224 | tf_op jit(solution)/shard_map/ppermute | solution.py:265
  76.0 1.0 shard_map.197
  77.0 4.6 %all-to-all-start.2 = ((bf16[32,8,512]{2,1,0:T(8,128)(2,1)}), bf16[32,8,512]{2,1,0:T(8,128)(2,1)S(1)}, u32[]{:S(2)}, u32[]{:S(2)}) async-start(bf16[32,8,512]{2,1,0:T(8,128)(2,1)} %bitcast.14), calls=%async_computation.2 | async-start | bytes 524288 | tf_op jit(solution)/shard_map/all_to_all | solution.py:209
  81.6 0.1 fusion.3.pick_t_ref
  81.7 10.9 %all-to-all-done.2 = bf16[32,8,512]{2,1,0:T(8,128)(2,1)S(1)} async-done(((bf16[32,8,512]{2,1,0:T(8,128)(2,1)}), bf16[32,8,512]{2,1,0:T(8,128)(2,1)S(1)}, u32[]{:S(2)}, u32[]{:S(2)}) %all-to-all-start.2) | async-done | bytes 262176 | tf_op jit(solution)/shard_map/all_to_all | solution.py:209
  92.5 1.6 %copy-done.14 = f32[1024,512]{1,0:T(8,128)S(1)} copy-done((f32[1024,512]{1,0:T(8,128)S(1)}, f32[1024,512]{1,0:T(8,128)}, u32[]{:S(2)}) %copy-start.14) | copy-done | bytes 2097176
  94.1 2.7 %shard_map.198 = (bf16[1024,512]{1,0:T(8,128)(2,1)S(1)}, bf16[256,512]{1,0:T(8,128)(2,1)}) custom-call(bf16[256,512]{1,0:T(8,128)(2,1)S(1)} %bitcast.21, bf16[1024,256]{1,0:T(8,128)(2,1)S(1)} %fusion.1.dst_ref, bf16[256,1024]{1,0:T(8,128)(2,1)S(1)} %fusion.2.dst_t_ref, f32[1024,512]{1,0:T(8,128)S(1)} %copy-done.14, bf16[512,512]{1,0:T(8,128)(2,1)S(1)} %copy-done.4), custom_call_target="tpu_custom_call" | custom-call | flops 4000000000 | bytes 4194304 | tf_op jit(solution)/shard_map/pallas_call | solution.py:62
  96.8 1.0 shard_map.199
  97.8 1.9 %collective-permute-start.6 = (bf16[256,512]{1,0:T(8,128)(2,1)S(1)}, bf16[256,512]{1,0:T(8,128)(2,1)S(1)}, u32[]{:S(2)}, u32[]{:S(2)}) collective-permute-start(bf16[256,512]{1,0:T(8,128)(2,1)S(1)} %get-tuple-element.28), channel_id=1, source_target_pairs={{0,1},{1,0},{2,3},{3,2},{4,5},{5,4},{6,7},{7,6},{8,9},{9,8},{10,11... | collective-permute-start | bytes 786440 | tf_op jit(solution)/shard_map/ppermute | solution.py:215
  99.7 4.5 %all-to-all-start.3 = ((bf16[32,8,512]{2,1,0:T(8,128)(2,1)}), bf16[32,8,512]{2,1,0:T(8,128)(2,1)S(1)}, u32[]{:S(2)}, u32[]{:S(2)}) async-start(bf16[32,8,512]{2,1,0:T(8,128)(2,1)} %bitcast.16), calls=%async_computation.3 | async-start | bytes 524288 | tf_op jit(solution)/shard_map/all_to_all | solution.py:209
  104.2 0.8 add_convert_fusion
  105.0 12.1 %all-to-all-done.3 = bf16[32,8,512]{2,1,0:T(8,128)(2,1)S(1)} async-done(((bf16[32,8,512]{2,1,0:T(8,128)(2,1)}), bf16[32,8,512]{2,1,0:T(8,128)(2,1)S(1)}, u32[]{:S(2)}, u32[]{:S(2)}) %all-to-all-start.3) | async-done | bytes 262176 | tf_op jit(solution)/shard_map/all_to_all | solution.py:209
  117.1 0.9 shard_map.200
  (34 shorter events, 0.1 us)
Async XLA Ops:
  0.6 18.3 %copy-start.7 = (bf16[256,512]{1,0:T(8,128)(2,1)S(1)}, bf16[256,512]{1,0:T(8,128)(2,1)}, u32[]{:S(2)}) copy-start(bf16[256,512]{1,0:T(8,128)(2,1)} %own_ref.1) | copy-start | bytes 786436
  0.6 18.2 %copy-start.9 = (f32[512]{0:T(512)S(1)}, f32[512]{0:T(512)}, u32[]{:S(2)}) copy-start(f32[512]{0:T(512)} %param.28) | copy-start | bytes 6148
  0.7 18.2 %copy-start.5 = (bf16[512,512]{1,0:T(8,128)(2,1)S(1)}, bf16[512,512]{1,0:T(8,128)(2,1)}, u32[]{:S(2)}) copy-start(bf16[512,512]{1,0:T(8,128)(2,1)} %weight_ref.10) | copy-start | bytes 1572868
  1.5 15.9 %collective-permute-start.1 = (s32[3,512]{1,0:T(4,128)S(1)}, s32[3,512]{1,0:T(4,128)S(1)}, u32[]{:S(2)}, u32[]{:S(2)}) collective-permute-start(s32[3,512]{1,0:T(4,128)S(1)} %pad_add_fusion), channel_id=1, source_target_pairs={{0,1},{1,0},{2,3},{3,2},{4,5},{5,4},{6,7},{7,6},{8,9},{9,8},{10,11... | collective-permute-start | bytes 18440 | tf_op jit(solution)/shard_map/ppermute | solution.py:215
  3.4 15.5 %collective-permute-start = (bf16[256,512]{1,0:T(8,128)(2,1)}, bf16[256,512]{1,0:T(8,128)(2,1)S(1)}, u32[]{:S(2)}, u32[]{:S(2)}) collective-permute-start(bf16[256,512]{1,0:T(8,128)(2,1)} %own_ref.1), channel_id=1, source_target_pairs={{0,1},{1,0},{2,3},{3,2},{4,5},{5,4},{6,7},{7,6},{8,9},{9,8},{10,11... | collective-permute-start | bytes 786440 | tf_op jit(solution)/shard_map/ppermute | solution.py:215
  7.2 22.6 %all-to-all-start = ((bf16[32,8,512]{2,1,0:T(8,128)(2,1)}), bf16[32,8,512]{2,1,0:T(8,128)(2,1)S(1)}, u32[]{:S(2)}, u32[]{:S(2)}) async-start(bf16[32,8,512]{2,1,0:T(8,128)(2,1)} %reshape_tile.3), calls=%async_computation | async-start | bytes 524288 | tf_op jit(solution)/shard_map/all_to_all | solution.py:209
  18.9 11.0 %copy-start.6 = (bf16[512,512]{1,0:T(8,128)(2,1)S(1)}, bf16[512,512]{1,0:T(8,128)(2,1)}, u32[]{:S(2)}) copy-start(bf16[512,512]{1,0:T(8,128)(2,1)} %weight_ref.11) | copy-start | bytes 1572868
  20.2 1.4 %copy-start.15 = (f32[1024,512]{1,0:T(8,128)}, f32[1024,512]{1,0:T(8,128)S(1)}, u32[]{:S(2)}) copy-start(f32[1024,512]{1,0:T(8,128)S(1)} %shard_map.193.pre_ref) | copy-start | bytes 6291460
  29.9 1.6 %copy-start.16 = (f32[1024,512]{1,0:T(8,128)S(1)}, f32[1024,512]{1,0:T(8,128)}, u32[]{:S(2)}) copy-start(f32[1024,512]{1,0:T(8,128)} %copy-done.15) | copy-start | bytes 6291460
  31.5 9.0 %copy-start.17 = (s32[256]{0:T(256)S(1)}, s32[256]{0:T(256)}, u32[]{:S(2)}) copy-start(s32[256]{0:T(256)} %param.23) | copy-start | bytes 3076
  31.5 9.0 %copy-start.18 = (s32[256]{0:T(256)S(1)}, s32[256]{0:T(256)}, u32[]{:S(2)}) copy-start(s32[256]{0:T(256)} %param.24) | copy-start | bytes 3076
  31.5 20.4 %copy-start = (bf16[8,512]{1,0:T(8,128)(2,1)S(1)}, bf16[8,512]{1,0:T(8,128)(2,1)}, u32[]{:S(2)}) copy-start(bf16[8,512]{1,0:T(8,128)(2,1)} %mesh_ref.1) | copy-start | bytes 24580
  31.5 20.4 %copy-start.4 = (bf16[512,512]{1,0:T(8,128)(2,1)S(1)}, bf16[512,512]{1,0:T(8,128)(2,1)}, u32[]{:S(2)}) copy-start(bf16[512,512]{1,0:T(8,128)(2,1)} %weight_ref.9) | copy-start | bytes 1572868
  31.5 20.4 %copy-start.12 = (f32[512]{0:T(512)S(1)}, f32[512]{0:T(512)}, u32[]{:S(2)}) copy-start(f32[512]{0:T(512)} %param.29) | copy-start | bytes 6148
  34.5 1.4 %copy-start.13 = (f32[1024,512]{1,0:T(8,128)}, f32[1024,512]{1,0:T(8,128)S(1)}, u32[]{:S(2)}) copy-start(f32[1024,512]{1,0:T(8,128)S(1)} %get-tuple-element.25.slope_ref) | copy-start | bytes 6291460
  35.8 16.1 %all-to-all-start.1 = ((bf16[32,8,512]{2,1,0:T(8,128)(2,1)}), bf16[32,8,512]{2,1,0:T(8,128)(2,1)S(1)}, u32[]{:S(2)}, u32[]{:S(2)}) async-start(bf16[32,8,512]{2,1,0:T(8,128)(2,1)} %bitcast.9), calls=%async_computation.1 | async-start | bytes 524288 | tf_op jit(solution)/shard_map/all_to_all | solution.py:209
  51.9 11.4 %copy-start.1 = (bf16[512,512]{1,0:T(8,128)(2,1)S(1)}, bf16[512,512]{1,0:T(8,128)(2,1)}, u32[]{:S(2)}) copy-start(bf16[512,512]{1,0:T(8,128)(2,1)} %src_w_ref.1) | copy-start | bytes 1572868
  51.9 11.4 %copy-start.2 = (bf16[512,512]{1,0:T(8,128)(2,1)S(1)}, bf16[512,512]{1,0:T(8,128)(2,1)}, u32[]{:S(2)}) copy-start(bf16[512,512]{1,0:T(8,128)(2,1)} %dst_w_ref.1) | copy-start | bytes 1572868
  51.9 11.4 %copy-start.3 = (bf16[512,512]{1,0:T(8,128)(2,1)S(1)}, bf16[512,512]{1,0:T(8,128)(2,1)}, u32[]{:S(2)}) copy-start(bf16[512,512]{1,0:T(8,128)(2,1)} %out_w_ref.1) | copy-start | bytes 1572868
  51.9 11.4 %copy-start.8 = (bf16[8,512]{1,0:T(8,128)(2,1)S(1)}, bf16[8,512]{1,0:T(8,128)(2,1)}, u32[]{:S(2)}) copy-start(bf16[8,512]{1,0:T(8,128)(2,1)} %cotangent_ref.1) | copy-start | bytes 24580
  51.9 11.4 %copy-start.10 = (f32[512]{0:T(512)S(1)}, f32[512]{0:T(512)}, u32[]{:S(2)}) copy-start(f32[512]{0:T(512)} %param.33) | copy-start | bytes 6148
  51.9 11.4 %copy-start.11 = (f32[512]{0:T(512)S(1)}, f32[512]{0:T(512)}, u32[]{:S(2)}) copy-start(f32[512]{0:T(512)} %param.34) | copy-start | bytes 6148
  52.3 8.7 %collective-permute-start.2 = (bf16[8,512]{1,0:T(8,128)(2,1)S(1)}, bf16[8,512]{1,0:T(8,128)(2,1)S(1)}, u32[]{:S(2)}, u32[]{:S(2)}) collective-permute-start(bf16[8,512]{1,0:T(8,128)(2,1)S(1)} %get-tuple-element.18.mid_ref), channel_id=1, source_target_pairs={{0,64},{64,0},{128,192},{192,128},{256,320},{320,256},{384,448},{4... | collective-permute-start | bytes 24584 | tf_op jit(solution)/shard_map/ppermute | solution.py:256
  57.8 5.5 %collective-permute-start.3 = (bf16[8,512]{1,0:T(8,128)(2,1)S(1)}, bf16[8,512]{1,0:T(8,128)(2,1)S(1)}, u32[]{:S(2)}, u32[]{:S(2)}) collective-permute-start(bf16[8,512]{1,0:T(8,128)(2,1)S(1)} %get-tuple-element.18.mid_ref), channel_id=1, source_target_pairs={{64,128},{128,64},{192,256},{256,192},{320,384},{384,320},{448,512... | collective-permute-start | bytes 24584 | tf_op jit(solution)/shard_map/ppermute | solution.py:257
  65.3 9.1 %collective-permute-start.4 = (bf16[8,512]{1,0:T(8,128)(2,1)S(1)}, bf16[8,512]{1,0:T(8,128)(2,1)S(1)}, u32[]{:S(2)}, u32[]{:S(2)}) collective-permute-start(bf16[8,512]{1,0:T(8,128)(2,1)S(1)} %get-tuple-element.21), channel_id=1, source_target_pairs={{0,64},{64,0},{128,192},{192,128},{256,320},{320,256},{384,448},{4... | collective-permute-start | bytes 24584 | tf_op jit(solution)/shard_map/ppermute | solution.py:264
  67.2 8.8 %collective-permute-start.5 = (bf16[8,512]{1,0:T(8,128)(2,1)S(1)}, bf16[8,512]{1,0:T(8,128)(2,1)S(1)}, u32[]{:S(2)}, u32[]{:S(2)}) collective-permute-start(bf16[8,512]{1,0:T(8,128)(2,1)S(1)} %get-tuple-element.22), channel_id=1, source_target_pairs={{64,128},{128,64},{192,256},{256,192},{320,384},{384,320},{448,512... | collective-permute-start | bytes 24584 | tf_op jit(solution)/shard_map/ppermute | solution.py:265
  77.0 15.6 %all-to-all-start.2 = ((bf16[32,8,512]{2,1,0:T(8,128)(2,1)}), bf16[32,8,512]{2,1,0:T(8,128)(2,1)S(1)}, u32[]{:S(2)}, u32[]{:S(2)}) async-start(bf16[32,8,512]{2,1,0:T(8,128)(2,1)} %bitcast.14), calls=%async_computation.2 | async-start | bytes 524288 | tf_op jit(solution)/shard_map/all_to_all | solution.py:209
  92.5 1.6 %copy-start.14 = (f32[1024,512]{1,0:T(8,128)S(1)}, f32[1024,512]{1,0:T(8,128)}, u32[]{:S(2)}) copy-start(f32[1024,512]{1,0:T(8,128)} %copy-done.13) | copy-start | bytes 6291460
  97.8 6.4 %collective-permute-start.6 = (bf16[256,512]{1,0:T(8,128)(2,1)S(1)}, bf16[256,512]{1,0:T(8,128)(2,1)S(1)}, u32[]{:S(2)}, u32[]{:S(2)}) collective-permute-start(bf16[256,512]{1,0:T(8,128)(2,1)S(1)} %get-tuple-element.28), channel_id=1, source_target_pairs={{0,1},{1,0},{2,3},{3,2},{4,5},{5,4},{6,7},{7,6},{8,9},{9,8},{10,11... | collective-permute-start | bytes 786440 | tf_op jit(solution)/shard_map/ppermute | solution.py:215
  99.7 17.4 %all-to-all-start.3 = ((bf16[32,8,512]{2,1,0:T(8,128)(2,1)}), bf16[32,8,512]{2,1,0:T(8,128)(2,1)S(1)}, u32[]{:S(2)}, u32[]{:S(2)}) async-start(bf16[32,8,512]{2,1,0:T(8,128)(2,1)} %bitcast.16), calls=%async_computation.3 | async-start | bytes 524288 | tf_op jit(solution)/shard_map/all_to_all | solution.py:209

commit v2 on v1

--- a/solution.py
+++ b/solution.py
@@ -1,5 +1,3 @@
-import functools
-
 import jax
 import jax.numpy as jnp
 from jax import lax
@@ -57,17 +55,34 @@
     )
 
 
-def call(body, out, *args, scratch=()):
-    flops = 4e9
+def call(body, out, *args, flops=1e8, limit=16):
     return pl.pallas_call(
         body,
         out_shape=out,
         in_specs=[pl.BlockSpec(memory_space=pltpu.VMEM)] * len(args),
         out_specs=jax.tree.map(lambda _: pl.BlockSpec(memory_space=pltpu.VMEM), out),
-        scratch_shapes=scratch,
-        compiler_params=pltpu.CompilerParams(vmem_limit_bytes=40 * 2**20),
-        cost_estimate=pl.CostEstimate(flops=int(flops), bytes_accessed=2**22, transcendentals=0),
+        compiler_params=pltpu.CompilerParams(vmem_limit_bytes=limit * 2**20),
+        cost_estimate=pl.CostEstimate(flops=int(flops), bytes_accessed=2**20, transcendentals=0),
     )(*args)
+
+
+def silu_parts(values):
+    sigma = 0.5 + 0.5 * jnp.tanh(0.5 * values)
+    hidden = values * sigma
+    return hidden.astype(BF16), sigma * (1.0 + (values - hidden))
+
+
+def prep_kernel(mesh_ref, grid_ref, src_ref, peer_ref, slot_ref, tiled_ref, pack_ref):
+    count, latent = mesh_ref.shape
+    times = tiled_ref.shape[0] // count
+    rows = mesh_ref[...].astype(F32)
+    tiled_ref[...] = jnp.concatenate([rows] * times, axis=0).astype(BF16)
+    grids = grid_ref.shape[0]
+    pack_ref[:grids, :] = grid_ref[...]
+    spare = pack_ref.shape[0] - grids
+    place = lax.broadcasted_iota(jnp.int32, (spare, latent), 0)
+    index = jnp.where(place == 0, src_ref[...], jnp.where(place == 1, peer_ref[...], slot_ref[...]))
+    pack_ref[grids:, :] = index.astype(F32).astype(BF16)
 
 
 def src_kernel(own_ref, mate_ref, pick_ref, weight_ref, bias_ref, pre_ref):
@@ -75,31 +90,40 @@
     edges = pick_ref.shape[0]
     for start in range(0, edges, tile):
         grid_ref = own_ref if start < edges // 2 else mate_ref
-        rows = dot(pick_ref[start : start + tile, :], grid_ref[...]).astype(BF16)
+        rows = dot(pick_ref[start : start + tile, :], grid_ref[:tile, :]).astype(BF16)
         pre_ref[start : start + tile, :] = dot(rows, weight_ref[...]) + bias_ref[...]
+
+
+def stack_split(values):
+    high = values.astype(BF16).astype(F32)
+    return jnp.concatenate([high, values - high], axis=0).astype(BF16)
 
 
 def enc_kernel(pre_ref, dst_ref, dst_t_ref, mesh_ref, weight_ref, sum_ref, slope_ref):
     tile = 256
+    latent = pre_ref.shape[1]
+    plane_nodes = mesh_ref.shape[0]
+    table = stack_split(dot(mesh_ref[...], weight_ref[...]))
     total = None
     for start in range(0, pre_ref.shape[0], tile):
-        rows = dot(dst_ref[start : start + tile, :], mesh_ref[...]).astype(BF16)
-        pre = pre_ref[start : start + tile, :] + dot(rows, weight_ref[...])
-        sigma = jax.nn.sigmoid(pre)
-        hidden = (pre * sigma).astype(BF16)
-        slope_ref[start : start + tile, :] = sigma * (1.0 + pre * (1.0 - sigma))
-        part = dot(dst_t_ref[:, start : start + tile], hidden)
+        pre = pre_ref[start : start + tile, :] + dot(dst_ref[start : start + tile, :], table)
+        hidden, slope = silu_parts(pre)
+        slope_ref[start : start + tile, :] = slope
+        both = jnp.concatenate([hidden, slope.astype(BF16)], axis=1)
+        part = dot(dst_t_ref[:, start : start + tile], both)
         total = part if total is None else total + part
-    sum_ref[...] = total.astype(BF16)
-
-
-def chunk_sum(ref, count):
-    values = ref[...].astype(F32)
-    return jnp.sum(values.reshape(values.shape[0] // count, count, values.shape[1]), axis=0)
-
-
-def mid_kernel(parts_ref, weight_ref, gain_ref, mesh_ref, mid_ref, agg_ref):
-    agg = wide_dot(chunk_sum(parts_ref, mesh_ref.shape[0]), weight_ref[...], dot)
+    nodes = sum_ref.shape[1] // 2
+    chunked = lambda v: v.reshape(plane_nodes // nodes, nodes, latent)
+    sum_ref[...] = jnp.concatenate(
+        [chunked(total[:, :latent]), chunked(total[:, latent:])], axis=1
+    ).astype(BF16)
+
+
+def mid_kernel(parts_ref, weight_ref, gain_ref, mesh_ref, mid_ref, agg_ref, slopes_ref):
+    count = mesh_ref.shape[0]
+    summed = jnp.sum(parts_ref[...].astype(F32), axis=0)
+    agg = wide_dot(summed[:count], weight_ref[...], dot)
+    slopes_ref[...] = summed[count:]
     agg_ref[...] = agg
     mid_ref[...] = (mesh_ref[...].astype(F32) + layer_norm(agg, gain_ref[...])[0]).astype(BF16)
 
@@ -115,10 +139,7 @@
         [dot(near.astype(BF16), src_w_ref[...]), dot(mid.astype(BF16), dst_w_ref[...]) + bias_ref[...]],
         axis=0,
     )
-    pre = dot(pick_ref[...], thirds(table))
-    sigma = jax.nn.sigmoid(pre)
-    hidden = (pre * sigma).astype(BF16)
-    slope = sigma * (1.0 + pre * (1.0 - sigma))
+    hidden, slope = silu_parts(dot(pick_ref[...], thirds(table)))
     summed = dot(pick_t_ref[...], hidden)[3 * count :]
     agg = wide_dot(summed, out_w_ref[...], dot)
     shifted, normed, inv_std = layer_norm(agg, gain_ref[...])
@@ -146,29 +167,32 @@
     tiled_ref[...] = jnp.concatenate([rows] * times, axis=0).astype(BF16)
 
 
-def enc_back_kernel(grad_ref, dst_ref, dst_t_ref, slope_ref, weight_ref, edge_ref, sum_ref):
-    tile = 256
-    total = None
-    for start in range(0, slope_ref.shape[0], tile):
-        rows = dot(dst_ref[start : start + tile, :], grad_ref[...]).astype(BF16)
-        edge = (dot_t(rows, weight_ref[...]) * slope_ref[start : start + tile, :]).astype(BF16)
-        edge_ref[start : start + tile, :] = edge
-        part = dot(dst_t_ref[:, start : start + tile], edge)
-        total = part if total is None else total + part
-    sum_ref[...] = total.astype(BF16)
-
-
-def grid_kernel(edge_ref, pick_t_ref, weight_ref, own_ref, mate_ref):
-    half = edge_ref.shape[0] // 2
-    own = dot(pick_t_ref[:, :half], edge_ref[:half, :])
-    mate = dot(pick_t_ref[:, half:], edge_ref[half:, :])
-    own_ref[...] = wide_dot(own, weight_ref[...], dot_t)
-    mate_ref[...] = wide_dot(mate, weight_ref[...], dot_t).astype(BF16)
-
-
-def mesh_kernel(parts_ref, weight_ref, grad_ref, out_ref):
-    summed = chunk_sum(parts_ref, grad_ref.shape[0])
-    out_ref[...] = (grad_ref[...] + wide_dot(summed, weight_ref[...], dot_t)).astype(BF16)
+def mesh_kernel(tiled_ref, slopes_ref, grad_ref, out_w_ref, dst_w_ref, out_ref):
+    count = grad_ref.shape[0]
+    rows = dot_t(tiled_ref[: 2 * count, :], out_w_ref[...])[:count]
+    out_ref[...] = (
+        grad_ref[...] + wide_dot(rows * slopes_ref[...], dst_w_ref[...], dot_t)
+    ).astype(BF16)
+
+
+def mate_kernel(grad_ref, dst_ref, pick_t_ref, slope_ref, out_w_ref, src_w_ref, table_ref, part_ref):
+    half = dst_ref.shape[0] // 2
+    table = stack_split(dot_t(grad_ref[...], out_w_ref[...]))
+    table_ref[...] = table
+    edge = (dot(dst_ref[half:, :], table) * slope_ref[half:, :]).astype(BF16)
+    summed = dot(pick_t_ref[:, half:], edge)
+    part_ref[...] = wide_dot(summed, src_w_ref[...], dot_t).astype(BF16)
+
+
+def own_kernel(table_ref, dst_ref, pick_t_ref, slope_ref, src_w_ref, part_ref):
+    half = dst_ref.shape[0] // 2
+    edge = (dot(dst_ref[:half, :], table_ref[...]) * slope_ref[:half, :]).astype(BF16)
+    summed = dot(pick_t_ref[:, :half], edge)
+    part_ref[...] = wide_dot(summed, src_w_ref[...], dot_t)
+
+
+def join_kernel(own_ref, mate_ref, out_ref):
+    out_ref[...] = (own_ref[...] + mate_ref[...].astype(F32)).astype(BF16)
 
 
 def per_device(
@@ -205,30 +229,34 @@
     row = lambda vector: vector.reshape(1, latent)
 
     def exchange(values):
-        parts = values.reshape(chips, nodes, latent)
-        parts = lax.all_to_all(
-            parts, "feat", split_axis=0, concat_axis=0, tiled=True, axis_index_groups=plane
+        return lax.all_to_all(
+            values.reshape(chips, -1, latent), "feat", split_axis=0, concat_axis=0, tiled=True,
+            axis_index_groups=plane,
         )
-        return parts.reshape(plane_nodes, latent)
 
     def swap(values):
         return lax.ppermute(values, "feat", [(i, i ^ 1) for i in range(feats)])
 
     first = [(i, i ^ 1) for i in range(bands)]
     second = [(i, j) for i in range(1, bands - 2, 2) for i, j in ((i, i + 1), (i + 1, i))]
-
-    mesh_all = exchange(jnp.tile(mesh_latent, (chips, 1)))
-
-    mate_grid = swap(grid_latent)
-    index = jnp.stack([g2m_src, g2m_peer[:, 0], g2m_slot])
-    index = jnp.concatenate([index, swap(index)], axis=1)
-    source, peer, slot = index[0], index[1], index[2]
+    line = lambda index: index.reshape(1, edges)
+
+    tiled_mesh, pack = call(
+        prep_kernel, (shape((plane_nodes, latent), BF16), shape((grids + 16, latent), BF16)),
+        mesh_latent, grid_latent, line(g2m_src), line(g2m_peer), line(g2m_slot),
+    )
+    mate_pack = swap(pack)
+    mesh_all = exchange(tiled_mesh).reshape(plane_nodes, latent)
+
+    mate_index = mate_pack[grids : grids + 3].astype(jnp.int32)
+    joined = lambda own, place: jnp.concatenate([own, mate_index[place]])
+    source, peer, slot = joined(g2m_src, 0), joined(g2m_peer[:, 0], 1), joined(g2m_slot, 2)
     target = jnp.where(peer % 2 == core, peer // 2 * nodes + slot, -1)
     grid_ids = jnp.arange(grids, dtype=jnp.int32)
     node_ids = jnp.arange(plane_nodes, dtype=jnp.int32)
     src_pick = (source[:, None] == grid_ids[None, :]).astype(BF16)
     src_pick_t = (source[None, :] == grid_ids[:, None]).astype(BF16)
-    dst_pick = (target[:, None] == node_ids[None, :]).astype(BF16)
+    dst_pick = (target[:, None] == jnp.tile(node_ids, 2)[None, :]).astype(BF16)
     dst_pick_t = (target[None, :] == node_ids[:, None]).astype(BF16)
 
     side = proc_src // nodes
@@ -243,14 +271,16 @@
 
     pre_src = call(
         src_kernel, shape((2 * edges, latent), F32),
-        grid_latent, mate_grid, src_pick, enc_src_w, row(enc_bias),
+        grid_latent, mate_pack, src_pick, enc_src_w, row(enc_bias), flops=8e8,
     )
     partial, slope = call(
-        enc_kernel, (shape((plane_nodes, latent), BF16), shape((2 * edges, latent), F32)),
-        pre_src, dst_pick, dst_pick_t, mesh_all, enc_dst_w,
-    )
-    mid, enc_agg = call(
-        mid_kernel, (shape((nodes, latent), BF16), shape((nodes, latent), F32)),
+        enc_kernel,
+        (shape((chips, 2 * nodes, latent), BF16), shape((2 * edges, latent), F32)),
+        pre_src, dst_pick, dst_pick_t, mesh_all, enc_dst_w, flops=1.2e9,
+    )
+    mid, enc_agg, slopes = call(
+        mid_kernel,
+        (shape((nodes, latent), BF16), shape((nodes, latent), F32), shape((nodes, latent), F32)),
         exchange(partial), enc_out_w, row(enc_gain), mesh_latent,
     )
     one = lax.ppermute(mid, "band", first)
@@ -267,19 +297,19 @@
         back_kernel, (shape((nodes, latent), F32), shape((plane_nodes, latent), BF16)),
         grad_part, back_one, back_two, enc_agg, row(enc_gain),
     )
-    edge_grad, node_part = call(
-        enc_back_kernel, (shape((2 * edges, latent), BF16), shape((plane_nodes, latent), BF16)),
-        exchange(tiled), dst_pick, dst_pick_t, slope, enc_out_w,
-    )
-    node_parts = exchange(node_part)
-    own_grad, mate_grad = call(
-        grid_kernel, (shape((grids, latent), F32), shape((grids, latent), BF16)),
-        edge_grad, src_pick_t, enc_src_w,
-    )
-    grad_grid = (own_grad + swap(mate_grad).astype(F32)).astype(BF16)
+    grad_all = exchange(tiled).reshape(plane_nodes, latent)
     grad_mesh = call(
-        mesh_kernel, shape((nodes, latent), BF16), node_parts, enc_dst_w, grad_mid,
-    )
+        mesh_kernel, shape((nodes, latent), BF16), tiled, slopes, grad_mid, enc_out_w, enc_dst_w,
+    )
+    table, mate_grad = call(
+        mate_kernel, (shape((2 * plane_nodes, latent), BF16), shape((grids, latent), BF16)),
+        grad_all, dst_pick, src_pick_t, slope, enc_out_w, enc_src_w, flops=8e8,
+    )
+    own_grad = call(
+        own_kernel, shape((grids, latent), F32),
+        table, dst_pick, src_pick_t, slope, enc_src_w, flops=6e8,
+    )
+    grad_grid = call(join_kernel, shape((grids, latent), BF16), own_grad, swap(mate_grad))
     return (mesh_out, grad_grid, grad_mesh)
 
 

time: 119 us -> 117 us (0.983)
  the two profiles are of different devices: /device:TPU:72 before, /device:TPU:73 now
where the time goes in v2:
time: 117 us; the launch traced here: 116 us
  starting transfers between devices  47.4 us (41%)
  waiting for transfers between devices  31.3 us (27%)
  local copies, waits for them, and re-layouts  20.3 us (17%)
  Pallas kernels  12 us (10%)
  other arithmetic  3.83 us (3%)
    all_to_all x3, waiting for transfers between devices, exchange(): lax.all_to_all(values.reshape(chips, -1, latent), 'feat', split_axis=0, c...  29.1 us
    all_to_all x3, starting transfers between devices, exchange(): lax.all_to_all(values.reshape(chips, -1, latent), 'feat', split_axis=0, c...  20.8 us
    unnamed x66, local copies, waits for them, and re-layouts  20.2 us
    pallas_call x10, Pallas kernels, call(): pl.pallas_call(body, out_shape=out, in_specs=[pl.BlockSpec(memory_space=p...  12 us
    ppermute x2, starting transfers between devices, swap(): return lax.ppermute(values, 'feat', [(i, i ^ 1) for i in range(feats)])  9.56 us
    ppermute x1, starting transfers between devices, per_device(): back_two = lax.ppermute(rim_two, 'band', second)  7.16 us
    ppermute x1, starting transfers between devices, per_device(): one = lax.ppermute(mid, 'band', first)  4.8 us
    ppermute x1, starting transfers between devices, per_device(): two = lax.ppermute(mid, 'band', second)  3.22 us
  transfers between devices with their start and end apart: 9, of which 5 were waited for; matrix products, arithmetic and copies ran while one was open for 3% of the time, Pallas kernels for 3%

profile of v2, /device:TPU:73, one launch (start us, length us, event | category | flops | bytes accessed | tf_op | source)
XLA Modules:
  0.0 115.8 jit_solution(11408332814979221089)
XLA Ops:
  0.6 0.9 copy-done.18
  1.6 0.7 copy-done.20
  2.3 0.7 copy-done.27
  3.0 0.7 copy-done.28
  3.6 0.7 copy-done.29
  4.3 0.7 shard_map.193
  5.1 2.6 %collective-permute-start = (bf16[272,512]{1,0:T(8,128)(2,1)S(1)}, bf16[272,512]{1,0:T(8,128)(2,1)S(1)}, u32[]{:S(2)}, u32[]{:S(2)}) collective-permute-start(bf16[272,512]{1,0:T(8,128)(2,1)S(1)} %get-tuple-element.18), channel_id=1, source_target_pairs={{0,1},{1,0},{2,3},{3,2},{4,5},{5,4},{6,7},{7,6},{8,9},{9,8},{10,11... | collective-permute-start | bytes 835592 | tf_op jit(solution)/shard_map/ppermute | solution.py:238
  7.6 9.6 %all-to-all-start = ((bf16[32,8,512]{2,1,0:T(8,128)(2,1)}), bf16[32,8,512]{2,1,0:T(8,128)(2,1)S(1)}, u32[]{:S(2)}, u32[]{:S(2)}) async-start(bf16[32,8,512]{2,1,0:T(8,128)(2,1)} %bitcast.8), calls=%async_computation | async-start | bytes 524288 | tf_op jit(solution)/shard_map/all_to_all | solution.py:232
  17.3 0.7 pad_add_fusion
  18.2 0.7 fusion.8
  19.0 1.0 copy-done.2
  20.0 0.9 copy-done.19
  21.0 0.7 copy-done.23
  21.6 1.3 %shard_map.194.pre_ref = f32[1024,512]{1,0:T(8,128)S(1)} custom-call(bf16[256,512]{1,0:T(8,128)(2,1)S(1)} %copy-done.19, bf16[272,512]{1,0:T(8,128)(2,1)S(1)} %collective-permute-done.mate_ref, bf16[1024,256]{1,0:T(8,128)(2,1)S(1)} %fusion.pick_ref, bf16[512,512]{1,0:T(8,128)(2,1)S(1)} %copy-done.2, f32[1,512]{1,0:T(1,128)S(1)} %bitcast.21), custom_call_target="tpu_custom_call" | custom-call | flops 800000000 | bytes 1048576 | tf_op jit(solution)/shard_map/pallas_call | solution.py:59
  22.9 1.3 %copy-done = f32[1024,512]{1,0:T(8,128)} copy-done((f32[1024,512]{1,0:T(8,128)}, f32[1024,512]{1,0:T(8,128)S(1)}, u32[]{:S(2)}) %copy-start) | copy-done | bytes 2097176
  24.3 0.9 fusion.1.dst_t_ref
  25.4 4.0 %all-to-all-done = bf16[32,8,512]{2,1,0:T(8,128)(2,1)S(1)} async-done(((bf16[32,8,512]{2,1,0:T(8,128)(2,1)}), bf16[32,8,512]{2,1,0:T(8,128)(2,1)S(1)}, u32[]{:S(2)}, u32[]{:S(2)}) %all-to-all-start) | async-done | bytes 262176 | tf_op jit(solution)/shard_map/all_to_all | solution.py:232
  29.4 1.6 %copy-done.1 = f32[1024,512]{1,0:T(8,128)S(1)} copy-done((f32[1024,512]{1,0:T(8,128)S(1)}, f32[1024,512]{1,0:T(8,128)}, u32[]{:S(2)}) %copy-start.1) | copy-done | bytes 2097176
  31.0 1.0 copy-done.9
  32.0 1.0 copy-done.10
  33.1 2.3 %shard_map.195 = (bf16[32,16,512]{2,1,0:T(8,128)(2,1)S(1)}, f32[1024,512]{1,0:T(8,128)S(1)}) custom-call(f32[1024,512]{1,0:T(8,128)S(1)} %copy-done.1, bf16[1024,512]{1,0:T(8,128)(2,1)S(1)} %compare_convert_fusion.dst_ref, bf16[256,1024]{1,0:T(8,128)(2,1)S(1)} %copy-done.9, bf16[256,512]{1,0:T(8,128)(2,1)S(1)} %bitcast.18, bf16[512,512]{1,0:T(8,128)(2,1)S(1)} %copy-done.10), custom_call_target="tpu_custom_call" | custom-call | flops 1200000000 | bytes 1048576 | tf_op jit(solution)/shard_map/pallas_call | solution.py:59
  35.4 0.8 copy-done.17
  36.2 5.4 %all-to-all-start.1 = ((bf16[32,16,512]{2,1,0:T(8,128)(2,1)}), bf16[32,16,512]{2,1,0:T(8,128)(2,1)}, u32[]{:S(2)}, u32[]{:S(2)}) async-start(bf16[32,16,512]{2,1,0:T(8,128)(2,1)} %copy-done.17), calls=%async_computation.1 | async-start | bytes 1048576 | tf_op jit(solution)/shard_map/all_to_all | solution.py:232
  42.0 15.8 %all-to-all-done.1.parts_ref = bf16[32,16,512]{2,1,0:T(8,128)(2,1)} async-done(((bf16[32,16,512]{2,1,0:T(8,128)(2,1)}), bf16[32,16,512]{2,1,0:T(8,128)(2,1)}, u32[]{:S(2)}, u32[]{:S(2)}) %all-to-all-start.1) | async-done | bytes 524320 | tf_op jit(solution)/shard_map/all_to_all | solution.py:232
  57.8 1.0 copy-done.7
  58.8 1.4 %shard_map.196 = (bf16[8,512]{1,0:T(8,128)(2,1)S(1)}, f32[8,512]{1,0:T(8,128)S(1)}, f32[8,512]{1,0:T(8,128)S(1)}) custom-call(bf16[32,16,512]{2,1,0:T(8,128)(2,1)} %all-to-all-done.1.parts_ref, bf16[512,512]{1,0:T(8,128)(2,1)S(1)} %copy-done.7, f32[1,512]{1,0:T(1,128)S(1)} %bitcast.24, bf16[8,512]{1,0:T(8,128)(2,1)S(1)} %copy-done.21), custom_call_target="tpu_custom_call" | custom-call | flops 100000000 | bytes 1048576 | tf_op jit(solution)/shard_map/pallas_call | solution.py:59
  60.2 4.8 %collective-permute-start.1 = (bf16[8,512]{1,0:T(8,128)(2,1)S(1)}, bf16[8,512]{1,0:T(8,128)(2,1)S(1)}, u32[]{:S(2)}, u32[]{:S(2)}) collective-permute-start(bf16[8,512]{1,0:T(8,128)(2,1)S(1)} %get-tuple-element.21.mid_ref), channel_id=1, source_target_pairs={{0,64},{64,0},{128,192},{192,128},{256,320},{320,256},{384,448},{4... | collective-permute-start | bytes 24584 | tf_op jit(solution)/shard_map/ppermute | solution.py:286
  65.0 3.2 %collective-permute-start.2 = (bf16[8,512]{1,0:T(8,128)(2,1)S(1)}, bf16[8,512]{1,0:T(8,128)(2,1)S(1)}, u32[]{:S(2)}, u32[]{:S(2)}) collective-permute-start(bf16[8,512]{1,0:T(8,128)(2,1)S(1)} %get-tuple-element.21.mid_ref), channel_id=1, source_target_pairs={{64,128},{128,64},{192,256},{256,192},{320,384},{384,320},{448,512... | collective-permute-start | bytes 24584 | tf_op jit(solution)/shard_map/ppermute | solution.py:287
  68.3 1.1 collective-permute-done.2.two_ref
  69.5 1.0 copy-done.14
  70.5 1.0 copy-done.15
  71.5 1.0 copy-done.16
  72.6 1.9 %shard_map.197 = (bf16[8,512]{1,0:T(8,128)(2,1)}, bf16[8,512]{1,0:T(8,128)(2,1)S(1)}, bf16[8,512]{1,0:T(8,128)(2,1)S(1)}, f32[8,512]{1,0:T(8,128)S(1)}) custom-call(bf16[8,512]{1,0:T(8,128)(2,1)S(1)} %collective-permute-done.1.one_ref, bf16[8,512]{1,0:T(8,128)(2,1)S(1)} %get-tuple-element.21.mid_ref, bf16[8,512]{1,0:T(8,128)(2,1)S(1)} %collective-permute-done.2.two_ref, ...), custom_call_target="tpu_custom_call" | custom-call | flops 100000000 | bytes 1048576 | tf_op jit(solution)/shard_map/pallas_call | solution.py:59
  74.5 1.9 %collective-permute-start.3 = (bf16[8,512]{1,0:T(8,128)(2,1)S(1)}, bf16[8,512]{1,0:T(8,128)(2,1)S(1)}, u32[]{:S(2)}, u32[]{:S(2)}) collective-permute-start(bf16[8,512]{1,0:T(8,128)(2,1)S(1)} %get-tuple-element.24), channel_id=1, source_target_pairs={{0,64},{64,0},{128,192},{192,128},{256,320},{320,256},{384,448},{4... | collective-permute-start | bytes 24584 | tf_op jit(solution)/shard_map/ppermute | solution.py:294
  76.4 7.2 %collective-permute-start.4 = (bf16[8,512]{1,0:T(8,128)(2,1)S(1)}, bf16[8,512]{1,0:T(8,128)(2,1)S(1)}, u32[]{:S(2)}, u32[]{:S(2)}) collective-permute-start(bf16[8,512]{1,0:T(8,128)(2,1)S(1)} %get-tuple-element.25), channel_id=1, source_target_pairs={{64,128},{128,64},{192,256},{256,192},{320,384},{384,320},{448,512... | collective-permute-start | bytes 24584 | tf_op jit(solution)/shard_map/ppermute | solution.py:295
  83.6 1.0 collective-permute-done.4.two_ref
  84.9 0.7 copy-done.12
  85.6 5.7 %all-to-all-start.2 = ((bf16[32,8,512]{2,1,0:T(8,128)(2,1)}), bf16[32,8,512]{2,1,0:T(8,128)(2,1)S(1)}, u32[]{:S(2)}, u32[]{:S(2)}) async-start(bf16[32,8,512]{2,1,0:T(8,128)(2,1)} %bitcast.20), calls=%async_computation.2 | async-start | bytes 524288 | tf_op jit(solution)/shard_map/all_to_all | solution.py:232
  91.3 0.9 fusion.2.pick_t_ref
  92.2 9.3 %all-to-all-done.2 = bf16[32,8,512]{2,1,0:T(8,128)(2,1)S(1)} async-done(((bf16[32,8,512]{2,1,0:T(8,128)(2,1)}), bf16[32,8,512]{2,1,0:T(8,128)(2,1)S(1)}, u32[]{:S(2)}, u32[]{:S(2)}) %all-to-all-start.2) | async-done | bytes 262176 | tf_op jit(solution)/shard_map/all_to_all | solution.py:232
  101.5 1.0 copy-done.3
  102.6 1.0 copy-done.5
  103.6 1.0 copy-done.8
  104.7 1.3 %shard_map.199 = (bf16[512,512]{1,0:T(8,128)(2,1)S(1)}, bf16[256,512]{1,0:T(8,128)(2,1)S(1)}) custom-call(bf16[256,512]{1,0:T(8,128)(2,1)S(1)} %bitcast.19, bf16[1024,512]{1,0:T(8,128)(2,1)S(1)} %compare_convert_fusion.dst_ref, bf16[256,1024]{1,0:T(8,128)(2,1)S(1)} %copy-done.5, f32[1024,512]{1,0:T(8,128)S(1)} %get-tuple-element.28.slope_ref, ...), custom_call_target="tpu_custom_call" | custom-call | flops 800000000 | bytes 1048576 | tf_op jit(solution)/shard_map/pallas_call | solution.py:59
  106.0 7.0 %collective-permute-start.5 = (bf16[256,512]{1,0:T(8,128)(2,1)S(1)}, bf16[256,512]{1,0:T(8,128)(2,1)S(1)}, u32[]{:S(2)}, u32[]{:S(2)}) collective-permute-start(bf16[256,512]{1,0:T(8,128)(2,1)S(1)} %get-tuple-element.30), channel_id=1, source_target_pairs={{0,1},{1,0},{2,3},{3,2},{4,5},{5,4},{6,7},{7,6},{8,9},{9,8},{10,11... | collective-permute-start | bytes 786440 | tf_op jit(solution)/shard_map/ppermute | solution.py:238
  113.0 1.0 shard_map.202
  114.0 1.0 shard_map.200.own_ref
  115.0 0.7 shard_map.201
  (59 shorter events, 1.1 us)
Async XLA Ops:
  0.6 1.0 copy-start.18
  1.6 0.7 copy-start.20
  2.3 0.7 copy-start.27
  3.0 0.7 copy-start.28
  3.6 0.7 copy-start.29
  5.1 12.2 %collective-permute-start = (bf16[272,512]{1,0:T(8,128)(2,1)S(1)}, bf16[272,512]{1,0:T(8,128)(2,1)S(1)}, u32[]{:S(2)}, u32[]{:S(2)}) collective-permute-start(bf16[272,512]{1,0:T(8,128)(2,1)S(1)} %get-tuple-element.18), channel_id=1, source_target_pairs={{0,1},{1,0},{2,3},{3,2},{4,5},{5,4},{6,7},{7,6},{8,9},{9,8},{10,11... | collective-permute-start | bytes 835592 | tf_op jit(solution)/shard_map/ppermute | solution.py:238
  7.6 21.8 %all-to-all-start = ((bf16[32,8,512]{2,1,0:T(8,128)(2,1)}), bf16[32,8,512]{2,1,0:T(8,128)(2,1)S(1)}, u32[]{:S(2)}, u32[]{:S(2)}) async-start(bf16[32,8,512]{2,1,0:T(8,128)(2,1)} %bitcast.8), calls=%async_computation | async-start | bytes 524288 | tf_op jit(solution)/shard_map/all_to_all | solution.py:232
  19.0 1.0 copy-start.2
  20.0 0.9 copy-start.19
  21.0 0.7 copy-start.23
  22.9 1.3 %copy-start = (f32[1024,512]{1,0:T(8,128)}, f32[1024,512]{1,0:T(8,128)S(1)}, u32[]{:S(2)}) copy-start(f32[1024,512]{1,0:T(8,128)S(1)} %shard_map.194.pre_ref) | copy-start | bytes 6291460
  29.4 1.6 %copy-start.1 = (f32[1024,512]{1,0:T(8,128)S(1)}, f32[1024,512]{1,0:T(8,128)}, u32[]{:S(2)}) copy-start(f32[1024,512]{1,0:T(8,128)} %copy-done) | copy-start | bytes 6291460
  31.0 1.0 copy-start.9
  32.0 1.0 copy-start.10
  33.1 8.7 %copy-start.30 = (s32[256]{0:T(256)S(1)}, s32[256]{0:T(256)}, u32[]{:S(2)}) copy-start(s32[256]{0:T(256)} %param.23) | copy-start | bytes 3076
  33.1 8.7 %copy-start.31 = (s32[256]{0:T(256)S(1)}, s32[256]{0:T(256)}, u32[]{:S(2)}) copy-start(s32[256]{0:T(256)} %param.24) | copy-start | bytes 3076
  33.1 24.7 %copy-start.21 = (bf16[8,512]{1,0:T(8,128)(2,1)S(1)}, bf16[8,512]{1,0:T(8,128)(2,1)}, u32[]{:S(2)}) copy-start(bf16[8,512]{1,0:T(8,128)(2,1)} %mesh_ref.3) | copy-start | bytes 24580
  33.1 24.7 %copy-start.26 = (f32[512]{0:T(512)S(1)}, f32[512]{0:T(512)}, u32[]{:S(2)}) copy-start(f32[512]{0:T(512)} %param.29) | copy-start | bytes 6148
  35.4 0.8 copy-start.17
  36.2 33.2 %copy-start.22 = (bf16[8,512]{1,0:T(8,128)(2,1)S(1)}, bf16[8,512]{1,0:T(8,128)(2,1)}, u32[]{:S(2)}) copy-start(bf16[8,512]{1,0:T(8,128)(2,1)} %cotangent_ref.1) | copy-start | bytes 24580
  36.2 33.2 %copy-start.24 = (f32[512]{0:T(512)S(1)}, f32[512]{0:T(512)}, u32[]{:S(2)}) copy-start(f32[512]{0:T(512)} %param.33) | copy-start | bytes 6148
  36.2 33.2 %copy-start.25 = (f32[512]{0:T(512)S(1)}, f32[512]{0:T(512)}, u32[]{:S(2)}) copy-start(f32[512]{0:T(512)} %param.34) | copy-start | bytes 6148
  36.2 21.5 %all-to-all-start.1 = ((bf16[32,16,512]{2,1,0:T(8,128)(2,1)}), bf16[32,16,512]{2,1,0:T(8,128)(2,1)}, u32[]{:S(2)}, u32[]{:S(2)}) async-start(bf16[32,16,512]{2,1,0:T(8,128)(2,1)} %copy-done.17), calls=%async_computation.1 | async-start | bytes 1048576 | tf_op jit(solution)/shard_map/all_to_all | solution.py:232
  57.8 1.0 copy-start.7
  60.2 8.1 %collective-permute-start.1 = (bf16[8,512]{1,0:T(8,128)(2,1)S(1)}, bf16[8,512]{1,0:T(8,128)(2,1)S(1)}, u32[]{:S(2)}, u32[]{:S(2)}) collective-permute-start(bf16[8,512]{1,0:T(8,128)(2,1)S(1)} %get-tuple-element.21.mid_ref), channel_id=1, source_target_pairs={{0,64},{64,0},{128,192},{192,128},{256,320},{320,256},{384,448},{4... | collective-permute-start | bytes 24584 | tf_op jit(solution)/shard_map/ppermute | solution.py:286
  65.0 4.4 %collective-permute-start.2 = (bf16[8,512]{1,0:T(8,128)(2,1)S(1)}, bf16[8,512]{1,0:T(8,128)(2,1)S(1)}, u32[]{:S(2)}, u32[]{:S(2)}) collective-permute-start(bf16[8,512]{1,0:T(8,128)(2,1)S(1)} %get-tuple-element.21.mid_ref), channel_id=1, source_target_pairs={{64,128},{128,64},{192,256},{256,192},{320,384},{384,320},{448,512... | collective-permute-start | bytes 24584 | tf_op jit(solution)/shard_map/ppermute | solution.py:287
  69.4 1.0 copy-start.14
  70.5 1.0 copy-start.15
  71.5 1.0 copy-start.16
  74.5 9.1 %collective-permute-start.3 = (bf16[8,512]{1,0:T(8,128)(2,1)S(1)}, bf16[8,512]{1,0:T(8,128)(2,1)S(1)}, u32[]{:S(2)}, u32[]{:S(2)}) collective-permute-start(bf16[8,512]{1,0:T(8,128)(2,1)S(1)} %get-tuple-element.24), channel_id=1, source_target_pairs={{0,64},{64,0},{128,192},{192,128},{256,320},{320,256},{384,448},{4... | collective-permute-start | bytes 24584 | tf_op jit(solution)/shard_map/ppermute | solution.py:294
  76.4 8.2 %collective-permute-start.4 = (bf16[8,512]{1,0:T(8,128)(2,1)S(1)}, bf16[8,512]{1,0:T(8,128)(2,1)S(1)}, u32[]{:S(2)}, u32[]{:S(2)}) collective-permute-start(bf16[8,512]{1,0:T(8,128)(2,1)S(1)} %get-tuple-element.25), channel_id=1, source_target_pairs={{64,128},{128,64},{192,256},{256,192},{320,384},{384,320},{448,512... | collective-permute-start | bytes 24584 | tf_op jit(solution)/shard_map/ppermute | solution.py:295
  84.9 0.7 copy-start.12
  85.6 16.0 %all-to-all-start.2 = ((bf16[32,8,512]{2,1,0:T(8,128)(2,1)}), bf16[32,8,512]{2,1,0:T(8,128)(2,1)S(1)}, u32[]{:S(2)}, u32[]{:S(2)}) async-start(bf16[32,8,512]{2,1,0:T(8,128)(2,1)} %bitcast.20), calls=%async_computation.2 | async-start | bytes 524288 | tf_op jit(solution)/shard_map/all_to_all | solution.py:232
  101.5 1.0 copy-start.3
  102.6 1.0 copy-start.5
  103.6 1.0 copy-start.8
  104.7 8.3 %copy-start.11 = (bf16[512,512]{1,0:T(8,128)(2,1)S(1)}, bf16[512,512]{1,0:T(8,128)(2,1)}, u32[]{:S(2)}) copy-start(bf16[512,512]{1,0:T(8,128)(2,1)} %dst_w_ref.3) | copy-start | bytes 1572868
  104.7 8.3 %copy-start.13 = (bf16[256,512]{1,0:T(8,128)(2,1)S(1)}, bf16[256,512]{1,0:T(8,128)(2,1)}, u32[]{:S(2)}) copy-start(bf16[256,512]{1,0:T(8,128)(2,1)} %copy-done.12) | copy-start | bytes 786436
  104.7 9.4 %copy-start.4 = (bf16[512,512]{1,0:T(8,128)(2,1)S(1)}, bf16[512,512]{1,0:T(8,128)(2,1)}, u32[]{:S(2)}) copy-start(bf16[512,512]{1,0:T(8,128)(2,1)} %src_w_ref.5) | copy-start | bytes 1572868
  104.7 9.4 %copy-start.6 = (bf16[256,1024]{1,0:T(8,128)(2,1)S(1)}, bf16[256,1024]{1,0:T(8,128)(2,1)}, u32[]{:S(2)}) copy-start(bf16[256,1024]{1,0:T(8,128)(2,1)} %fusion.2.pick_t_ref) | copy-start | bytes 1572868
  106.0 9.1 %collective-permute-start.5 = (bf16[256,512]{1,0:T(8,128)(2,1)S(1)}, bf16[256,512]{1,0:T(8,128)(2,1)S(1)}, u32[]{:S(2)}, u32[]{:S(2)}) collective-permute-start(bf16[256,512]{1,0:T(8,128)(2,1)S(1)} %get-tuple-element.30), channel_id=1, source_target_pairs={{0,1},{1,0},{2,3},{3,2},{4,5},{5,4},{6,7},{7,6},{8,9},{9,8},{10,11... | collective-permute-start | bytes 786440 | tf_op jit(solution)/shard_map/ppermute | solution.py:238

commit v3 on v2

--- a/solution.py
+++ b/solution.py
@@ -55,15 +55,40 @@
     )
 
 
-def call(body, out, *args, flops=1e8, limit=16):
+def call(body, out, *args, far=(), far_out=(), scratch=(), limit=16, cost=1):
+    place = lambda there: pl.BlockSpec(memory_space=pltpu.HBM if there else pltpu.VMEM)
+    single = not isinstance(out, tuple)
+    outs = (out,) if single else out
+    out_specs = tuple(place(i in far_out) for i in range(len(outs)))
+    outs = tuple(
+        pltpu.HBM(one.shape, one.dtype) if i in far_out else one for i, one in enumerate(outs)
+    )
+    args = tuple(
+        pltpu.with_memory_space_constraint(arg, pltpu.HBM) if i in far else arg
+        for i, arg in enumerate(args)
+    )
     return pl.pallas_call(
         body,
-        out_shape=out,
-        in_specs=[pl.BlockSpec(memory_space=pltpu.VMEM)] * len(args),
-        out_specs=jax.tree.map(lambda _: pl.BlockSpec(memory_space=pltpu.VMEM), out),
-        compiler_params=pltpu.CompilerParams(vmem_limit_bytes=limit * 2**20),
-        cost_estimate=pl.CostEstimate(flops=int(flops), bytes_accessed=2**20, transcendentals=0),
+        out_shape=outs[0] if single else outs,
+        in_specs=[place(i in far) for i in range(len(args))],
+        out_specs=out_specs[0] if single else out_specs,
+        scratch_shapes=scratch,
+        compiler_params=pltpu.CompilerParams(vmem_limit_bytes=limit * 2**20 or None),
+        cost_estimate=pl.CostEstimate(
+            flops=cost * 4 * 10**9, bytes_accessed=cost * 2**22, transcendentals=0
+        ),
     )(*args)
+
+
+def row_copies(source, target, sems, tile, offset=0):
+    return [
+        pltpu.make_async_copy(
+            source.at[offset + i * tile : offset + (i + 1) * tile, :],
+            target.at[i * tile : (i + 1) * tile, :],
+            sems.at[i],
+        )
+        for i in range(sems.shape[0])
+    ]
 
 
 def silu_parts(values):
@@ -72,26 +97,42 @@
     return hidden.astype(BF16), sigma * (1.0 + (values - hidden))
 
 
-def prep_kernel(mesh_ref, grid_ref, src_ref, peer_ref, slot_ref, tiled_ref, pack_ref):
-    count, latent = mesh_ref.shape
+def prep_kernel(
+    mesh_ref, grid_ref, src_ref, peer_ref, slot_ref, tiled_ref, pack_ref, mesh_buf, index_buf, sems
+):
+    count, latent = mesh_buf.shape
+    grids = grid_ref.shape[0]
+    copies = [
+        pltpu.make_async_copy(mesh_ref, mesh_buf, sems.at[0]),
+        pltpu.make_async_copy(src_ref, index_buf.at[0], sems.at[1]),
+        pltpu.make_async_copy(peer_ref, index_buf.at[1], sems.at[2]),
+        pltpu.make_async_copy(slot_ref, index_buf.at[2], sems.at[3]),
+        pltpu.make_async_copy(grid_ref, pack_ref.at[:grids, :], sems.at[4]),
+    ]
+    for copy in copies:
+        copy.start()
+    for copy in copies[:4]:
+        copy.wait()
     times = tiled_ref.shape[0] // count
-    rows = mesh_ref[...].astype(F32)
+    rows = mesh_buf[...].astype(F32)
     tiled_ref[...] = jnp.concatenate([rows] * times, axis=0).astype(BF16)
-    grids = grid_ref.shape[0]
-    pack_ref[:grids, :] = grid_ref[...]
     spare = pack_ref.shape[0] - grids
     place = lax.broadcasted_iota(jnp.int32, (spare, latent), 0)
-    index = jnp.where(place == 0, src_ref[...], jnp.where(place == 1, peer_ref[...], slot_ref[...]))
+    index = jnp.where(place == 0, index_buf[0], jnp.where(place == 1, index_buf[1], index_buf[2]))
     pack_ref[grids:, :] = index.astype(F32).astype(BF16)
-
-
-def src_kernel(own_ref, mate_ref, pick_ref, weight_ref, bias_ref, pre_ref):
+    copies[4].wait()
+
+
+def src_kernel(own_ref, mate_ref, pick_ref, weight_ref, bias_ref, pre_ref, buf, sems):
     tile = own_ref.shape[0]
-    edges = pick_ref.shape[0]
-    for start in range(0, edges, tile):
-        grid_ref = own_ref if start < edges // 2 else mate_ref
-        rows = dot(pick_ref[start : start + tile, :], grid_ref[:tile, :]).astype(BF16)
-        pre_ref[start : start + tile, :] = dot(rows, weight_ref[...]) + bias_ref[...]
+    copies = row_copies(buf, pre_ref, sems, tile)
+    for i, copy in enumerate(copies):
+        grid_ref = own_ref if i < len(copies) // 2 else mate_ref
+        rows = dot(pick_ref[i * tile : (i + 1) * tile, :], grid_ref[:tile, :]).astype(BF16)
+        buf[i * tile : (i + 1) * tile, :] = dot(rows, weight_ref[...]) + bias_ref[...]
+        copy.start()
+    for copy in copies:
+        copy.wait()
 
 
 def stack_split(values):
@@ -99,24 +140,40 @@
     return jnp.concatenate([high, values - high], axis=0).astype(BF16)
 
 
-def enc_kernel(pre_ref, dst_ref, dst_t_ref, mesh_ref, weight_ref, sum_ref, slope_ref):
-    tile = 256
-    latent = pre_ref.shape[1]
+def spread_rows(pick, table):
+    half = table.shape[0] // 2
+    return dot(pick, table[:half]) + dot(pick, table[half:])
+
+
+def enc_kernel(
+    pre_ref, dst_ref, dst_t_ref, mesh_ref, weight_ref, sum_ref, slope_ref,
+    pre_buf, slope_buf, both, in_sems, out_sems,
+):
+    latent = weight_ref.shape[1]
     plane_nodes = mesh_ref.shape[0]
+    tile = pre_buf.shape[0] // in_sems.shape[0]
+    arriving = row_copies(pre_ref, pre_buf, in_sems, tile)
+    leaving = row_copies(slope_buf, slope_ref, out_sems, tile)
+    for copy in arriving:
+        copy.start()
     table = stack_split(dot(mesh_ref[...], weight_ref[...]))
-    total = None
-    for start in range(0, pre_ref.shape[0], tile):
-        pre = pre_ref[start : start + tile, :] + dot(dst_ref[start : start + tile, :], table)
-        hidden, slope = silu_parts(pre)
-        slope_ref[start : start + tile, :] = slope
-        both = jnp.concatenate([hidden, slope.astype(BF16)], axis=1)
-        part = dot(dst_t_ref[:, start : start + tile], both)
-        total = part if total is None else total + part
+    for i in range(len(arriving)):
+        rows = slice(i * tile, (i + 1) * tile)
+        spread = spread_rows(dst_ref[rows, :], table)
+        arriving[i].wait()
+        hidden, slope = silu_parts(pre_buf[rows, :] + spread)
+        slope_buf[rows, :] = slope
+        leaving[i].start()
+        both[rows, :latent] = hidden
+        both[rows, latent:] = slope.astype(BF16)
+    total = dot(dst_t_ref[...], both[...])
     nodes = sum_ref.shape[1] // 2
     chunked = lambda v: v.reshape(plane_nodes // nodes, nodes, latent)
     sum_ref[...] = jnp.concatenate(
         [chunked(total[:, :latent]), chunked(total[:, latent:])], axis=1
     ).astype(BF16)
+    for copy in leaving:
+        copy.wait()
 
 
 def mid_kernel(parts_ref, weight_ref, gain_ref, mesh_ref, mid_ref, agg_ref, slopes_ref):
@@ -175,19 +232,33 @@
     ).astype(BF16)
 
 
-def mate_kernel(grad_ref, dst_ref, pick_t_ref, slope_ref, out_w_ref, src_w_ref, table_ref, part_ref):
+def mate_kernel(
+    grad_ref, dst_ref, pick_t_ref, slope_ref, out_w_ref, src_w_ref, table_ref, part_ref, buf, sems
+):
     half = dst_ref.shape[0] // 2
+    tile = half // sems.shape[0]
+    arriving = row_copies(slope_ref, buf, sems, tile, half)
+    for copy in arriving:
+        copy.start()
     table = stack_split(dot_t(grad_ref[...], out_w_ref[...]))
     table_ref[...] = table
-    edge = (dot(dst_ref[half:, :], table) * slope_ref[half:, :]).astype(BF16)
-    summed = dot(pick_t_ref[:, half:], edge)
+    spread = spread_rows(dst_ref[half:, :], table)
+    for copy in arriving:
+        copy.wait()
+    summed = dot(pick_t_ref[:, half:], (spread * buf[...]).astype(BF16))
     part_ref[...] = wide_dot(summed, src_w_ref[...], dot_t).astype(BF16)
 
 
-def own_kernel(table_ref, dst_ref, pick_t_ref, slope_ref, src_w_ref, part_ref):
+def own_kernel(table_ref, dst_ref, pick_t_ref, slope_ref, src_w_ref, part_ref, buf, sems):
     half = dst_ref.shape[0] // 2
-    edge = (dot(dst_ref[:half, :], table_ref[...]) * slope_ref[:half, :]).astype(BF16)
-    summed = dot(pick_t_ref[:, :half], edge)
+    tile = half // sems.shape[0]
+    arriving = row_copies(slope_ref, buf, sems, tile)
+    for copy in arriving:
+        copy.start()
+    spread = spread_rows(dst_ref[:half, :], table_ref[...])
+    for copy in arriving:
+        copy.wait()
+    summed = dot(pick_t_ref[:, :half], (spread * buf[...]).astype(BF16))
     part_ref[...] = wide_dot(summed, src_w_ref[...], dot_t)
 
 
@@ -240,10 +311,14 @@
     first = [(i, i ^ 1) for i in range(bands)]
     second = [(i, j) for i in range(1, bands - 2, 2) for i, j in ((i, i + 1), (i + 1, i))]
     line = lambda index: index.reshape(1, edges)
+    sem = lambda count: pltpu.SemaphoreType.DMA((count,))
+    wide = pltpu.VMEM((2 * edges, latent), F32)
 
     tiled_mesh, pack = call(
         prep_kernel, (shape((plane_nodes, latent), BF16), shape((grids + 16, latent), BF16)),
         mesh_latent, grid_latent, line(g2m_src), line(g2m_peer), line(g2m_slot),
+        far=range(5),
+        scratch=(pltpu.VMEM((nodes, latent), BF16), pltpu.VMEM((3, 1, edges), jnp.int32), sem(5)),
     )
     mate_pack = swap(pack)
     mesh_all = exchange(tiled_mesh).reshape(plane_nodes, latent)
@@ -256,7 +331,7 @@
     node_ids = jnp.arange(plane_nodes, dtype=jnp.int32)
     src_pick = (source[:, None] == grid_ids[None, :]).astype(BF16)
     src_pick_t = (source[None, :] == grid_ids[:, None]).astype(BF16)
-    dst_pick = (target[:, None] == jnp.tile(node_ids, 2)[None, :]).astype(BF16)
+    dst_pick = (target[:, None] == node_ids[None, :]).astype(BF16)
     dst_pick_t = (target[None, :] == node_ids[:, None]).astype(BF16)
 
     side = proc_src // nodes
@@ -271,12 +346,15 @@
 
     pre_src = call(
         src_kernel, shape((2 * edges, latent), F32),
-        grid_latent, mate_pack, src_pick, enc_src_w, row(enc_bias), flops=8e8,
+        grid_latent, mate_pack, src_pick, enc_src_w, row(enc_bias),
+        far_out=(0,), scratch=(wide, sem(4)),
     )
     partial, slope = call(
         enc_kernel,
         (shape((chips, 2 * nodes, latent), BF16), shape((2 * edges, latent), F32)),
-        pre_src, dst_pick, dst_pick_t, mesh_all, enc_dst_w, flops=1.2e9,
+        pre_src, dst_pick, dst_pick_t, mesh_all, enc_dst_w,
+        far=(0,), far_out=(1,), limit=16,
+        scratch=(wide, wide, pltpu.VMEM((2 * edges, 2 * latent), BF16), sem(4), sem(4)),
     )
     mid, enc_agg, slopes = call(
         mid_kernel,
@@ -303,11 +381,13 @@
     )
     table, mate_grad = call(
         mate_kernel, (shape((2 * plane_nodes, latent), BF16), shape((grids, latent), BF16)),
-        grad_all, dst_pick, src_pick_t, slope, enc_out_w, enc_src_w, flops=8e8,
+        grad_all, dst_pick, src_pick_t, slope, enc_out_w, enc_src_w, far=(3,), limit=16,
+        scratch=(pltpu.VMEM((edges, latent), F32), sem(2)),
     )
     own_grad = call(
         own_kernel, shape((grids, latent), F32),
-        table, dst_pick, src_pick_t, slope, enc_src_w, flops=6e8,
+        table, dst_pick, src_pick_t, slope, enc_src_w, far=(3,), limit=16,
+        scratch=(pltpu.VMEM((edges, latent), F32), sem(2)),
     )
     grad_grid = call(join_kernel, shape((grids, latent), BF16), own_grad, swap(mate_grad))
     return (mesh_out, grad_grid, grad_mesh)

time: 117 us -> 104 us (0.89)
  local copies, waits for them, and re-layouts: 20.3 us -> 0.19 us
  Pallas kernels: 12 us -> 19.1 us
  waiting for transfers between devices: 31.3 us -> 35.2 us
  other arithmetic: 3.83 us -> 0.81 us
    unnamed x66 -> x36, local copies, waits for them, and re-layouts: 20.2 us -> 0.1 us
    pallas_call x10, Pallas kernels: 12 us -> 19.1 us  [call(): pl.pallas_call(body, out_shape=outs[0] if single else outs, in_specs=[pla...]
    all_to_all x3, waiting for transfers between devices: 29.1 us -> 32.7 us  [exchange(): lax.all_to_all(values.reshape(chips, -1, latent), 'feat', split_axis=0, c...]
  transfers between devices with their start and end apart: 9 -> 9, of which waited for: 5 -> 5; matrix products, arithmetic and copies ran while one was open for 3% -> 1% of each run, Pallas kernels for 3% -> 6%
where the time goes in v3:
time: 104 us; the launch traced here: 103 us
  starting transfers between devices  46.9 us (45%)
  waiting for transfers between devices  35.2 us (34%)
  Pallas kernels  19.1 us (18%)
  between operations  1.1 us (1%)
    all_to_all x3, waiting for transfers between devices, exchange(): lax.all_to_all(values.reshape(chips, -1, latent), 'feat', split_axis=0, c...  32.7 us
    all_to_all x3, starting transfers between devices, exchange(): lax.all_to_all(values.reshape(chips, -1, latent), 'feat', split_axis=0, c...  20.3 us
    pallas_call x10, Pallas kernels, call(): pl.pallas_call(body, out_shape=outs[0] if single else outs, in_specs=[pla...  19.1 us
    ppermute x2, starting transfers between devices, swap(): return lax.ppermute(values, 'feat', [(i, i ^ 1) for i in range(feats)])  9.67 us
    ppermute x1, starting transfers between devices, per_device(): back_two = lax.ppermute(rim_two, 'band', second)  6.81 us
    ppermute x1, starting transfers between devices, per_device(): one = lax.ppermute(mid, 'band', first)  5.25 us
    ppermute x1, starting transfers between devices, per_device(): two = lax.ppermute(mid, 'band', second)  2.87 us
  transfers between devices with their start and end apart: 9, of which 5 were waited for; matrix products, arithmetic and copies ran while one was open for 1% of the time, Pallas kernels for 6%

profile of v3, /device:TPU:73, one launch (start us, length us, event | category | flops | bytes accessed | tf_op | source)
XLA Modules:
  0.0 103.3 jit_solution(1666378784361831210)
XLA Ops:
  0.6 0.0 copy-start.13
  0.6 0.0 copy-start.14
  0.7 1.8 %shard_map.193 = (bf16[256,512]{1,0:T(8,128)(2,1)}, bf16[272,512]{1,0:T(8,128)(2,1)S(1)}) custom-call(bf16[8,512]{1,0:T(8,128)(2,1)} %mesh_ref.3, bf16[256,512]{1,0:T(8,128)(2,1)} %own_ref.1, s32[1,512]{1,0:T(1,128)} %bitcast.28, s32[1,512]{1,0:T(1,128)} %bitcast.25, s32[1,512]{1,0:T(1,128)} %bitcast.27), custom_call_target="tpu_custom_call" | custom-call | flops 4000000000 | bytes 4194304 | tf_op jit(solution)/shard_map/pallas_call | solution.py:70
  2.4 0.0 copy-start.5
  2.5 0.0 copy-start.6
  2.5 0.0 copy-start.9
  2.5 2.7 %collective-permute-start = (bf16[272,512]{1,0:T(8,128)(2,1)S(1)}, bf16[272,512]{1,0:T(8,128)(2,1)S(1)}, u32[]{:S(2)}, u32[]{:S(2)}) collective-permute-start(bf16[272,512]{1,0:T(8,128)(2,1)S(1)} %get-tuple-element.18), channel_id=1, source_target_pairs={{0,1},{1,0},{2,3},{3,2},{4,5},{5,4},{6,7},{7,6},{8,9},{9,8},{10,11... | collective-permute-start | bytes 835592 | tf_op jit(solution)/shard_map/ppermute | solution.py:309
  5.2 9.6 %all-to-all-start = ((bf16[32,8,512]{2,1,0:T(8,128)(2,1)}), bf16[32,8,512]{2,1,0:T(8,128)(2,1)S(1)}, u32[]{:S(2)}, u32[]{:S(2)}) async-start(bf16[32,8,512]{2,1,0:T(8,128)(2,1)} %bitcast.8), calls=%async_computation | async-start | bytes 524288 | tf_op jit(solution)/shard_map/all_to_all | solution.py:303
  14.8 0.0 collective-permute-done.mate_ref
  14.9 0.2 fusion.1.dst_ref
  15.1 0.1 fusion.2.dst_t_ref
  15.3 0.2 fusion.pick_ref
  15.5 0.0 copy-start.3
  15.5 2.1 %shard_map.194.pre_ref = f32[1024,512]{1,0:T(8,128)} custom-call(bf16[256,512]{1,0:T(8,128)(2,1)S(1)} %copy-done.6, bf16[272,512]{1,0:T(8,128)(2,1)S(1)} %collective-permute-done.mate_ref, bf16[1024,256]{1,0:T(8,128)(2,1)S(1)} %fusion.pick_ref, bf16[512,512]{1,0:T(8,128)(2,1)S(1)} %copy-done.5, f32[1,512]{1,0:T(1,128)S(1)} %bitcast.17), custom_call_target="tpu_custom_call" | custom-call | flops 4000000000 | bytes 4194304 | tf_op jit(solution)/shard_map/pallas_call | solution.py:70
  17.7 9.3 %all-to-all-done = bf16[32,8,512]{2,1,0:T(8,128)(2,1)S(1)} async-done(((bf16[32,8,512]{2,1,0:T(8,128)(2,1)}), bf16[32,8,512]{2,1,0:T(8,128)(2,1)S(1)}, u32[]{:S(2)}, u32[]{:S(2)}) %all-to-all-start) | async-done | bytes 262176 | tf_op jit(solution)/shard_map/all_to_all | solution.py:303
  27.0 0.0 copy-start.7
  27.0 0.0 copy-start.12
  27.0 5.0 %shard_map.195 = (bf16[32,16,512]{2,1,0:T(8,128)(2,1)}, f32[1024,512]{1,0:T(8,128)}) custom-call(f32[1024,512]{1,0:T(8,128)} %shard_map.194.pre_ref, bf16[1024,256]{1,0:T(8,128)(2,1)S(1)} %fusion.1.dst_ref, bf16[256,1024]{1,0:T(8,128)(2,1)S(1)} %fusion.2.dst_t_ref, bf16[256,512]{1,0:T(8,128)(2,1)S(1)} %bitcast.15, bf16[512,512]{1,0:T(8,128)(2,1)S(1)} %copy-done.3), custom_call_target="tpu_custom_call" | custom-call | flops 4000000000 | bytes 4194304 | tf_op jit(solution)/shard_map/pallas_call | solution.py:70
  32.0 4.5 %all-to-all-start.1 = ((bf16[32,16,512]{2,1,0:T(8,128)(2,1)}), bf16[32,16,512]{2,1,0:T(8,128)(2,1)S(1)}, u32[]{:S(2)}, u32[]{:S(2)}) async-start(bf16[32,16,512]{2,1,0:T(8,128)(2,1)} %get-tuple-element.20), calls=%async_computation.1 | async-start | bytes 1048576 | tf_op jit(solution)/shard_map/all_to_all | solution.py:303
  36.5 0.1 eq.145
  36.6 0.1 or_convert_fusion.pick_ref
  36.8 15.4 %all-to-all-done.1.parts_ref = bf16[32,16,512]{2,1,0:T(8,128)(2,1)S(1)} async-done(((bf16[32,16,512]{2,1,0:T(8,128)(2,1)}), bf16[32,16,512]{2,1,0:T(8,128)(2,1)S(1)}, u32[]{:S(2)}, u32[]{:S(2)}) %all-to-all-start.1) | async-done | bytes 524320 | tf_op jit(solution)/shard_map/all_to_all | solution.py:303
  52.1 0.0 copy-start
  52.1 0.0 copy-start.1
  52.2 0.0 copy-start.2
  52.2 0.0 copy-start.8
  52.2 0.0 copy-start.10
  52.2 0.0 copy-start.11
  52.2 0.4 shard_map.196
  52.6 5.2 %collective-permute-start.1 = (bf16[8,512]{1,0:T(8,128)(2,1)S(1)}, bf16[8,512]{1,0:T(8,128)(2,1)S(1)}, u32[]{:S(2)}, u32[]{:S(2)}) collective-permute-start(bf16[8,512]{1,0:T(8,128)(2,1)S(1)} %get-tuple-element.21.mid_ref), channel_id=1, source_target_pairs={{0,64},{64,0},{128,192},{192,128},{256,320},{320,256},{384,448},{4... | collective-permute-start | bytes 24584 | tf_op jit(solution)/shard_map/ppermute | solution.py:364
  57.9 2.9 %collective-permute-start.2 = (bf16[8,512]{1,0:T(8,128)(2,1)S(1)}, bf16[8,512]{1,0:T(8,128)(2,1)S(1)}, u32[]{:S(2)}, u32[]{:S(2)}) collective-permute-start(bf16[8,512]{1,0:T(8,128)(2,1)S(1)} %get-tuple-element.21.mid_ref), channel_id=1, source_target_pairs={{64,128},{128,64},{192,256},{256,192},{320,384},{384,320},{448,512... | collective-permute-start | bytes 24584 | tf_op jit(solution)/shard_map/ppermute | solution.py:365
  60.8 0.0 collective-permute-done.1.one_ref
  60.8 1.5 %collective-permute-done.2.two_ref = bf16[8,512]{1,0:T(8,128)(2,1)S(1)} collective-permute-done((bf16[8,512]{1,0:T(8,128)(2,1)S(1)}, bf16[8,512]{1,0:T(8,128)(2,1)S(1)}, u32[]{:S(2)}, u32[]{:S(2)}) %collective-permute-start.2) | collective-permute-done | bytes 8224 | tf_op jit(solution)/shard_map/ppermute | solution.py:365
  62.3 1.9 %shard_map.197 = (bf16[8,512]{1,0:T(8,128)(2,1)}, bf16[8,512]{1,0:T(8,128)(2,1)S(1)}, bf16[8,512]{1,0:T(8,128)(2,1)S(1)}, f32[8,512]{1,0:T(8,128)S(1)}) custom-call(bf16[8,512]{1,0:T(8,128)(2,1)S(1)} %collective-permute-done.1.one_ref, bf16[8,512]{1,0:T(8,128)(2,1)S(1)} %get-tuple-element.21.mid_ref, bf16[8,512]{1,0:T(8,128)(2,1)S(1)} %collective-permute-done.2.two_ref, ...), custom_call_target="tpu_custom_call" | custom-call | flops 4000000000 | bytes 4194304 | tf_op jit(solution)/shard_map/pallas_call | solution.py:70
  64.2 1.9 %collective-permute-start.3 = (bf16[8,512]{1,0:T(8,128)(2,1)S(1)}, bf16[8,512]{1,0:T(8,128)(2,1)S(1)}, u32[]{:S(2)}, u32[]{:S(2)}) collective-permute-start(bf16[8,512]{1,0:T(8,128)(2,1)S(1)} %get-tuple-element.24), channel_id=1, source_target_pairs={{0,64},{64,0},{128,192},{192,128},{256,320},{320,256},{384,448},{4... | collective-permute-start | bytes 24584 | tf_op jit(solution)/shard_map/ppermute | solution.py:372
  66.1 6.8 %collective-permute-start.4 = (bf16[8,512]{1,0:T(8,128)(2,1)S(1)}, bf16[8,512]{1,0:T(8,128)(2,1)S(1)}, u32[]{:S(2)}, u32[]{:S(2)}) collective-permute-start(bf16[8,512]{1,0:T(8,128)(2,1)S(1)} %get-tuple-element.25), channel_id=1, source_target_pairs={{64,128},{128,64},{192,256},{256,192},{320,384},{384,320},{448,512... | collective-permute-start | bytes 24584 | tf_op jit(solution)/shard_map/ppermute | solution.py:373
  72.9 0.0 collective-permute-done.3.one_ref
  73.0 1.0 collective-permute-done.4.two_ref
  74.0 1.0 shard_map.198
  74.9 6.2 %all-to-all-start.2 = ((bf16[32,8,512]{2,1,0:T(8,128)(2,1)}), bf16[32,8,512]{2,1,0:T(8,128)(2,1)S(1)}, u32[]{:S(2)}, u32[]{:S(2)}) async-start(bf16[32,8,512]{2,1,0:T(8,128)(2,1)} %bitcast.13), calls=%async_computation.2 | async-start | bytes 524288 | tf_op jit(solution)/shard_map/all_to_all | solution.py:303
  81.2 0.1 fusion.3.pick_t_ref
  81.3 2.0 %shard_map.202 = bf16[8,512]{1,0:T(8,128)(2,1)} custom-call(bf16[256,512]{1,0:T(8,128)(2,1)} %get-tuple-element.27.tiled_ref, f32[8,512]{1,0:T(8,128)S(1)} %get-tuple-element.31.slopes_ref, f32[8,512]{1,0:T(8,128)S(1)} %get-tuple-element.32.grad_ref, bf16[512,512]{1,0:T(8,128)(2,1)S(1)} %copy-done.4, bf16[512,512]{1,0:T(8,128)(2,1)S(1)} %copy-done.3), custom_call_target="tpu_custom_call" | custom-call | flops 4000000000 | bytes 4194304 | tf_op jit(solution)/shard_map/pallas_call | solution.py:70
  83.3 8.1 %all-to-all-done.2 = bf16[32,8,512]{2,1,0:T(8,128)(2,1)S(1)} async-done(((bf16[32,8,512]{2,1,0:T(8,128)(2,1)}), bf16[32,8,512]{2,1,0:T(8,128)(2,1)S(1)}, u32[]{:S(2)}, u32[]{:S(2)}) %all-to-all-start.2) | async-done | bytes 262176 | tf_op jit(solution)/shard_map/all_to_all | solution.py:303
  91.3 2.3 %shard_map.199 = (bf16[512,512]{1,0:T(8,128)(2,1)S(1)}, bf16[256,512]{1,0:T(8,128)(2,1)S(1)}) custom-call(bf16[256,512]{1,0:T(8,128)(2,1)S(1)} %bitcast.16, bf16[1024,256]{1,0:T(8,128)(2,1)S(1)} %fusion.1.dst_ref, bf16[256,1024]{1,0:T(8,128)(2,1)S(1)} %fusion.3.pick_t_ref, f32[1024,512]{1,0:T(8,128)} %get-tuple-element.28.slope_ref, ...), custom_call_target="tpu_custom_call" | custom-call | flops 4000000000 | bytes 4194304 | tf_op jit(solution)/shard_map/pallas_call | solution.py:70
  93.6 7.0 %collective-permute-start.5 = (bf16[256,512]{1,0:T(8,128)(2,1)S(1)}, bf16[256,512]{1,0:T(8,128)(2,1)S(1)}, u32[]{:S(2)}, u32[]{:S(2)}) collective-permute-start(bf16[256,512]{1,0:T(8,128)(2,1)S(1)} %get-tuple-element.30), channel_id=1, source_target_pairs={{0,1},{1,0},{2,3},{3,2},{4,5},{5,4},{6,7},{7,6},{8,9},{9,8},{10,11... | collective-permute-start | bytes 786440 | tf_op jit(solution)/shard_map/ppermute | solution.py:309
  100.6 2.0 %shard_map.200.own_ref = f32[256,512]{1,0:T(8,128)S(1)} custom-call(bf16[512,512]{1,0:T(8,128)(2,1)S(1)} %get-tuple-element.29.table_ref, bf16[1024,256]{1,0:T(8,128)(2,1)S(1)} %fusion.1.dst_ref, bf16[256,1024]{1,0:T(8,128)(2,1)S(1)} %fusion.3.pick_t_ref, f32[1024,512]{1,0:T(8,128)} %get-tuple-element.28.slope_ref, bf16[512,512]{1,0:T(8,128)(2,1)S(1)} %copy-done.5), custom_call_target="tpu_custom_call" | custom-call | flops 4000000000 | bytes 4194304 | tf_op jit(solution)/shard_map/pallas_call | solution.py:70
  102.6 0.0 collective-permute-done.5.mate_ref
  102.6 0.7 shard_map.201
  (29 shorter events, 0.1 us)
Async XLA Ops:
  0.6 14.2 %copy-start.13 = (s32[512,1]{0,1:T(1,128)S(1)}, s32[512,1]{0,1:T(1,128)}, u32[]{:S(2)}) copy-start(s32[512,1]{0,1:T(1,128)} %param.21) | copy-start | bytes 6148
  0.6 14.2 %copy-start.14 = (s32[512]{0:T(512)S(1)}, s32[512]{0:T(512)}, u32[]{:S(2)}) copy-start(s32[512]{0:T(512)} %param.22) | copy-start | bytes 6148
  0.7 14.6 %copy-start.15 = (s32[512]{0:T(512)S(1)}, s32[512]{0:T(512)}, u32[]{:S(2)}) copy-start(s32[512]{0:T(512)} %param.20) | copy-start | bytes 6148
  2.4 13.0 %copy-start.5 = (bf16[512,512]{1,0:T(8,128)(2,1)S(1)}, bf16[512,512]{1,0:T(8,128)(2,1)}, u32[]{:S(2)}) copy-start(bf16[512,512]{1,0:T(8,128)(2,1)} %src_w_ref.5) | copy-start | bytes 1572868
  2.5 13.0 %copy-start.6 = (bf16[256,512]{1,0:T(8,128)(2,1)S(1)}, bf16[256,512]{1,0:T(8,128)(2,1)}, u32[]{:S(2)}) copy-start(bf16[256,512]{1,0:T(8,128)(2,1)} %own_ref.1) | copy-start | bytes 786436
  2.5 13.0 %copy-start.9 = (f32[512]{0:T(512)S(1)}, f32[512]{0:T(512)}, u32[]{:S(2)}) copy-start(f32[512]{0:T(512)} %param.28) | copy-start | bytes 6148
  2.5 12.4 %collective-permute-start = (bf16[272,512]{1,0:T(8,128)(2,1)S(1)}, bf16[272,512]{1,0:T(8,128)(2,1)S(1)}, u32[]{:S(2)}, u32[]{:S(2)}) collective-permute-start(bf16[272,512]{1,0:T(8,128)(2,1)S(1)} %get-tuple-element.18), channel_id=1, source_target_pairs={{0,1},{1,0},{2,3},{3,2},{4,5},{5,4},{6,7},{7,6},{8,9},{9,8},{10,11... | collective-permute-start | bytes 835592 | tf_op jit(solution)/shard_map/ppermute | solution.py:309
  5.2 21.8 %all-to-all-start = ((bf16[32,8,512]{2,1,0:T(8,128)(2,1)}), bf16[32,8,512]{2,1,0:T(8,128)(2,1)S(1)}, u32[]{:S(2)}, u32[]{:S(2)}) async-start(bf16[32,8,512]{2,1,0:T(8,128)(2,1)} %bitcast.8), calls=%async_computation | async-start | bytes 524288 | tf_op jit(solution)/shard_map/all_to_all | solution.py:303
  15.5 11.5 %copy-start.3 = (bf16[512,512]{1,0:T(8,128)(2,1)S(1)}, bf16[512,512]{1,0:T(8,128)(2,1)}, u32[]{:S(2)}) copy-start(bf16[512,512]{1,0:T(8,128)(2,1)} %dst_w_ref.3) | copy-start | bytes 1572868
  27.0 9.6 %copy-start.16 = (s32[256]{0:T(256)S(1)}, s32[256]{0:T(256)}, u32[]{:S(2)}) copy-start(s32[256]{0:T(256)} %param.23) | copy-start | bytes 3076
  27.0 9.6 %copy-start.17 = (s32[256]{0:T(256)S(1)}, s32[256]{0:T(256)}, u32[]{:S(2)}) copy-start(s32[256]{0:T(256)} %param.24) | copy-start | bytes 3076
  27.0 25.1 %copy-start.4 = (bf16[512,512]{1,0:T(8,128)(2,1)S(1)}, bf16[512,512]{1,0:T(8,128)(2,1)}, u32[]{:S(2)}) copy-start(bf16[512,512]{1,0:T(8,128)(2,1)} %out_w_ref.5) | copy-start | bytes 1572868
  27.0 25.1 %copy-start.7 = (bf16[8,512]{1,0:T(8,128)(2,1)S(1)}, bf16[8,512]{1,0:T(8,128)(2,1)}, u32[]{:S(2)}) copy-start(bf16[8,512]{1,0:T(8,128)(2,1)} %mesh_ref.3) | copy-start | bytes 24580
  27.0 25.1 %copy-start.12 = (f32[512]{0:T(512)S(1)}, f32[512]{0:T(512)}, u32[]{:S(2)}) copy-start(f32[512]{0:T(512)} %param.29) | copy-start | bytes 6148
  32.0 20.1 %all-to-all-start.1 = ((bf16[32,16,512]{2,1,0:T(8,128)(2,1)}), bf16[32,16,512]{2,1,0:T(8,128)(2,1)S(1)}, u32[]{:S(2)}, u32[]{:S(2)}) async-start(bf16[32,16,512]{2,1,0:T(8,128)(2,1)} %get-tuple-element.20), calls=%async_computation.1 | async-start | bytes 1048576 | tf_op jit(solution)/shard_map/all_to_all | solution.py:303
  52.1 10.1 %copy-start = (bf16[512,512]{1,0:T(8,128)(2,1)S(1)}, bf16[512,512]{1,0:T(8,128)(2,1)}, u32[]{:S(2)}) copy-start(bf16[512,512]{1,0:T(8,128)(2,1)} %src_w_ref.3) | copy-start | bytes 1572868
  52.1 10.1 %copy-start.1 = (bf16[512,512]{1,0:T(8,128)(2,1)S(1)}, bf16[512,512]{1,0:T(8,128)(2,1)}, u32[]{:S(2)}) copy-start(bf16[512,512]{1,0:T(8,128)(2,1)} %dst_w_ref.2) | copy-start | bytes 1572868
  52.2 10.1 %copy-start.2 = (bf16[512,512]{1,0:T(8,128)(2,1)S(1)}, bf16[512,512]{1,0:T(8,128)(2,1)}, u32[]{:S(2)}) copy-start(bf16[512,512]{1,0:T(8,128)(2,1)} %out_w_ref.3) | copy-start | bytes 1572868
  52.2 10.1 %copy-start.8 = (bf16[8,512]{1,0:T(8,128)(2,1)S(1)}, bf16[8,512]{1,0:T(8,128)(2,1)}, u32[]{:S(2)}) copy-start(bf16[8,512]{1,0:T(8,128)(2,1)} %cotangent_ref.1) | copy-start | bytes 24580
  52.2 10.1 %copy-start.10 = (f32[512]{0:T(512)S(1)}, f32[512]{0:T(512)}, u32[]{:S(2)}) copy-start(f32[512]{0:T(512)} %param.33) | copy-start | bytes 6148
  52.2 10.1 %copy-start.11 = (f32[512]{0:T(512)S(1)}, f32[512]{0:T(512)}, u32[]{:S(2)}) copy-start(f32[512]{0:T(512)} %param.34) | copy-start | bytes 6148
  52.6 8.2 %collective-permute-start.1 = (bf16[8,512]{1,0:T(8,128)(2,1)S(1)}, bf16[8,512]{1,0:T(8,128)(2,1)S(1)}, u32[]{:S(2)}, u32[]{:S(2)}) collective-permute-start(bf16[8,512]{1,0:T(8,128)(2,1)S(1)} %get-tuple-element.21.mid_ref), channel_id=1, source_target_pairs={{0,64},{64,0},{128,192},{192,128},{256,320},{320,256},{384,448},{4... | collective-permute-start | bytes 24584 | tf_op jit(solution)/shard_map/ppermute | solution.py:364
  57.9 4.4 %collective-permute-start.2 = (bf16[8,512]{1,0:T(8,128)(2,1)S(1)}, bf16[8,512]{1,0:T(8,128)(2,1)S(1)}, u32[]{:S(2)}, u32[]{:S(2)}) collective-permute-start(bf16[8,512]{1,0:T(8,128)(2,1)S(1)} %get-tuple-element.21.mid_ref), channel_id=1, source_target_pairs={{64,128},{128,64},{192,256},{256,192},{320,384},{384,320},{448,512... | collective-permute-start | bytes 24584 | tf_op jit(solution)/shard_map/ppermute | solution.py:365
  64.2 8.7 %collective-permute-start.3 = (bf16[8,512]{1,0:T(8,128)(2,1)S(1)}, bf16[8,512]{1,0:T(8,128)(2,1)S(1)}, u32[]{:S(2)}, u32[]{:S(2)}) collective-permute-start(bf16[8,512]{1,0:T(8,128)(2,1)S(1)} %get-tuple-element.24), channel_id=1, source_target_pairs={{0,64},{64,0},{128,192},{192,128},{256,320},{320,256},{384,448},{4... | collective-permute-start | bytes 24584 | tf_op jit(solution)/shard_map/ppermute | solution.py:372
  66.1 7.8 %collective-permute-start.4 = (bf16[8,512]{1,0:T(8,128)(2,1)S(1)}, bf16[8,512]{1,0:T(8,128)(2,1)S(1)}, u32[]{:S(2)}, u32[]{:S(2)}) collective-permute-start(bf16[8,512]{1,0:T(8,128)(2,1)S(1)} %get-tuple-element.25), channel_id=1, source_target_pairs={{64,128},{128,64},{192,256},{256,192},{320,384},{384,320},{448,512... | collective-permute-start | bytes 24584 | tf_op jit(solution)/shard_map/ppermute | solution.py:373
  74.9 16.4 %all-to-all-start.2 = ((bf16[32,8,512]{2,1,0:T(8,128)(2,1)}), bf16[32,8,512]{2,1,0:T(8,128)(2,1)S(1)}, u32[]{:S(2)}, u32[]{:S(2)}) async-start(bf16[32,8,512]{2,1,0:T(8,128)(2,1)} %bitcast.13), calls=%async_computation.2 | async-start | bytes 524288 | tf_op jit(solution)/shard_map/all_to_all | solution.py:303
  93.6 8.9 %collective-permute-start.5 = (bf16[256,512]{1,0:T(8,128)(2,1)S(1)}, bf16[256,512]{1,0:T(8,128)(2,1)S(1)}, u32[]{:S(2)}, u32[]{:S(2)}) collective-permute-start(bf16[256,512]{1,0:T(8,128)(2,1)S(1)} %get-tuple-element.30), channel_id=1, source_target_pairs={{0,1},{1,0},{2,3},{3,2},{4,5},{5,4},{6,7},{7,6},{8,9},{9,8},{10,11... | collective-permute-start | bytes 786440 | tf_op jit(solution)/shard_map/ppermute | solution.py:309

commit v4 on v3

v4 whole, which is shorter than its diff:
```python
import jax
import jax.numpy as jnp
from jax import lax
from jax.experimental import pallas as pl
from jax.experimental.pallas import tpu as pltpu
from jax.sharding import PartitionSpec as P

BF16 = jnp.bfloat16
F32 = jnp.float32


def dot(left, right):
    return jnp.dot(left, right, preferred_element_type=F32)


def dot_t(left, right):
    return lax.dot_general(left, right, (((1,), (1,)), ((), ())), preferred_element_type=F32)


def split(values):
    high = values.astype(BF16)
    return high, (values - high.astype(F32)).astype(BF16)


def wide_dot(values, weight, product):
    rows = values.shape[0]
    high, low = split(values)
    both = product(jnp.concatenate([high.astype(F32), low.astype(F32)], axis=0).astype(BF16), weight)
    return both[:rows] + both[rows:]


def thirds(values):
    high, rest = values.astype(BF16), values
    rest = rest - high.astype(F32)
    mid = rest.astype(BF16).astype(F32)
    low = (rest - mid).astype(BF16).astype(F32)
    return jnp.concatenate([high.astype(F32), mid, low], axis=0).astype(BF16)


def layer_norm(values, gain):
    average = jnp.mean(values, axis=-1, keepdims=True)
    centred = values - average
    spread = jnp.mean(centred * centred, axis=-1, keepdims=True)
    inv_std = lax.rsqrt(spread + 1e-05)
    normed = centred * inv_std
    return normed * gain, normed, inv_std


def norm_back(normed, inv_std, gain, upstream):
    scaled = upstream * gain
    return inv_std * (
        scaled
        - jnp.mean(scaled, axis=-1, keepdims=True)
        - normed * jnp.mean(scaled * normed, axis=-1, keepdims=True)
    )


def call(body, out, *args, far=(), far_out=(), small=(), scratch=(), limit=16, cost=1):
    place = lambda there: pl.BlockSpec(memory_space=pltpu.HBM if there else pltpu.VMEM)
    single = not isinstance(out, tuple)
    outs = (out,) if single else out
    out_specs = tuple(place(i in far_out) for i in range(len(outs)))
    outs = tuple(
        pltpu.HBM(one.shape, one.dtype) if i in far_out else one for i, one in enumerate(outs)
    )
    args = tuple(
        pltpu.with_memory_space_constraint(arg, pltpu.HBM) if i in far else arg
        for i, arg in enumerate(args)
    )
    return pl.pallas_call(
        body,
        out_shape=outs[0] if single else outs,
        in_specs=[
            pl.BlockSpec(memory_space=pltpu.SMEM) if i in small else place(i in far)
            for i in range(len(args))
        ],
        out_specs=out_specs[0] if single else out_specs,
        scratch_shapes=scratch,
        compiler_params=pltpu.CompilerParams(vmem_limit_bytes=limit * 2**20 or None),
        cost_estimate=pl.CostEstimate(
            flops=cost * 4 * 10**9, bytes_accessed=cost * 2**22, transcendentals=0
        ),
    )(*args)


def dot_first(left, right):
    return lax.dot_general(left, right, (((0,), (0,)), ((), ())), preferred_element_type=F32)


def row_copies(source, target, sems, tile, offset=0):
    return [
        pltpu.make_async_copy(
            source.at[offset + i * tile : offset + (i + 1) * tile, :],
            target.at[i * tile : (i + 1) * tile, :],
            sems.at[i],
        )
        for i in range(sems.shape[0])
    ]


def silu_parts(values):
    sigma = 0.5 + 0.5 * jnp.tanh(0.5 * values)
    hidden = values * sigma
    return hidden.astype(BF16), sigma * (1.0 + (values - hidden))


def prep_kernel(
    mesh_ref, grid_ref, cotangent_ref, src_ref, peer_ref, slot_ref, sender_ref, receiver_ref,
    tiled_ref, pack_ref, near_ref, mesh_buf, cotangent_buf, index_buf, near_buf, sems,
):
    count, latent = mesh_buf.shape
    grids = grid_ref.shape[0]
    half = sender_ref.shape[1]
    pairs = (
        (mesh_ref, mesh_buf),
        (src_ref, index_buf.at[0]),
        (peer_ref, index_buf.at[1]),
        (slot_ref, index_buf.at[2]),
        (sender_ref, near_buf.at[:, :half]),
        (receiver_ref, near_buf.at[:, half:]),
        (cotangent_ref, cotangent_buf),
        (grid_ref, pack_ref.at[:grids, :]),
    )
    copies = [pltpu.make_async_copy(*pair, sems.at[i]) for i, pair in enumerate(pairs)]
    for copy in copies:
        copy.start()
    for copy in copies[:7]:
        copy.wait()
    times = tiled_ref.shape[0] // count
    rows = mesh_buf[...].astype(F32)
    tiled_ref[...] = jnp.concatenate([rows] * times, axis=0).astype(BF16)
    spare = pack_ref.shape[0] - grids
    place = lax.broadcasted_iota(jnp.int32, (spare, latent), 0)
    index = jnp.where(place == 0, index_buf[0], jnp.where(place == 1, index_buf[1], index_buf[2]))
    pack_ref[grids:, :] = index.astype(F32).astype(BF16)
    ends = jnp.broadcast_to(near_buf[...], (count, 2 * half)).astype(F32)
    near_ref[...] = jnp.concatenate([cotangent_buf[...].astype(F32), ends], axis=0).astype(BF16)
    copies[7].wait()


def src_kernel(own_ref, mate_ref, pick_ref, weight_ref, bias_ref, pre_ref, buf, sems):
    tile = own_ref.shape[0]
    copies = row_copies(buf, pre_ref, sems, tile)
    for i, copy in enumerate(copies):
        grid_ref = own_ref if i < len(copies) // 2 else mate_ref
        rows = dot(pick_ref[i * tile : (i + 1) * tile, :], grid_ref[:tile, :]).astype(BF16)
        buf[i * tile : (i + 1) * tile, :] = dot(rows, weight_ref[...]) + bias_ref[...]
        copy.start()
    for copy in copies:
        copy.wait()


def stack_split(values):
    high = values.astype(BF16).astype(F32)
    return jnp.concatenate([high, values - high], axis=0).astype(BF16)


def spread_rows(pick, table):
    half = table.shape[0] // 2
    return dot(pick, table[:half]) + dot(pick, table[half:])


def enc_kernel(
    pre_ref, dst_ref, mesh_ref, weight_ref, sum_ref, slope_ref,
    pre_buf, hidden_buf, slope_buf, in_sems, out_sems,
):
    latent = weight_ref.shape[1]
    plane_nodes = mesh_ref.shape[0]
    tile = pre_buf.shape[0] // in_sems.shape[0]
    arriving = row_copies(pre_ref, pre_buf, in_sems, tile)
    leaving = row_copies(slope_buf, slope_ref, out_sems, tile)
    for copy in arriving:
        copy.start()
    table = stack_split(dot(mesh_ref[...], weight_ref[...]))
    for i in range(len(arriving)):
        rows = slice(i * tile, (i + 1) * tile)
        spread = spread_rows(dst_ref[rows, :], table)
        arriving[i].wait()
        hidden, slope = silu_parts(pre_buf[rows, :] + spread)
        hidden_buf[rows, :] = hidden
        slope_buf[rows, :] = slope.astype(BF16)
        leaving[i].start()
    nodes = sum_ref.shape[1] // 2
    node_sums = lambda values: dot_first(dst_ref[...], values).reshape(-1, nodes, latent)
    sum_ref[...] = jnp.concatenate(
        [node_sums(hidden_buf[...]), node_sums(slope_buf[...])], axis=1
    ).astype(BF16)
    for copy in leaving:
        copy.wait()


def mid_kernel(
    parts_ref, weight_ref, gain_ref, mesh_ref, near_ref, mid_ref, packet_ref, agg_ref, slopes_ref
):
    count = mesh_ref.shape[0]
    summed = jnp.sum(parts_ref[...].astype(F32), axis=0)
    agg = wide_dot(summed[:count], weight_ref[...], dot)
    slopes_ref[...] = summed[count:]
    agg_ref[...] = agg
    mid = mesh_ref[...].astype(F32) + layer_norm(agg, gain_ref[...])[0]
    mid_ref[...] = mid.astype(BF16)
    packet_ref[...] = jnp.concatenate([mid, near_ref[...].astype(F32)], axis=0).astype(BF16)


def edge_ends(index, info_ref, offset, inside, group, count):
    half = index.shape[1] // 2
    source, receiver = index[:, :half], index[:, half:]
    bits = count.bit_length() - 1
    shift = offset + jnp.right_shift(source, bits) - 1
    one, two = info_ref[0], info_ref[1]
    spot = jnp.where(
        shift == 0, 4,
        jnp.where(
            shift == one, 0, jnp.where(shift == -one, 1, jnp.where(shift == two, 2, 3))
        ),
    )
    keep = lambda column: column * inside + (inside - 1)
    return (
        keep(spot * count + jnp.bitwise_and(source, count - 1)),
        keep((5 + group) * count + receiver),
    )


def proc_kernel(
    one_ref, two_ref, three_ref, four_ref, own_ref, info_ref, src_w_ref, dst_w_ref, out_w_ref,
    bias_ref, gain_ref, enc_agg_ref, enc_gain_ref, out_ref, grad_ref, tiled_ref,
):
    count = three_ref.shape[0]
    packets = [ref[...].astype(F32) for ref in (one_ref, two_ref, own_ref)]
    one, two, mid = (packet[:count] for packet in packets)
    upstreams = jnp.concatenate([packet[count : 2 * count] for packet in packets], axis=0)
    index = [packet[2 * count : 2 * count + 1].astype(jnp.int32) for packet in packets]
    step = info_ref[0]
    columns = [
        edge_ends(index[0], info_ref, step, info_ref[2], 0, count),
        edge_ends(index[1], info_ref, -step, info_ref[3], 1, count),
        edge_ends(index[2], info_ref, 0, 1, 2, count),
    ]
    sender, receiver = (jnp.concatenate(column, axis=1) for column in zip(*columns))
    ids = lax.broadcasted_iota(jnp.int32, (8 * count, sender.shape[1]), 0)
    chosen = jnp.where(jnp.logical_or(ids == sender, ids == receiver), 1.0, 0.0)
    pick_t = chosen.astype(BF16)
    pick = jnp.concatenate([chosen] * 3, axis=0).astype(BF16)

    rows = [one, two, three_ref[...].astype(F32), four_ref[...].astype(F32), mid]
    senders = jnp.concatenate(rows, axis=0).astype(BF16)
    receivers = jnp.concatenate([one, two, mid], axis=0).astype(BF16)
    table = jnp.concatenate(
        [dot(senders, src_w_ref[...]), dot(receivers, dst_w_ref[...]) + bias_ref[...]], axis=0
    )
    hidden, slope = silu_parts(dot_first(pick, thirds(table)))
    summed = dot(pick_t, hidden)[5 * count :]
    agg = wide_dot(summed, out_w_ref[...], dot)
    shifted, normed, inv_std = layer_norm(agg, gain_ref[...])
    out_ref[...] = (mid + shifted[2 * count :]).astype(BF16)
    grad_agg = norm_back(normed, inv_std, gain_ref[...], upstreams).astype(BF16)
    back = dot_t(grad_agg, out_w_ref[...])
    blank = jnp.zeros((5 * count, back.shape[1]), F32)
    spread = dot_first(pick, thirds(jnp.concatenate([blank, back], axis=0)))
    sums = dot(pick_t, (spread * slope).astype(BF16))
    sender_sum = wide_dot(sums[4 * count : 5 * count], src_w_ref[...], dot_t)
    receiver_sum = wide_dot(sums[7 * count :], dst_w_ref[...], dot_t)
    grad = upstreams[2 * count :] + receiver_sum + sender_sum
    grad_ref[...] = grad
    _, normed, inv_std = layer_norm(enc_agg_ref[...], enc_gain_ref[...])
    rows = norm_back(normed, inv_std, enc_gain_ref[...], grad)
    times = tiled_ref.shape[0] // count
    tiled_ref[...] = jnp.concatenate([rows] * times, axis=0).astype(BF16)


def mesh_kernel(tiled_ref, slopes_ref, grad_ref, out_w_ref, dst_w_ref, out_ref):
    count = grad_ref.shape[0]
    rows = dot_t(tiled_ref[: 2 * count, :], out_w_ref[...])[:count]
    out_ref[...] = (
        grad_ref[...] + wide_dot(rows * slopes_ref[...], dst_w_ref[...], dot_t)
    ).astype(BF16)


def mate_kernel(
    grad_ref, dst_ref, pick_t_ref, slope_ref, out_w_ref, src_w_ref, table_ref, part_ref, buf, sems
):
    half = dst_ref.shape[0] // 2
    (arriving,) = row_copies(slope_ref, buf, sems, half, half)
    arriving.start()
    table = stack_split(dot_t(grad_ref[...], out_w_ref[...]))
    table_ref[...] = table
    spread = spread_rows(dst_ref[half:, :], table)
    arriving.wait()
    edge = (spread * buf[...].astype(F32)).astype(BF16)
    part_ref[...] = wide_dot(dot(pick_t_ref[:, half:], edge), src_w_ref[...], dot_t).astype(BF16)


def own_kernel(table_ref, dst_ref, pick_t_ref, slope_ref, src_w_ref, part_ref, buf, sems):
    half = dst_ref.shape[0] // 2
    (arriving,) = row_copies(slope_ref, buf, sems, half)
    arriving.start()
    spread = spread_rows(dst_ref[:half, :], table_ref[...])
    arriving.wait()
    edge = (spread * buf[...].astype(F32)).astype(BF16)
    part_ref[...] = wide_dot(dot(pick_t_ref[:, :half], edge), src_w_ref[...], dot_t)


def join_kernel(own_ref, mate_ref, out_ref):
    out_ref[...] = (own_ref[...] + mate_ref[...].astype(F32)).astype(BF16)


def per_device(
    grid_latent,
    mesh_latent,
    g2m_src,
    g2m_peer,
    g2m_slot,
    proc_src,
    proc_dst,
    enc_src_w,
    enc_dst_w,
    enc_out_w,
    enc_bias,
    enc_gain,
    proc_src_w,
    proc_dst_w,
    proc_out_w,
    proc_bias,
    proc_gain,
    cotangent,
):
    feats = lax.axis_size("feat")
    bands = lax.axis_size("band")
    chips = feats // 2
    core = lax.axis_index("feat") % 2
    band = lax.axis_index("band")
    edges = g2m_src.shape[0]
    grids, latent = grid_latent.shape
    nodes = mesh_latent.shape[0]
    plane_nodes = chips * nodes
    plane = [[2 * chip + side for chip in range(chips)] for side in range(2)]
    shape = jax.ShapeDtypeStruct
    row = lambda vector: vector.reshape(1, latent)
    sem = lambda count: pltpu.SemaphoreType.DMA((count,))
    edge_buf = lambda count, kind: pltpu.VMEM((count, latent), kind)

    def exchange(values):
        return lax.all_to_all(
            values.reshape(chips, -1, latent), "feat", split_axis=0, concat_axis=0, tiled=True,
            axis_index_groups=plane,
        )

    def swap(values):
        return lax.ppermute(values, "feat", [(i, i ^ 1) for i in range(feats)])

    far_side = lambda step: [
        pair
        for i in range(bands - step)
        if i & step
        for pair in ((i, i + step), (i + step, i))
    ]
    near_side = lambda step: [(i, i ^ step) for i in range(bands)]
    line = lambda index: index.reshape(1, edges)

    tiled_mesh, pack, near = call(
        prep_kernel,
        (
            shape((plane_nodes, latent), BF16),
            shape((grids + 16, latent), BF16),
            shape((2 * nodes, latent), BF16),
        ),
        mesh_latent, grid_latent, cotangent, line(g2m_src), line(g2m_peer), line(g2m_slot),
        proc_src.reshape(1, -1), proc_dst.reshape(1, -1),
        far=range(8),
        scratch=(
            pltpu.VMEM((nodes, latent), BF16),
            pltpu.VMEM((nodes, latent), BF16),
            pltpu.VMEM((3, 1, edges), jnp.int32),
            pltpu.VMEM((1, latent), jnp.int32),
            pltpu.SemaphoreType.DMA((8,)),
        ),
    )
    mate_pack = swap(pack)
    mesh_all = exchange(tiled_mesh).reshape(plane_nodes, latent)

    mate_index = mate_pack[grids : grids + 3].astype(jnp.int32)
    joined = lambda own, place: jnp.concatenate([own, mate_index[place]])
    source, peer, slot = joined(g2m_src, 0), joined(g2m_peer[:, 0], 1), joined(g2m_slot, 2)
    target = jnp.where(peer % 2 == core, peer // 2 * nodes + slot, -1)
    grid_ids = jnp.arange(grids, dtype=jnp.int32)
    node_ids = jnp.arange(plane_nodes, dtype=jnp.int32)
    src_pick = (source[:, None] == grid_ids[None, :]).astype(BF16)
    src_pick_t = (source[None, :] == grid_ids[:, None]).astype(BF16)
    dst_pick = (target[:, None] == node_ids[None, :]).astype(BF16)

    step_one = jnp.where(band & 1 == 0, 1, -1)
    step_two = jnp.where(band & 2 == 0, 2, -2)
    inside = lambda place: jnp.logical_and(place >= 0, place < bands)
    info = jnp.stack([step_one, step_two, inside(band + step_one), inside(band - step_one)])

    pre_src = call(
        src_kernel, shape((2 * edges, latent), F32),
        grid_latent, mate_pack, src_pick, enc_src_w, row(enc_bias),
        far_out=(0,), scratch=(edge_buf(2 * edges, F32), sem(4)),
    )
    partial, slope = call(
        enc_kernel,
        (shape((chips, 2 * nodes, latent), BF16), shape((2 * edges, latent), BF16)),
        pre_src, dst_pick, mesh_all, enc_dst_w,
        far=(0,), far_out=(1,),
        scratch=(
            edge_buf(2 * edges, F32), edge_buf(2 * edges, BF16), edge_buf(2 * edges, BF16),
            sem(4), sem(4),
        ),
    )
    mid, packet, enc_agg, slopes = call(
        mid_kernel,
        (
            shape((nodes, latent), BF16),
            shape((3 * nodes, latent), BF16),
            shape((nodes, latent), F32),
            shape((nodes, latent), F32),
        ),
        exchange(partial), enc_out_w, row(enc_gain), mesh_latent, near,
    )
    mesh_out, grad_mid, tiled = call(
        proc_kernel,
        (
            shape((nodes, latent), BF16),
            shape((nodes, latent), F32),
            shape((plane_nodes, latent), BF16),
        ),
        lax.ppermute(packet, "band", near_side(1)),
        lax.ppermute(packet, "band", far_side(1)),
        lax.ppermute(mid, "band", near_side(2)),
        lax.ppermute(mid, "band", far_side(2)),
        packet, info.astype(jnp.int32), proc_src_w, proc_dst_w, proc_out_w, row(proc_bias),
        row(proc_gain), enc_agg, row(enc_gain),
        small=(5,),
    )
    grad_all = exchange(tiled).reshape(plane_nodes, latent)
    grad_mesh = call(
        mesh_kernel, shape((nodes, latent), BF16), tiled, slopes, grad_mid, enc_out_w, enc_dst_w,
    )
    table, mate_grad = call(
        mate_kernel, (shape((2 * plane_nodes, latent), BF16), shape((grids, latent), BF16)),
        grad_all, dst_pick, src_pick_t, slope, enc_out_w, enc_src_w,
        far=(3,), scratch=(edge_buf(edges, BF16), sem(1)),
    )
    own_grad = call(
        own_kernel, shape((grids, latent), F32), table, dst_pick, src_pick_t, slope, enc_src_w,
        far=(3,), scratch=(edge_buf(edges, BF16), sem(1)),
    )
    grad_grid = call(join_kernel, shape((grids, latent), BF16), own_grad, swap(mate_grad))
    return (mesh_out, grad_grid, grad_mesh)


def solution(mesh):
    shard = ("band", "feat")
    placed = (P(shard, None), P(shard, None), P(shard), P(shard, None), P(shard), P(shard), P(shard))
    placed += (P(),) * 10 + (P(shard, None),)
    return jax.shard_map(
        per_device,
        mesh=mesh,
        in_specs=placed,
        out_specs=(P(shard, None), P(shard, None), P(shard, None)),
        check_vma=False,
    )
```

time: 104 us -> 104 us (level)
  the two profiles are of different devices: /device:TPU:73 before, /device:TPU:201 now
where the time goes in v4:
time: 104 us; the launch traced here: 103 us
  starting transfers between devices  48.2 us (46%)
  waiting for transfers between devices  34 us (33%)
  Pallas kernels  19.1 us (18%)
  between operations  1.05 us (1%)
    all_to_all x3, waiting for transfers between devices, exchange(): lax.all_to_all(values.reshape(chips, -1, latent), 'feat', split_axis=0, c...  33 us
    all_to_all x3, starting transfers between devices, exchange(): lax.all_to_all(values.reshape(chips, -1, latent), 'feat', split_axis=0, c...  20.3 us
    pallas_call x9, Pallas kernels, call(): pl.pallas_call(body, out_shape=outs[0] if single else outs, in_specs=[pl....  19.1 us
    ppermute x2, starting transfers between devices, swap(): return lax.ppermute(values, 'feat', [(i, i ^ 1) for i in range(feats)])  9.02 us
    ppermute x1, starting transfers between devices, per_device(): lax.ppermute(mid, 'band', far_side(2))  7.6 us
    ppermute x1, starting transfers between devices, per_device(): lax.ppermute(packet, 'band', far_side(1))  7.3 us
  transfers between devices with their start and end apart: 9, of which 4 were waited for; matrix products, arithmetic and copies ran while one was open for 1% of the time, Pallas kernels for 6%

profile of v4, /device:TPU:201, one launch (start us, length us, event | category | flops | bytes accessed | tf_op | source)
XLA Modules:
  0.0 103.1 jit_solution(15820927619631514889)
XLA Ops:
  0.6 0.0 copy-start.12
  0.6 0.0 copy-start.13
  0.7 0.0 copy-start.14
  0.7 0.0 copy-start.5
  0.7 0.0 copy-start.6
  0.7 0.0 copy-start.8
  0.7 1.9 %shard_map.193 = (bf16[256,512]{1,0:T(8,128)(2,1)}, bf16[272,512]{1,0:T(8,128)(2,1)S(1)}, bf16[16,512]{1,0:T(8,128)(2,1)S(1)}) custom-call(bf16[8,512]{1,0:T(8,128)(2,1)} %mesh_ref.3, bf16[256,512]{1,0:T(8,128)(2,1)} %own_ref.1, bf16[8,512]{1,0:T(8,128)(2,1)} %cotangent_ref.1, s32[1,512]{1,0:T(1,128)} %bitcast.34, s32[1,512]{1,0:T(1,128)} %bitcast.31, ...), custom_call_target="tpu_custom_call" | custom-call | flops 4000000000 | bytes 4194304 | tf_op jit(solution)/shard_map/pallas_call | solution.py:70
  2.6 2.6 %collective-permute-start = (bf16[272,512]{1,0:T(8,128)(2,1)S(1)}, bf16[272,512]{1,0:T(8,128)(2,1)S(1)}, u32[]{:S(2)}, u32[]{:S(2)}) collective-permute-start(bf16[272,512]{1,0:T(8,128)(2,1)S(1)} %get-tuple-element.17), channel_id=1, source_target_pairs={{0,1},{1,0},{2,3},{3,2},{4,5},{5,4},{6,7},{7,6},{8,9},{9,8},{10,11... | collective-permute-start | bytes 835592 | tf_op jit(solution)/shard_map/ppermute | solution.py:349
  5.2 9.6 %all-to-all-start = ((bf16[32,8,512]{2,1,0:T(8,128)(2,1)}), bf16[32,8,512]{2,1,0:T(8,128)(2,1)S(1)}, u32[]{:S(2)}, u32[]{:S(2)}) async-start(bf16[32,8,512]{2,1,0:T(8,128)(2,1)} %bitcast.10), calls=%async_computation | async-start | bytes 524288 | tf_op jit(solution)/shard_map/all_to_all | solution.py:343
  14.8 0.0 collective-permute-done.mate_ref
  14.8 0.0 copy-done.12
  14.9 0.0 copy-done.13
  14.9 0.2 fusion.1.dst_ref
  15.1 0.0 copy-done.14
  15.1 0.2 fusion.pick_ref
  15.3 0.0 copy-done.5
  15.4 0.0 copy-start.3
  15.4 2.1 %shard_map.194.pre_ref = f32[1024,512]{1,0:T(8,128)} custom-call(bf16[256,512]{1,0:T(8,128)(2,1)S(1)} %copy-done.6, bf16[272,512]{1,0:T(8,128)(2,1)S(1)} %collective-permute-done.mate_ref, bf16[1024,256]{1,0:T(8,128)(2,1)S(1)} %fusion.pick_ref, bf16[512,512]{1,0:T(8,128)(2,1)S(1)} %copy-done.5, f32[1,512]{1,0:T(1,128)S(1)} %bitcast.23), custom_call_target="tpu_custom_call" | custom-call | flops 4000000000 | bytes 4194304 | tf_op jit(solution)/shard_map/pallas_call | solution.py:70
  17.5 9.4 %all-to-all-done = bf16[32,8,512]{2,1,0:T(8,128)(2,1)S(1)} async-done(((bf16[32,8,512]{2,1,0:T(8,128)(2,1)}), bf16[32,8,512]{2,1,0:T(8,128)(2,1)S(1)}, u32[]{:S(2)}, u32[]{:S(2)}) %all-to-all-start) | async-done | bytes 262176 | tf_op jit(solution)/shard_map/all_to_all | solution.py:343
  27.0 4.6 %shard_map.195 = (bf16[32,16,512]{2,1,0:T(8,128)(2,1)}, bf16[1024,512]{1,0:T(8,128)(2,1)}) custom-call(f32[1024,512]{1,0:T(8,128)} %shard_map.194.pre_ref, bf16[1024,256]{1,0:T(8,128)(2,1)S(1)} %fusion.1.dst_ref, bf16[256,512]{1,0:T(8,128)(2,1)S(1)} %bitcast.21, bf16[512,512]{1,0:T(8,128)(2,1)S(1)} %copy-done.3), custom_call_target="tpu_custom_call" | custom-call | flops 4000000000 | bytes 4194304 | tf_op jit(solution)/shard_map/pallas_call | solution.py:70
  31.6 4.5 %all-to-all-start.1 = ((bf16[32,16,512]{2,1,0:T(8,128)(2,1)}), bf16[32,16,512]{2,1,0:T(8,128)(2,1)S(1)}, u32[]{:S(2)}, u32[]{:S(2)}) async-start(bf16[32,16,512]{2,1,0:T(8,128)(2,1)} %get-tuple-element.19), calls=%async_computation.1 | async-start | bytes 1048576 | tf_op jit(solution)/shard_map/all_to_all | solution.py:343
  36.1 15.6 %all-to-all-done.1.parts_ref = bf16[32,16,512]{2,1,0:T(8,128)(2,1)S(1)} async-done(((bf16[32,16,512]{2,1,0:T(8,128)(2,1)}), bf16[32,16,512]{2,1,0:T(8,128)(2,1)S(1)}, u32[]{:S(2)}, u32[]{:S(2)}) %all-to-all-start.1) | async-done | bytes 524320 | tf_op jit(solution)/shard_map/all_to_all | solution.py:343
  51.7 0.0 copy-done.4
  51.7 0.0 copy-start
  51.8 0.0 copy-start.1
  51.8 0.0 copy-start.2
  51.8 0.0 copy-start.10
  51.8 0.0 copy-start.11
  51.8 0.4 shard_map.196
  52.2 2.0 %collective-permute-start.1 = (bf16[24,512]{1,0:T(8,128)(2,1)S(1)}, bf16[24,512]{1,0:T(8,128)(2,1)S(1)}, u32[]{:S(2)}, u32[]{:S(2)}) collective-permute-start(bf16[24,512]{1,0:T(8,128)(2,1)S(1)} %get-tuple-element.21.own_ref), channel_id=1, source_target_pairs={{0,64},{64,0},{128,192},{192,128},{256,320},{320,256},{384,448},{4... | collective-permute-start | bytes 73736 | tf_op jit(solution)/shard_map/ppermute | solution.py:428
  54.3 7.3 %collective-permute-start.2 = (bf16[24,512]{1,0:T(8,128)(2,1)S(1)}, bf16[24,512]{1,0:T(8,128)(2,1)S(1)}, u32[]{:S(2)}, u32[]{:S(2)}) collective-permute-start(bf16[24,512]{1,0:T(8,128)(2,1)S(1)} %get-tuple-element.21.own_ref), channel_id=1, source_target_pairs={{64,128},{128,64},{192,256},{256,192},{320,384},{384,320},{448,512... | collective-permute-start | bytes 73736 | tf_op jit(solution)/shard_map/ppermute | solution.py:429
  61.6 1.9 %collective-permute-start.3 = (bf16[8,512]{1,0:T(8,128)(2,1)S(1)}, bf16[8,512]{1,0:T(8,128)(2,1)S(1)}, u32[]{:S(2)}, u32[]{:S(2)}) collective-permute-start(bf16[8,512]{1,0:T(8,128)(2,1)S(1)} %get-tuple-element.22), channel_id=1, source_target_pairs={{0,128},{64,192},{128,0},{192,64},{256,384},{320,448},{384,256},{4... | collective-permute-start | bytes 24584 | tf_op jit(solution)/shard_map/ppermute | solution.py:430
  63.5 7.6 %collective-permute-start.4 = (bf16[8,512]{1,0:T(8,128)(2,1)S(1)}, bf16[8,512]{1,0:T(8,128)(2,1)S(1)}, u32[]{:S(2)}, u32[]{:S(2)}) collective-permute-start(bf16[8,512]{1,0:T(8,128)(2,1)S(1)} %get-tuple-element.22), channel_id=1, source_target_pairs={{128,256},{256,128},{192,320},{320,192},{384,512},{512,384},{448,5... | collective-permute-start | bytes 24584 | tf_op jit(solution)/shard_map/ppermute | solution.py:431
  71.1 0.1 pad_add_fusion.2.info_ref
  71.2 0.0 collective-permute-done.3.three_ref
  71.2 0.9 collective-permute-done.4.four_ref
  72.1 0.0 collective-permute-done.1.one_ref
  72.1 0.0 collective-permute-done.2.two_ref
  72.2 3.8 %shard_map.197 = (bf16[8,512]{1,0:T(8,128)(2,1)}, f32[8,512]{1,0:T(8,128)S(1)}, bf16[256,512]{1,0:T(8,128)(2,1)}) custom-call(bf16[24,512]{1,0:T(8,128)(2,1)S(1)} %collective-permute-done.1.one_ref, bf16[24,512]{1,0:T(8,128)(2,1)S(1)} %collective-permute-done.2.two_ref, bf16[8,512]{1,0:T(8,128)(2,1)S(1)} %collective-permute-done.3.three_ref, ...), custom_call_target="tpu_custom_call" | custom-call | flops 4000000000 | bytes 4194304 | tf_op jit(solution)/shard_map/pallas_call | solution.py:70
  76.0 6.2 %all-to-all-start.2 = ((bf16[32,8,512]{2,1,0:T(8,128)(2,1)}), bf16[32,8,512]{2,1,0:T(8,128)(2,1)S(1)}, u32[]{:S(2)}, u32[]{:S(2)}) async-start(bf16[32,8,512]{2,1,0:T(8,128)(2,1)} %bitcast.19), calls=%async_computation.2 | async-start | bytes 524288 | tf_op jit(solution)/shard_map/all_to_all | solution.py:343
  82.2 0.1 fusion.2.pick_t_ref
  82.3 2.0 %shard_map.201 = bf16[8,512]{1,0:T(8,128)(2,1)} custom-call(bf16[256,512]{1,0:T(8,128)(2,1)} %get-tuple-element.25.tiled_ref, f32[8,512]{1,0:T(8,128)S(1)} %get-tuple-element.29.slopes_ref, f32[8,512]{1,0:T(8,128)S(1)} %get-tuple-element.30.grad_ref, bf16[512,512]{1,0:T(8,128)(2,1)S(1)} %copy-done.4, bf16[512,512]{1,0:T(8,128)(2,1)S(1)} %copy-done.3), custom_call_target="tpu_custom_call" | custom-call | flops 4000000000 | bytes 4194304 | tf_op jit(solution)/shard_map/pallas_call | solution.py:70
  84.3 8.0 %all-to-all-done.2 = bf16[32,8,512]{2,1,0:T(8,128)(2,1)S(1)} async-done(((bf16[32,8,512]{2,1,0:T(8,128)(2,1)}), bf16[32,8,512]{2,1,0:T(8,128)(2,1)S(1)}, u32[]{:S(2)}, u32[]{:S(2)}) %all-to-all-start.2) | async-done | bytes 262176 | tf_op jit(solution)/shard_map/all_to_all | solution.py:343
  92.3 1.7 %shard_map.198 = (bf16[512,512]{1,0:T(8,128)(2,1)S(1)}, bf16[256,512]{1,0:T(8,128)(2,1)S(1)}) custom-call(bf16[256,512]{1,0:T(8,128)(2,1)S(1)} %bitcast.22, bf16[1024,256]{1,0:T(8,128)(2,1)S(1)} %fusion.1.dst_ref, bf16[256,1024]{1,0:T(8,128)(2,1)S(1)} %fusion.2.pick_t_ref, bf16[1024,512]{1,0:T(8,128)(2,1)} %get-tuple-element.26.slope_ref, ...), custom_call_target="tpu_custom_call" | custom-call | flops 4000000000 | bytes 4194304 | tf_op jit(solution)/shard_map/pallas_call | solution.py:70
  94.0 6.4 %collective-permute-start.5 = (bf16[256,512]{1,0:T(8,128)(2,1)S(1)}, bf16[256,512]{1,0:T(8,128)(2,1)S(1)}, u32[]{:S(2)}, u32[]{:S(2)}) collective-permute-start(bf16[256,512]{1,0:T(8,128)(2,1)S(1)} %get-tuple-element.28), channel_id=1, source_target_pairs={{0,1},{1,0},{2,3},{3,2},{4,5},{5,4},{6,7},{7,6},{8,9},{9,8},{10,11... | collective-permute-start | bytes 786440 | tf_op jit(solution)/shard_map/ppermute | solution.py:349
  100.5 1.8 %shard_map.199.own_ref = f32[256,512]{1,0:T(8,128)S(1)} custom-call(bf16[512,512]{1,0:T(8,128)(2,1)S(1)} %get-tuple-element.27.table_ref, bf16[1024,256]{1,0:T(8,128)(2,1)S(1)} %fusion.1.dst_ref, bf16[256,1024]{1,0:T(8,128)(2,1)S(1)} %fusion.2.pick_t_ref, bf16[1024,512]{1,0:T(8,128)(2,1)} %get-tuple-element.26.slope_ref, bf16[512,512]{1,0:T(8,128)(2,1)S(1)} %copy-done.5), custom_call_target="tpu_custom_call" | custom-call | flops 4000000000 | bytes 4194304 | tf_op jit(solution)/shard_map/pallas_call | solution.py:70
  102.3 0.0 collective-permute-done.5.mate_ref
  102.3 0.7 shard_map.200
  (17 shorter events, 0.1 us)
Async XLA Ops:
  0.6 14.2 %copy-start.12 = (s32[512,1]{0,1:T(1,128)S(1)}, s32[512,1]{0,1:T(1,128)}, u32[]{:S(2)}) copy-start(s32[512,1]{0,1:T(1,128)} %param.21) | copy-start | bytes 6148
  0.6 14.2 %copy-start.13 = (s32[512]{0:T(512)S(1)}, s32[512]{0:T(512)}, u32[]{:S(2)}) copy-start(s32[512]{0:T(512)} %param.22) | copy-start | bytes 6148
  0.7 14.4 %copy-start.14 = (s32[512]{0:T(512)S(1)}, s32[512]{0:T(512)}, u32[]{:S(2)}) copy-start(s32[512]{0:T(512)} %param.20) | copy-start | bytes 6148
  0.7 14.7 %copy-start.5 = (bf16[512,512]{1,0:T(8,128)(2,1)S(1)}, bf16[512,512]{1,0:T(8,128)(2,1)}, u32[]{:S(2)}) copy-start(bf16[512,512]{1,0:T(8,128)(2,1)} %src_w_ref.5) | copy-start | bytes 1572868
  0.7 14.7 %copy-start.6 = (bf16[256,512]{1,0:T(8,128)(2,1)S(1)}, bf16[256,512]{1,0:T(8,128)(2,1)}, u32[]{:S(2)}) copy-start(bf16[256,512]{1,0:T(8,128)(2,1)} %own_ref.1) | copy-start | bytes 786436
  0.7 14.7 %copy-start.8 = (f32[512]{0:T(512)S(1)}, f32[512]{0:T(512)}, u32[]{:S(2)}) copy-start(f32[512]{0:T(512)} %param.28) | copy-start | bytes 6148
  2.6 12.2 %collective-permute-start = (bf16[272,512]{1,0:T(8,128)(2,1)S(1)}, bf16[272,512]{1,0:T(8,128)(2,1)S(1)}, u32[]{:S(2)}, u32[]{:S(2)}) collective-permute-start(bf16[272,512]{1,0:T(8,128)(2,1)S(1)} %get-tuple-element.17), channel_id=1, source_target_pairs={{0,1},{1,0},{2,3},{3,2},{4,5},{5,4},{6,7},{7,6},{8,9},{9,8},{10,11... | collective-permute-start | bytes 835592 | tf_op jit(solution)/shard_map/ppermute | solution.py:349
  5.2 21.8 %all-to-all-start = ((bf16[32,8,512]{2,1,0:T(8,128)(2,1)}), bf16[32,8,512]{2,1,0:T(8,128)(2,1)S(1)}, u32[]{:S(2)}, u32[]{:S(2)}) async-start(bf16[32,8,512]{2,1,0:T(8,128)(2,1)} %bitcast.10), calls=%async_computation | async-start | bytes 524288 | tf_op jit(solution)/shard_map/all_to_all | solution.py:343
  15.4 11.6 %copy-start.3 = (bf16[512,512]{1,0:T(8,128)(2,1)S(1)}, bf16[512,512]{1,0:T(8,128)(2,1)}, u32[]{:S(2)}) copy-start(bf16[512,512]{1,0:T(8,128)(2,1)} %dst_w_ref.3) | copy-start | bytes 1572868
  26.9 24.8 %copy-start.4 = (bf16[512,512]{1,0:T(8,128)(2,1)S(1)}, bf16[512,512]{1,0:T(8,128)(2,1)}, u32[]{:S(2)}) copy-start(bf16[512,512]{1,0:T(8,128)(2,1)} %out_w_ref.5) | copy-start | bytes 1572868
  26.9 24.8 %copy-start.7 = (bf16[8,512]{1,0:T(8,128)(2,1)S(1)}, bf16[8,512]{1,0:T(8,128)(2,1)}, u32[]{:S(2)}) copy-start(bf16[8,512]{1,0:T(8,128)(2,1)} %mesh_ref.3) | copy-start | bytes 24580
  26.9 24.8 %copy-start.9 = (f32[512]{0:T(512)S(1)}, f32[512]{0:T(512)}, u32[]{:S(2)}) copy-start(f32[512]{0:T(512)} %param.29) | copy-start | bytes 6148
  31.6 20.1 %all-to-all-start.1 = ((bf16[32,16,512]{2,1,0:T(8,128)(2,1)}), bf16[32,16,512]{2,1,0:T(8,128)(2,1)S(1)}, u32[]{:S(2)}, u32[]{:S(2)}) async-start(bf16[32,16,512]{2,1,0:T(8,128)(2,1)} %get-tuple-element.19), calls=%async_computation.1 | async-start | bytes 1048576 | tf_op jit(solution)/shard_map/all_to_all | solution.py:343
  51.7 20.4 %copy-start = (bf16[512,512]{1,0:T(8,128)(2,1)S(1)}, bf16[512,512]{1,0:T(8,128)(2,1)}, u32[]{:S(2)}) copy-start(bf16[512,512]{1,0:T(8,128)(2,1)} %src_w_ref.3) | copy-start | bytes 1572868
  51.8 20.4 %copy-start.1 = (bf16[512,512]{1,0:T(8,128)(2,1)S(1)}, bf16[512,512]{1,0:T(8,128)(2,1)}, u32[]{:S(2)}) copy-start(bf16[512,512]{1,0:T(8,128)(2,1)} %dst_w_ref.2) | copy-start | bytes 1572868
  51.8 20.4 %copy-start.2 = (bf16[512,512]{1,0:T(8,128)(2,1)S(1)}, bf16[512,512]{1,0:T(8,128)(2,1)}, u32[]{:S(2)}) copy-start(bf16[512,512]{1,0:T(8,128)(2,1)} %out_w_ref.3) | copy-start | bytes 1572868
  51.8 20.4 %copy-start.10 = (f32[512]{0:T(512)S(1)}, f32[512]{0:T(512)}, u32[]{:S(2)}) copy-start(f32[512]{0:T(512)} %param.33) | copy-start | bytes 6148
  51.8 20.4 %copy-start.11 = (f32[512]{0:T(512)S(1)}, f32[512]{0:T(512)}, u32[]{:S(2)}) copy-start(f32[512]{0:T(512)} %param.34) | copy-start | bytes 6148
  52.2 19.9 %collective-permute-start.1 = (bf16[24,512]{1,0:T(8,128)(2,1)S(1)}, bf16[24,512]{1,0:T(8,128)(2,1)S(1)}, u32[]{:S(2)}, u32[]{:S(2)}) collective-permute-start(bf16[24,512]{1,0:T(8,128)(2,1)S(1)} %get-tuple-element.21.own_ref), channel_id=1, source_target_pairs={{0,64},{64,0},{128,192},{192,128},{256,320},{320,256},{384,448},{4... | collective-permute-start | bytes 73736 | tf_op jit(solution)/shard_map/ppermute | solution.py:428
  54.3 17.9 %collective-permute-start.2 = (bf16[24,512]{1,0:T(8,128)(2,1)S(1)}, bf16[24,512]{1,0:T(8,128)(2,1)S(1)}, u32[]{:S(2)}, u32[]{:S(2)}) collective-permute-start(bf16[24,512]{1,0:T(8,128)(2,1)S(1)} %get-tuple-element.21.own_ref), channel_id=1, source_target_pairs={{64,128},{128,64},{192,256},{256,192},{320,384},{384,320},{448,512... | collective-permute-start | bytes 73736 | tf_op jit(solution)/shard_map/ppermute | solution.py:429
  61.6 9.6 %collective-permute-start.3 = (bf16[8,512]{1,0:T(8,128)(2,1)S(1)}, bf16[8,512]{1,0:T(8,128)(2,1)S(1)}, u32[]{:S(2)}, u32[]{:S(2)}) collective-permute-start(bf16[8,512]{1,0:T(8,128)(2,1)S(1)} %get-tuple-element.22), channel_id=1, source_target_pairs={{0,128},{64,192},{128,0},{192,64},{256,384},{320,448},{384,256},{4... | collective-permute-start | bytes 24584 | tf_op jit(solution)/shard_map/ppermute | solution.py:430
  63.5 8.6 %collective-permute-start.4 = (bf16[8,512]{1,0:T(8,128)(2,1)S(1)}, bf16[8,512]{1,0:T(8,128)(2,1)S(1)}, u32[]{:S(2)}, u32[]{:S(2)}) collective-permute-start(bf16[8,512]{1,0:T(8,128)(2,1)S(1)} %get-tuple-element.22), channel_id=1, source_target_pairs={{128,256},{256,128},{192,320},{320,192},{384,512},{512,384},{448,5... | collective-permute-start | bytes 24584 | tf_op jit(solution)/shard_map/ppermute | solution.py:431
  76.0 16.3 %all-to-all-start.2 = ((bf16[32,8,512]{2,1,0:T(8,128)(2,1)}), bf16[32,8,512]{2,1,0:T(8,128)(2,1)S(1)}, u32[]{:S(2)}, u32[]{:S(2)}) async-start(bf16[32,8,512]{2,1,0:T(8,128)(2,1)} %bitcast.19), calls=%async_computation.2 | async-start | bytes 524288 | tf_op jit(solution)/shard_map/all_to_all | solution.py:343
  94.0 8.3 %collective-permute-start.5 = (bf16[256,512]{1,0:T(8,128)(2,1)S(1)}, bf16[256,512]{1,0:T(8,128)(2,1)S(1)}, u32[]{:S(2)}, u32[]{:S(2)}) collective-permute-start(bf16[256,512]{1,0:T(8,128)(2,1)S(1)} %get-tuple-element.28), channel_id=1, source_target_pairs={{0,1},{1,0},{2,3},{3,2},{4,5},{5,4},{6,7},{7,6},{8,9},{9,8},{10,11... | collective-permute-start | bytes 786440 | tf_op jit(solution)/shard_map/ppermute | solution.py:349

commit v5 on v4

--- a/solution.py
+++ b/solution.py
@@ -104,15 +104,25 @@
     return hidden.astype(BF16), sigma * (1.0 + (values - hidden))
 
 
+def tile_kernel(mesh_ref, tiled_ref, sems):
+    copies = [
+        pltpu.make_async_copy(mesh_ref, tiled_ref.at[i], sems.at[i])
+        for i in range(tiled_ref.shape[0])
+    ]
+    for copy in copies:
+        copy.start()
+    for copy in copies:
+        copy.wait()
+
+
 def prep_kernel(
-    mesh_ref, grid_ref, cotangent_ref, src_ref, peer_ref, slot_ref, sender_ref, receiver_ref,
-    tiled_ref, pack_ref, near_ref, mesh_buf, cotangent_buf, index_buf, near_buf, sems,
-):
-    count, latent = mesh_buf.shape
+    grid_ref, cotangent_ref, src_ref, peer_ref, slot_ref, sender_ref, receiver_ref,
+    pack_ref, near_ref, cotangent_buf, index_buf, near_buf, pack_buf, sems,
+):
+    count, latent = cotangent_buf.shape
     grids = grid_ref.shape[0]
     half = sender_ref.shape[1]
     pairs = (
-        (mesh_ref, mesh_buf),
         (src_ref, index_buf.at[0]),
         (peer_ref, index_buf.at[1]),
         (slot_ref, index_buf.at[2]),
@@ -120,21 +130,20 @@
         (receiver_ref, near_buf.at[:, half:]),
         (cotangent_ref, cotangent_buf),
         (grid_ref, pack_ref.at[:grids, :]),
+        (pack_buf, pack_ref.at[grids:, :]),
     )
     copies = [pltpu.make_async_copy(*pair, sems.at[i]) for i, pair in enumerate(pairs)]
-    for copy in copies:
+    for copy in copies[:7]:
         copy.start()
-    for copy in copies[:7]:
+    for copy in copies[:6]:
         copy.wait()
-    times = tiled_ref.shape[0] // count
-    rows = mesh_buf[...].astype(F32)
-    tiled_ref[...] = jnp.concatenate([rows] * times, axis=0).astype(BF16)
-    spare = pack_ref.shape[0] - grids
-    place = lax.broadcasted_iota(jnp.int32, (spare, latent), 0)
+    place = lax.broadcasted_iota(jnp.int32, pack_buf.shape, 0)
     index = jnp.where(place == 0, index_buf[0], jnp.where(place == 1, index_buf[1], index_buf[2]))
-    pack_ref[grids:, :] = index.astype(F32).astype(BF16)
+    pack_buf[...] = index.astype(F32).astype(BF16)
+    copies[7].start()
     ends = jnp.broadcast_to(near_buf[...], (count, 2 * half)).astype(F32)
     near_ref[...] = jnp.concatenate([cotangent_buf[...].astype(F32), ends], axis=0).astype(BF16)
+    copies[6].wait()
     copies[7].wait()
 
 
@@ -162,30 +171,34 @@
 
 def enc_kernel(
     pre_ref, dst_ref, mesh_ref, weight_ref, sum_ref, slope_ref,
-    pre_buf, hidden_buf, slope_buf, in_sems, out_sems,
+    pre_buf, hidden_buf, slope_buf, sum_buf, in_sems, slope_sem, sum_sems,
 ):
     latent = weight_ref.shape[1]
-    plane_nodes = mesh_ref.shape[0]
     tile = pre_buf.shape[0] // in_sems.shape[0]
     arriving = row_copies(pre_ref, pre_buf, in_sems, tile)
-    leaving = row_copies(slope_buf, slope_ref, out_sems, tile)
-    for copy in arriving:
-        copy.start()
+    (leaving,) = row_copies(slope_buf, slope_ref, slope_sem, slope_buf.shape[0])
+    halves = [slice(0, latent), slice(latent, 2 * latent)]
+    sums = [
+        pltpu.make_async_copy(sum_buf.at[:, half], sum_ref.at[:, half], sum_sems.at[i])
+        for i, half in enumerate(halves)
+    ]
+    arriving[0].start()
+    arriving[1].start()
     table = stack_split(dot(mesh_ref[...], weight_ref[...]))
     for i in range(len(arriving)):
         rows = slice(i * tile, (i + 1) * tile)
         spread = spread_rows(dst_ref[rows, :], table)
         arriving[i].wait()
+        if i + 2 < len(arriving):
+            arriving[i + 2].start()
         hidden, slope = silu_parts(pre_buf[rows, :] + spread)
         hidden_buf[rows, :] = hidden
         slope_buf[rows, :] = slope.astype(BF16)
-        leaving[i].start()
-    nodes = sum_ref.shape[1] // 2
-    node_sums = lambda values: dot_first(dst_ref[...], values).reshape(-1, nodes, latent)
-    sum_ref[...] = jnp.concatenate(
-        [node_sums(hidden_buf[...]), node_sums(slope_buf[...])], axis=1
-    ).astype(BF16)
-    for copy in leaving:
+    for i, values in enumerate((hidden_buf, slope_buf)):
+        sum_buf[:, halves[i]] = dot_first(dst_ref[...], values[...]).astype(BF16)
+        sums[i].start()
+    leaving.start()
+    for copy in (*sums, leaving):
         copy.wait()
 
 
@@ -193,9 +206,10 @@
     parts_ref, weight_ref, gain_ref, mesh_ref, near_ref, mid_ref, packet_ref, agg_ref, slopes_ref
 ):
     count = mesh_ref.shape[0]
+    latent = mesh_ref.shape[1]
     summed = jnp.sum(parts_ref[...].astype(F32), axis=0)
-    agg = wide_dot(summed[:count], weight_ref[...], dot)
-    slopes_ref[...] = summed[count:]
+    agg = wide_dot(summed[:, :latent], weight_ref[...], dot)
+    slopes_ref[...] = summed[:, latent:]
     agg_ref[...] = agg
     mid = mesh_ref[...].astype(F32) + layer_norm(agg, gain_ref[...])[0]
     mid_ref[...] = mid.astype(BF16)
@@ -341,7 +355,7 @@
 
     def exchange(values):
         return lax.all_to_all(
-            values.reshape(chips, -1, latent), "feat", split_axis=0, concat_axis=0, tiled=True,
+            values.reshape(chips, nodes, -1), "feat", split_axis=0, concat_axis=0, tiled=True,
             axis_index_groups=plane,
         )
 
@@ -357,25 +371,28 @@
     near_side = lambda step: [(i, i ^ step) for i in range(bands)]
     line = lambda index: index.reshape(1, edges)
 
-    tiled_mesh, pack, near = call(
+    tiled_mesh = call(
+        tile_kernel, shape((chips, nodes, latent), BF16), mesh_latent,
+        far=(0,), far_out=(0,), scratch=(sem(chips),),
+    )
+    pack, near = call(
         prep_kernel,
-        (
-            shape((plane_nodes, latent), BF16),
-            shape((grids + 16, latent), BF16),
-            shape((2 * nodes, latent), BF16),
-        ),
-        mesh_latent, grid_latent, cotangent, line(g2m_src), line(g2m_peer), line(g2m_slot),
+        (shape((grids + 16, latent), BF16), shape((2 * nodes, latent), BF16)),
+        grid_latent, cotangent, line(g2m_src), line(g2m_peer), line(g2m_slot),
         proc_src.reshape(1, -1), proc_dst.reshape(1, -1),
-        far=range(8),
+        far=range(7), far_out=(0,), cost=0,
         scratch=(
-            pltpu.VMEM((nodes, latent), BF16),
-            pltpu.VMEM((nodes, latent), BF16),
+            edge_buf(nodes, BF16),
             pltpu.VMEM((3, 1, edges), jnp.int32),
             pltpu.VMEM((1, latent), jnp.int32),
-            pltpu.SemaphoreType.DMA((8,)),
-        ),
-    )
-    mate_pack = swap(pack)
+            edge_buf(16, BF16),
+            sem(8),
+        ),
+    )
+    packs = lax.all_gather(
+        pack, "feat", axis=0, tiled=True, axis_index_groups=[[i, i + 1] for i in range(0, feats, 2)]
+    )
+    mate_pack = lax.dynamic_slice_in_dim(packs, (1 - core) * pack.shape[0], pack.shape[0])
     mesh_all = exchange(tiled_mesh).reshape(plane_nodes, latent)
 
     mate_index = mate_pack[grids : grids + 3].astype(jnp.int32)
@@ -396,16 +413,16 @@
     pre_src = call(
         src_kernel, shape((2 * edges, latent), F32),
         grid_latent, mate_pack, src_pick, enc_src_w, row(enc_bias),
-        far_out=(0,), scratch=(edge_buf(2 * edges, F32), sem(4)),
+        far_out=(0,), scratch=(edge_buf(2 * edges, F32), sem(4)), cost=0,
     )
     partial, slope = call(
         enc_kernel,
-        (shape((chips, 2 * nodes, latent), BF16), shape((2 * edges, latent), BF16)),
+        (shape((plane_nodes, 2 * latent), BF16), shape((2 * edges, latent), BF16)),
         pre_src, dst_pick, mesh_all, enc_dst_w,
-        far=(0,), far_out=(1,),
+        far=(0,), far_out=(0, 1),
         scratch=(
             edge_buf(2 * edges, F32), edge_buf(2 * edges, BF16), edge_buf(2 * edges, BF16),
-            sem(4), sem(4),
+            pltpu.VMEM((plane_nodes, 2 * latent), BF16), sem(8), sem(1), sem(2),
         ),
     )
     mid, packet, enc_agg, slopes = call(

time: 104 us -> 118 us (1.13)
  Pallas kernels: 19.1 us -> 36.8 us
  waiting for transfers between devices: 34 us -> 25.5 us
  blocking collectives: 0 us -> 3.28 us
  starting transfers between devices: 48.2 us -> 49.6 us
    pallas_call x9 -> x10, Pallas kernels: 19.1 us -> 36.8 us  [call(): pl.pallas_call(body, out_shape=outs[0] if single else outs, in_specs=[pl....]
    all_to_all x3, waiting for transfers between devices: 33 us -> 24.5 us  [exchange(): lax.all_to_all(values.reshape(chips, nodes, -1), 'feat', split_axis=0, co...]
    all_to_all x3, starting transfers between devices: 20.3 us -> 25 us  [exchange(): lax.all_to_all(values.reshape(chips, nodes, -1), 'feat', split_axis=0, co...]
    ppermute x2 -> x1, starting transfers between devices: 9.02 us -> 5.74 us  [swap(): return lax.ppermute(values, 'feat', [(i, i ^ 1) for i in range(feats)])]
    all_gather x0 -> x1, blocking collectives: none -> 3.28 us  [per_device(): lax.all_gather(pack, 'feat', axis=0, tiled=True, axis_index_groups=[[i, i...]
  transfers between devices with their start and end apart: 9 -> 8, of which waited for: 4 -> 3; matrix products, arithmetic and copies ran while one was open for 1% -> 1% of each run, Pallas kernels for 6% -> 13%
where the time goes in v5:
time: 118 us; the launch traced here: 117 us
  starting transfers between devices  49.6 us (42%)
  Pallas kernels  36.8 us (31%)
  waiting for transfers between devices  25.5 us (22%)
  blocking collectives  3.28 us (3%)
    pallas_call x10, Pallas kernels, call(): pl.pallas_call(body, out_shape=outs[0] if single else outs, in_specs=[pl....  36.8 us
    all_to_all x3, starting transfers between devices, exchange(): lax.all_to_all(values.reshape(chips, nodes, -1), 'feat', split_axis=0, co...  25 us
    all_to_all x3, waiting for transfers between devices, exchange(): lax.all_to_all(values.reshape(chips, nodes, -1), 'feat', split_axis=0, co...  24.5 us
    ppermute x1, starting transfers between devices, per_device(): lax.ppermute(mid, 'band', far_side(2))  7.61 us
    ppermute x1, starting transfers between devices, per_device(): lax.ppermute(packet, 'band', far_side(1))  7.29 us
    ppermute x1, starting transfers between devices, swap(): return lax.ppermute(values, 'feat', [(i, i ^ 1) for i in range(feats)])  5.74 us
    all_gather x1, blocking collectives, per_device(): lax.all_gather(pack, 'feat', axis=0, tiled=True, axis_index_groups=[[i, i...  3.28 us
  transfers between devices with their start and end apart: 8, of which 3 were waited for; matrix products, arithmetic and copies ran while one was open for 1% of the time, Pallas kernels for 13%

profile of v5, /device:TPU:201, one launch (start us, length us, event | category | flops | bytes accessed | tf_op | source)
XLA Modules:
  0.0 117.0 jit_solution(239289822229899053)
XLA Ops:
  0.6 0.0 copy-start.14
  0.6 9.3 %shard_map.195 = bf16[32,8,512]{2,1,0:T(8,128)(2,1)} custom-call(bf16[8,512]{1,0:T(8,128)(2,1)} %mesh_ref.3), custom_call_target="tpu_custom_call" | custom-call | flops 4000000000 | bytes 4194304 | tf_op jit(solution)/shard_map/pallas_call | solution.py:70
  10.0 0.0 copy-start
  10.0 0.0 copy-start.1
  10.0 0.0 copy-start.2
  10.0 9.7 %all-to-all-start = ((bf16[32,8,512]{2,1,0:T(8,128)(2,1)}), bf16[32,8,512]{2,1,0:T(8,128)(2,1)S(1)}, u32[]{:S(2)}, u32[]{:S(2)}) async-start(bf16[32,8,512]{2,1,0:T(8,128)(2,1)} %shard_map.195), calls=%async_computation | async-start | bytes 524288 | tf_op jit(solution)/shard_map/all_to_all | solution.py:357
  19.8 9.1 %shard_map.193 = (bf16[272,512]{1,0:T(8,128)(2,1)}, bf16[16,512]{1,0:T(8,128)(2,1)S(1)}) custom-call(bf16[256,512]{1,0:T(8,128)(2,1)} %own_ref.1, bf16[8,512]{1,0:T(8,128)(2,1)} %cotangent_ref.1, s32[1,512]{1,0:T(1,128)} %bitcast.32, s32[1,512]{1,0:T(1,128)} %bitcast.29, s32[1,512]{1,0:T(1,128)} %bitcast.31, s32[1,256]{1,0:T(1,128)} %bitcast.36, ...), custom_call_target="tpu_custom_call" | custom-call | tf_op jit(solution)/shard_map/pallas_call | solution.py:70
  28.9 3.3 %all_gather.3 = bf16[544,512]{1,0:T(8,128)(2,1)S(1)} all-gather(bf16[272,512]{1,0:T(8,128)(2,1)} %get-tuple-element.16), channel_id=1, replica_groups={{0,1},{2,3},{4,5},{6,7},{8,9},{10,11},{12,13},{14,15},{16,17},{18,19},{..., dimensions={0}, use_global_device_ids=true | all-gather | bytes 835584 | tf_op jit(solution)/shard_map/all_gather | solution.py:392
  32.2 0.0 copy-done.14
  32.2 0.2 fusion.pick_ref
  32.5 0.0 copy-start.12
  32.5 0.0 copy-start.13
  32.5 0.0 copy-start.6
  32.6 2.1 %shard_map.194.pre_ref = f32[1024,512]{1,0:T(8,128)} custom-call(bf16[256,512]{1,0:T(8,128)(2,1)S(1)} %copy-done, bf16[272,512]{1,0:T(8,128)(2,1)S(1)} %constant_dynamic-slice_fusion.mate_ref, bf16[1024,256]{1,0:T(8,128)(2,1)S(1)} %fusion.pick_ref, bf16[512,512]{1,0:T(8,128)(2,1)S(1)} %copy-done.1, f32[1,512]{1,0:T(1,128)S(1)} %bitcast.23), custom_call_target="tpu_custom_call" | custom-call | tf_op jit(solution)/shard_map/pallas_call | solution.py:70
  34.7 0.0 copy-done.12
  34.7 0.2 fusion.1.dst_ref
  35.0 0.0 all-to-all-done
  35.0 0.0 copy-start.7
  35.0 0.0 copy-start.8
  35.0 0.0 copy-start.9
  35.0 5.8 %shard_map.196 = (bf16[256,1024]{1,0:T(8,128)(2,1)}, bf16[1024,512]{1,0:T(8,128)(2,1)}) custom-call(f32[1024,512]{1,0:T(8,128)} %shard_map.194.pre_ref, bf16[1024,256]{1,0:T(8,128)(2,1)S(1)} %fusion.1.dst_ref, bf16[256,512]{1,0:T(8,128)(2,1)S(1)} %bitcast.21, bf16[512,512]{1,0:T(8,128)(2,1)S(1)} %copy-done.6), custom_call_target="tpu_custom_call" | custom-call | flops 4000000000 | bytes 4194304 | tf_op jit(solution)/shard_map/pallas_call | solution.py:70
  40.8 9.2 %all-to-all-start.1 = ((bf16[32,8,1024]{2,1,0:T(8,128)(2,1)}), bf16[32,8,1024]{2,1,0:T(8,128)(2,1)S(1)}, u32[]{:S(2)}, u32[]{:S(2)}) async-start(bf16[32,8,1024]{2,1,0:T(8,128)(2,1)} %bitcast.28), calls=%async_computation.1 | async-start | bytes 1048576 | tf_op jit(solution)/shard_map/all_to_all | solution.py:357
  50.1 16.2 %all-to-all-done.1.parts_ref = bf16[32,8,1024]{2,1,0:T(8,128)(2,1)S(1)} async-done(((bf16[32,8,1024]{2,1,0:T(8,128)(2,1)}), bf16[32,8,1024]{2,1,0:T(8,128)(2,1)S(1)}, u32[]{:S(2)}, u32[]{:S(2)}) %all-to-all-start.1) | async-done | bytes 524320 | tf_op jit(solution)/shard_map/all_to_all | solution.py:357
  66.3 0.0 copy-start.3
  66.3 0.0 copy-start.4
  66.3 0.0 copy-start.5
  66.3 0.0 copy-start.10
  66.4 0.0 copy-start.11
  66.4 0.4 shard_map.197
  66.8 2.0 %collective-permute-start = (bf16[24,512]{1,0:T(8,128)(2,1)S(1)}, bf16[24,512]{1,0:T(8,128)(2,1)S(1)}, u32[]{:S(2)}, u32[]{:S(2)}) collective-permute-start(bf16[24,512]{1,0:T(8,128)(2,1)S(1)} %get-tuple-element.19.own_ref), channel_id=1, source_target_pairs={{0,64},{64,0},{128,192},{192,128},{256,320},{320,256},{384,448},{4... | collective-permute-start | bytes 73736 | tf_op jit(solution)/shard_map/ppermute | solution.py:445
  68.8 7.3 %collective-permute-start.1 = (bf16[24,512]{1,0:T(8,128)(2,1)S(1)}, bf16[24,512]{1,0:T(8,128)(2,1)S(1)}, u32[]{:S(2)}, u32[]{:S(2)}) collective-permute-start(bf16[24,512]{1,0:T(8,128)(2,1)S(1)} %get-tuple-element.19.own_ref), channel_id=1, source_target_pairs={{64,128},{128,64},{192,256},{256,192},{320,384},{384,320},{448,512... | collective-permute-start | bytes 73736 | tf_op jit(solution)/shard_map/ppermute | solution.py:446
  76.1 1.9 %collective-permute-start.2 = (bf16[8,512]{1,0:T(8,128)(2,1)S(1)}, bf16[8,512]{1,0:T(8,128)(2,1)S(1)}, u32[]{:S(2)}, u32[]{:S(2)}) collective-permute-start(bf16[8,512]{1,0:T(8,128)(2,1)S(1)} %get-tuple-element.20), channel_id=1, source_target_pairs={{0,128},{64,192},{128,0},{192,64},{256,384},{320,448},{384,256},{4... | collective-permute-start | bytes 24584 | tf_op jit(solution)/shard_map/ppermute | solution.py:447
  78.1 7.6 %collective-permute-start.3 = (bf16[8,512]{1,0:T(8,128)(2,1)S(1)}, bf16[8,512]{1,0:T(8,128)(2,1)S(1)}, u32[]{:S(2)}, u32[]{:S(2)}) collective-permute-start(bf16[8,512]{1,0:T(8,128)(2,1)S(1)} %get-tuple-element.20), channel_id=1, source_target_pairs={{128,256},{256,128},{192,320},{320,192},{384,512},{512,384},{448,5... | collective-permute-start | bytes 24584 | tf_op jit(solution)/shard_map/ppermute | solution.py:448
  85.7 0.1 pad_add_fusion.2.info_ref
  85.8 0.0 collective-permute-done.2.three_ref
  85.8 0.9 collective-permute-done.3.four_ref
  86.7 0.0 collective-permute-done.one_ref
  86.7 0.0 collective-permute-done.1.two_ref
  86.8 3.8 %shard_map.198 = (bf16[8,512]{1,0:T(8,128)(2,1)}, f32[8,512]{1,0:T(8,128)S(1)}, bf16[256,512]{1,0:T(8,128)(2,1)}) custom-call(bf16[24,512]{1,0:T(8,128)(2,1)S(1)} %collective-permute-done.one_ref, bf16[24,512]{1,0:T(8,128)(2,1)S(1)} %collective-permute-done.1.two_ref, bf16[8,512]{1,0:T(8,128)(2,1)S(1)} %collective-permute-done.2.three_ref, ...), custom_call_target="tpu_custom_call" | custom-call | flops 4000000000 | bytes 4194304 | tf_op jit(solution)/shard_map/pallas_call | solution.py:70
  90.5 6.0 %all-to-all-start.2 = ((bf16[32,8,512]{2,1,0:T(8,128)(2,1)}), bf16[32,8,512]{2,1,0:T(8,128)(2,1)S(1)}, u32[]{:S(2)}, u32[]{:S(2)}) async-start(bf16[32,8,512]{2,1,0:T(8,128)(2,1)} %bitcast.19), calls=%async_computation.2 | async-start | bytes 524288 | tf_op jit(solution)/shard_map/all_to_all | solution.py:357
  96.6 0.1 fusion.2.pick_t_ref
  96.7 2.0 %shard_map.202 = bf16[8,512]{1,0:T(8,128)(2,1)} custom-call(bf16[256,512]{1,0:T(8,128)(2,1)} %get-tuple-element.23.tiled_ref, f32[8,512]{1,0:T(8,128)S(1)} %get-tuple-element.27.slopes_ref, f32[8,512]{1,0:T(8,128)S(1)} %get-tuple-element.28.grad_ref, bf16[512,512]{1,0:T(8,128)(2,1)S(1)} %copy-done.7, bf16[512,512]{1,0:T(8,128)(2,1)S(1)} %copy-done.6), custom_call_target="tpu_custom_call" | custom-call | flops 4000000000 | bytes 4194304 | tf_op jit(solution)/shard_map/pallas_call | solution.py:70
  98.7 8.3 %all-to-all-done.2 = bf16[32,8,512]{2,1,0:T(8,128)(2,1)S(1)} async-done(((bf16[32,8,512]{2,1,0:T(8,128)(2,1)}), bf16[32,8,512]{2,1,0:T(8,128)(2,1)S(1)}, u32[]{:S(2)}, u32[]{:S(2)}) %all-to-all-start.2) | async-done | bytes 262176 | tf_op jit(solution)/shard_map/all_to_all | solution.py:357
  107.0 1.7 %shard_map.199 = (bf16[512,512]{1,0:T(8,128)(2,1)S(1)}, bf16[256,512]{1,0:T(8,128)(2,1)S(1)}) custom-call(bf16[256,512]{1,0:T(8,128)(2,1)S(1)} %bitcast.22, bf16[1024,256]{1,0:T(8,128)(2,1)S(1)} %fusion.1.dst_ref, bf16[256,1024]{1,0:T(8,128)(2,1)S(1)} %fusion.2.pick_t_ref, bf16[1024,512]{1,0:T(8,128)(2,1)} %get-tuple-element.24.slope_ref, ...), custom_call_target="tpu_custom_call" | custom-call | flops 4000000000 | bytes 4194304 | tf_op jit(solution)/shard_map/pallas_call | solution.py:70
  108.7 5.7 %collective-permute-start.4 = (bf16[256,512]{1,0:T(8,128)(2,1)S(1)}, bf16[256,512]{1,0:T(8,128)(2,1)S(1)}, u32[]{:S(2)}, u32[]{:S(2)}) collective-permute-start(bf16[256,512]{1,0:T(8,128)(2,1)S(1)} %get-tuple-element.26), channel_id=1, source_target_pairs={{0,1},{1,0},{2,3},{3,2},{4,5},{5,4},{6,7},{7,6},{8,9},{9,8},{10,11... | collective-permute-start | bytes 786440 | tf_op jit(solution)/shard_map/ppermute | solution.py:363
  114.4 1.8 %shard_map.200.own_ref = f32[256,512]{1,0:T(8,128)S(1)} custom-call(bf16[512,512]{1,0:T(8,128)(2,1)S(1)} %get-tuple-element.25.table_ref, bf16[1024,256]{1,0:T(8,128)(2,1)S(1)} %fusion.1.dst_ref, bf16[256,1024]{1,0:T(8,128)(2,1)S(1)} %fusion.2.pick_t_ref, bf16[1024,512]{1,0:T(8,128)(2,1)} %get-tuple-element.24.slope_ref, bf16[512,512]{1,0:T(8,128)(2,1)S(1)} %copy-done.1), custom_call_target="tpu_custom_call" | custom-call | flops 4000000000 | bytes 4194304 | tf_op jit(solution)/shard_map/pallas_call | solution.py:70
  116.2 0.0 collective-permute-done.4.mate_ref
  116.2 0.7 shard_map.201
  (18 shorter events, 0.1 us)
Async XLA Ops:
  0.6 31.6 %copy-start.14 = (s32[512]{0:T(512)S(1)}, s32[512]{0:T(512)}, u32[]{:S(2)}) copy-start(s32[512]{0:T(512)} %param.20) | copy-start | bytes 6148
  10.0 22.5 %copy-start = (bf16[256,512]{1,0:T(8,128)(2,1)S(1)}, bf16[256,512]{1,0:T(8,128)(2,1)}, u32[]{:S(2)}) copy-start(bf16[256,512]{1,0:T(8,128)(2,1)} %own_ref.1) | copy-start | bytes 786436
  10.0 22.5 %copy-start.1 = (bf16[512,512]{1,0:T(8,128)(2,1)S(1)}, bf16[512,512]{1,0:T(8,128)(2,1)}, u32[]{:S(2)}) copy-start(bf16[512,512]{1,0:T(8,128)(2,1)} %src_w_ref.5) | copy-start | bytes 1572868
  10.0 22.5 %copy-start.2 = (f32[512]{0:T(512)S(1)}, f32[512]{0:T(512)}, u32[]{:S(2)}) copy-start(f32[512]{0:T(512)} %param.28) | copy-start | bytes 6148
  10.0 24.9 %all-to-all-start = ((bf16[32,8,512]{2,1,0:T(8,128)(2,1)}), bf16[32,8,512]{2,1,0:T(8,128)(2,1)S(1)}, u32[]{:S(2)}, u32[]{:S(2)}) async-start(bf16[32,8,512]{2,1,0:T(8,128)(2,1)} %shard_map.195), calls=%async_computation | async-start | bytes 524288 | tf_op jit(solution)/shard_map/all_to_all | solution.py:357
  32.5 2.2 %copy-start.12 = (s32[512,1]{0,1:T(1,128)S(1)}, s32[512,1]{0,1:T(1,128)}, u32[]{:S(2)}) copy-start(s32[512,1]{0,1:T(1,128)} %param.21) | copy-start | bytes 6148
  32.5 2.2 %copy-start.13 = (s32[512]{0:T(512)S(1)}, s32[512]{0:T(512)}, u32[]{:S(2)}) copy-start(s32[512]{0:T(512)} %param.22) | copy-start | bytes 6148
  32.5 2.4 %copy-start.6 = (bf16[512,512]{1,0:T(8,128)(2,1)S(1)}, bf16[512,512]{1,0:T(8,128)(2,1)}, u32[]{:S(2)}) copy-start(bf16[512,512]{1,0:T(8,128)(2,1)} %dst_w_ref.3) | copy-start | bytes 1572868
  35.0 31.3 %copy-start.7 = (bf16[512,512]{1,0:T(8,128)(2,1)S(1)}, bf16[512,512]{1,0:T(8,128)(2,1)}, u32[]{:S(2)}) copy-start(bf16[512,512]{1,0:T(8,128)(2,1)} %out_w_ref.5) | copy-start | bytes 1572868
  35.0 31.3 %copy-start.8 = (bf16[8,512]{1,0:T(8,128)(2,1)S(1)}, bf16[8,512]{1,0:T(8,128)(2,1)}, u32[]{:S(2)}) copy-start(bf16[8,512]{1,0:T(8,128)(2,1)} %mesh_ref.3) | copy-start | bytes 24580
  35.0 31.3 %copy-start.9 = (f32[512]{0:T(512)S(1)}, f32[512]{0:T(512)}, u32[]{:S(2)}) copy-start(f32[512]{0:T(512)} %param.29) | copy-start | bytes 6148
  40.8 25.5 %all-to-all-start.1 = ((bf16[32,8,1024]{2,1,0:T(8,128)(2,1)}), bf16[32,8,1024]{2,1,0:T(8,128)(2,1)S(1)}, u32[]{:S(2)}, u32[]{:S(2)}) async-start(bf16[32,8,1024]{2,1,0:T(8,128)(2,1)} %bitcast.28), calls=%async_computation.1 | async-start | bytes 1048576 | tf_op jit(solution)/shard_map/all_to_all | solution.py:357
  66.3 20.4 %copy-start.3 = (bf16[512,512]{1,0:T(8,128)(2,1)S(1)}, bf16[512,512]{1,0:T(8,128)(2,1)}, u32[]{:S(2)}) copy-start(bf16[512,512]{1,0:T(8,128)(2,1)} %src_w_ref.3) | copy-start | bytes 1572868
  66.3 20.4 %copy-start.4 = (bf16[512,512]{1,0:T(8,128)(2,1)S(1)}, bf16[512,512]{1,0:T(8,128)(2,1)}, u32[]{:S(2)}) copy-start(bf16[512,512]{1,0:T(8,128)(2,1)} %dst_w_ref.2) | copy-start | bytes 1572868
  66.3 20.4 %copy-start.5 = (bf16[512,512]{1,0:T(8,128)(2,1)S(1)}, bf16[512,512]{1,0:T(8,128)(2,1)}, u32[]{:S(2)}) copy-start(bf16[512,512]{1,0:T(8,128)(2,1)} %out_w_ref.3) | copy-start | bytes 1572868
  66.3 20.4 %copy-start.10 = (f32[512]{0:T(512)S(1)}, f32[512]{0:T(512)}, u32[]{:S(2)}) copy-start(f32[512]{0:T(512)} %param.33) | copy-start | bytes 6148
  66.4 20.4 %copy-start.11 = (f32[512]{0:T(512)S(1)}, f32[512]{0:T(512)}, u32[]{:S(2)}) copy-start(f32[512]{0:T(512)} %param.34) | copy-start | bytes 6148
  66.8 19.9 %collective-permute-start = (bf16[24,512]{1,0:T(8,128)(2,1)S(1)}, bf16[24,512]{1,0:T(8,128)(2,1)S(1)}, u32[]{:S(2)}, u32[]{:S(2)}) collective-permute-start(bf16[24,512]{1,0:T(8,128)(2,1)S(1)} %get-tuple-element.19.own_ref), channel_id=1, source_target_pairs={{0,64},{64,0},{128,192},{192,128},{256,320},{320,256},{384,448},{4... | collective-permute-start | bytes 73736 | tf_op jit(solution)/shard_map/ppermute | solution.py:445
  68.8 17.9 %collective-permute-start.1 = (bf16[24,512]{1,0:T(8,128)(2,1)S(1)}, bf16[24,512]{1,0:T(8,128)(2,1)S(1)}, u32[]{:S(2)}, u32[]{:S(2)}) collective-permute-start(bf16[24,512]{1,0:T(8,128)(2,1)S(1)} %get-tuple-element.19.own_ref), channel_id=1, source_target_pairs={{64,128},{128,64},{192,256},{256,192},{320,384},{384,320},{448,512... | collective-permute-start | bytes 73736 | tf_op jit(solution)/shard_map/ppermute | solution.py:446
  76.1 9.6 %collective-permute-start.2 = (bf16[8,512]{1,0:T(8,128)(2,1)S(1)}, bf16[8,512]{1,0:T(8,128)(2,1)S(1)}, u32[]{:S(2)}, u32[]{:S(2)}) collective-permute-start(bf16[8,512]{1,0:T(8,128)(2,1)S(1)} %get-tuple-element.20), channel_id=1, source_target_pairs={{0,128},{64,192},{128,0},{192,64},{256,384},{320,448},{384,256},{4... | collective-permute-start | bytes 24584 | tf_op jit(solution)/shard_map/ppermute | solution.py:447
  78.1 8.6 %collective-permute-start.3 = (bf16[8,512]{1,0:T(8,128)(2,1)S(1)}, bf16[8,512]{1,0:T(8,128)(2,1)S(1)}, u32[]{:S(2)}, u32[]{:S(2)}) collective-permute-start(bf16[8,512]{1,0:T(8,128)(2,1)S(1)} %get-tuple-element.20), channel_id=1, source_target_pairs={{128,256},{256,128},{192,320},{320,192},{384,512},{512,384},{448,5... | collective-permute-start | bytes 24584 | tf_op jit(solution)/shard_map/ppermute | solution.py:448
  90.5 16.4 %all-to-all-start.2 = ((bf16[32,8,512]{2,1,0:T(8,128)(2,1)}), bf16[32,8,512]{2,1,0:T(8,128)(2,1)S(1)}, u32[]{:S(2)}, u32[]{:S(2)}) async-start(bf16[32,8,512]{2,1,0:T(8,128)(2,1)} %bitcast.19), calls=%async_computation.2 | async-start | bytes 524288 | tf_op jit(solution)/shard_map/all_to_all | solution.py:357
  108.7 7.6 %collective-permute-start.4 = (bf16[256,512]{1,0:T(8,128)(2,1)S(1)}, bf16[256,512]{1,0:T(8,128)(2,1)S(1)}, u32[]{:S(2)}, u32[]{:S(2)}) collective-permute-start(bf16[256,512]{1,0:T(8,128)(2,1)S(1)} %get-tuple-element.26), channel_id=1, source_target_pairs={{0,1},{1,0},{2,3},{3,2},{4,5},{5,4},{6,7},{7,6},{8,9},{9,8},{10,11... | collective-permute-start | bytes 786440 | tf_op jit(solution)/shard_map/ppermute | solution.py:363

commit v6 on v4

--- a/solution.py
+++ b/solution.py
@@ -104,15 +104,22 @@
     return hidden.astype(BF16), sigma * (1.0 + (values - hidden))
 
 
+def tile_kernel(mesh_ref, tiled_ref, buf, sem):
+    copy = pltpu.make_async_copy(mesh_ref, buf, sem.at[0])
+    copy.start()
+    copy.wait()
+    times = tiled_ref.shape[0] // buf.shape[0]
+    tiled_ref[...] = jnp.concatenate([buf[...].astype(F32)] * times, axis=0).astype(BF16)
+
+
 def prep_kernel(
-    mesh_ref, grid_ref, cotangent_ref, src_ref, peer_ref, slot_ref, sender_ref, receiver_ref,
-    tiled_ref, pack_ref, near_ref, mesh_buf, cotangent_buf, index_buf, near_buf, sems,
-):
-    count, latent = mesh_buf.shape
+    grid_ref, cotangent_ref, src_ref, peer_ref, slot_ref, sender_ref, receiver_ref,
+    pack_ref, near_ref, cotangent_buf, index_buf, near_buf, sems,
+):
+    count, latent = cotangent_buf.shape
     grids = grid_ref.shape[0]
     half = sender_ref.shape[1]
     pairs = (
-        (mesh_ref, mesh_buf),
         (src_ref, index_buf.at[0]),
         (peer_ref, index_buf.at[1]),
         (slot_ref, index_buf.at[2]),
@@ -124,30 +131,24 @@
     copies = [pltpu.make_async_copy(*pair, sems.at[i]) for i, pair in enumerate(pairs)]
     for copy in copies:
         copy.start()
-    for copy in copies[:7]:
+    for copy in copies[:6]:
         copy.wait()
-    times = tiled_ref.shape[0] // count
-    rows = mesh_buf[...].astype(F32)
-    tiled_ref[...] = jnp.concatenate([rows] * times, axis=0).astype(BF16)
     spare = pack_ref.shape[0] - grids
     place = lax.broadcasted_iota(jnp.int32, (spare, latent), 0)
     index = jnp.where(place == 0, index_buf[0], jnp.where(place == 1, index_buf[1], index_buf[2]))
     pack_ref[grids:, :] = index.astype(F32).astype(BF16)
     ends = jnp.broadcast_to(near_buf[...], (count, 2 * half)).astype(F32)
     near_ref[...] = jnp.concatenate([cotangent_buf[...].astype(F32), ends], axis=0).astype(BF16)
-    copies[7].wait()
-
-
-def src_kernel(own_ref, mate_ref, pick_ref, weight_ref, bias_ref, pre_ref, buf, sems):
+    copies[6].wait()
+
+
+def src_kernel(own_ref, mate_ref, pick_ref, rows_ref):
     tile = own_ref.shape[0]
-    copies = row_copies(buf, pre_ref, sems, tile)
-    for i, copy in enumerate(copies):
-        grid_ref = own_ref if i < len(copies) // 2 else mate_ref
-        rows = dot(pick_ref[i * tile : (i + 1) * tile, :], grid_ref[:tile, :]).astype(BF16)
-        buf[i * tile : (i + 1) * tile, :] = dot(rows, weight_ref[...]) + bias_ref[...]
-        copy.start()
-    for copy in copies:
-        copy.wait()
+    edges = pick_ref.shape[0]
+    for start in range(0, edges, tile):
+        grid_ref = own_ref if start < edges // 2 else mate_ref
+        picked = dot(pick_ref[start : start + tile, :], grid_ref[:tile, :])
+        rows_ref[start : start + tile, :] = picked.astype(BF16)
 
 
 def stack_split(values):
@@ -161,29 +162,26 @@
 
 
 def enc_kernel(
-    pre_ref, dst_ref, mesh_ref, weight_ref, sum_ref, slope_ref,
-    pre_buf, hidden_buf, slope_buf, in_sems, out_sems,
-):
-    latent = weight_ref.shape[1]
-    plane_nodes = mesh_ref.shape[0]
-    tile = pre_buf.shape[0] // in_sems.shape[0]
-    arriving = row_copies(pre_ref, pre_buf, in_sems, tile)
-    leaving = row_copies(slope_buf, slope_ref, out_sems, tile)
-    for copy in arriving:
-        copy.start()
-    table = stack_split(dot(mesh_ref[...], weight_ref[...]))
-    for i in range(len(arriving)):
+    rows_ref, dst_ref, dst_t_ref, mesh_ref, src_w_ref, dst_w_ref, bias_ref, sum_ref, slope_ref,
+    both, slope_buf, sems,
+):
+    latent = dst_w_ref.shape[1]
+    tile = slope_buf.shape[0] // sems.shape[0]
+    leaving = row_copies(slope_buf, slope_ref, sems, tile)
+    table = stack_split(dot(mesh_ref[...], dst_w_ref[...]) + bias_ref[...])
+    for i, copy in enumerate(leaving):
         rows = slice(i * tile, (i + 1) * tile)
         spread = spread_rows(dst_ref[rows, :], table)
-        arriving[i].wait()
-        hidden, slope = silu_parts(pre_buf[rows, :] + spread)
-        hidden_buf[rows, :] = hidden
+        hidden, slope = silu_parts(dot(rows_ref[rows, :], src_w_ref[...]) + spread)
+        both[rows, :latent] = hidden
+        both[rows, latent:] = slope.astype(BF16)
         slope_buf[rows, :] = slope.astype(BF16)
-        leaving[i].start()
+        copy.start()
+    total = dot(dst_t_ref[...], both[...])
     nodes = sum_ref.shape[1] // 2
-    node_sums = lambda values: dot_first(dst_ref[...], values).reshape(-1, nodes, latent)
+    chunked = lambda v: v.reshape(-1, nodes, latent)
     sum_ref[...] = jnp.concatenate(
-        [node_sums(hidden_buf[...]), node_sums(slope_buf[...])], axis=1
+        [chunked(total[:, :latent]), chunked(total[:, latent:])], axis=1
     ).astype(BF16)
     for copy in leaving:
         copy.wait()
@@ -221,12 +219,24 @@
     )
 
 
+def partner_rows(ref, first, valid):
+    rows = ref[...].astype(F32)
+    half = rows.shape[0] // 2
+    return jnp.where(first == 0, rows[half:], rows[:half]) * valid.astype(F32)
+
+
 def proc_kernel(
     one_ref, two_ref, three_ref, four_ref, own_ref, info_ref, src_w_ref, dst_w_ref, out_w_ref,
     bias_ref, gain_ref, enc_agg_ref, enc_gain_ref, out_ref, grad_ref, tiled_ref,
 ):
-    count = three_ref.shape[0]
-    packets = [ref[...].astype(F32) for ref in (one_ref, two_ref, own_ref)]
+    count = out_ref.shape[0]
+    packets = [
+        partner_rows(one_ref, info_ref[4], info_ref[2]),
+        partner_rows(two_ref, 1 - info_ref[4], info_ref[3]),
+        own_ref[...].astype(F32),
+    ]
+    three = partner_rows(three_ref, info_ref[5], info_ref[6])
+    four = partner_rows(four_ref, 1 - info_ref[5], info_ref[7])
     one, two, mid = (packet[:count] for packet in packets)
     upstreams = jnp.concatenate([packet[count : 2 * count] for packet in packets], axis=0)
     index = [packet[2 * count : 2 * count + 1].astype(jnp.int32) for packet in packets]
@@ -242,7 +252,7 @@
     pick_t = chosen.astype(BF16)
     pick = jnp.concatenate([chosen] * 3, axis=0).astype(BF16)
 
-    rows = [one, two, three_ref[...].astype(F32), four_ref[...].astype(F32), mid]
+    rows = [one, two, three, four, mid]
     senders = jnp.concatenate(rows, axis=0).astype(BF16)
     receivers = jnp.concatenate([one, two, mid], axis=0).astype(BF16)
     table = jnp.concatenate(
@@ -348,34 +358,35 @@
     def swap(values):
         return lax.ppermute(values, "feat", [(i, i ^ 1) for i in range(feats)])
 
-    far_side = lambda step: [
-        pair
-        for i in range(bands - step)
-        if i & step
-        for pair in ((i, i + step), (i + step, i))
-    ]
-    near_side = lambda step: [(i, i ^ step) for i in range(bands)]
+    near_side = lambda step: [[i, i + step] for i in range(bands) if not i & step]
+    far_side = lambda step: [[i, (i + step) % bands] for i in range(bands) if i & step]
+
+    def meet(values, groups):
+        return lax.all_gather(values, "band", axis=0, tiled=True, axis_index_groups=groups)
+
     line = lambda index: index.reshape(1, edges)
 
-    tiled_mesh, pack, near = call(
+    tiled_mesh = call(
+        tile_kernel, shape((plane_nodes, latent), BF16), mesh_latent,
+        far=(0,), scratch=(edge_buf(nodes, BF16), sem(1)),
+    )
+    pack, near = call(
         prep_kernel,
-        (
-            shape((plane_nodes, latent), BF16),
-            shape((grids + 16, latent), BF16),
-            shape((2 * nodes, latent), BF16),
-        ),
-        mesh_latent, grid_latent, cotangent, line(g2m_src), line(g2m_peer), line(g2m_slot),
+        (shape((grids + 16, latent), BF16), shape((2 * nodes, latent), BF16)),
+        grid_latent, cotangent, line(g2m_src), line(g2m_peer), line(g2m_slot),
         proc_src.reshape(1, -1), proc_dst.reshape(1, -1),
-        far=range(8),
+        far=range(7), cost=0,
         scratch=(
-            pltpu.VMEM((nodes, latent), BF16),
-            pltpu.VMEM((nodes, latent), BF16),
+            edge_buf(nodes, BF16),
             pltpu.VMEM((3, 1, edges), jnp.int32),
             pltpu.VMEM((1, latent), jnp.int32),
-            pltpu.SemaphoreType.DMA((8,)),
+            sem(7),
         ),
     )
-    mate_pack = swap(pack)
+    packs = lax.all_gather(
+        pack, "feat", axis=0, tiled=True, axis_index_groups=[[i, i + 1] for i in range(0, feats, 2)]
+    )
+    mate_pack = lax.dynamic_slice_in_dim(packs, (1 - core) * pack.shape[0], pack.shape[0])
     mesh_all = exchange(tiled_mesh).reshape(plane_nodes, latent)
 
     mate_index = mate_pack[grids : grids + 3].astype(jnp.int32)
@@ -387,26 +398,25 @@
     src_pick = (source[:, None] == grid_ids[None, :]).astype(BF16)
     src_pick_t = (source[None, :] == grid_ids[:, None]).astype(BF16)
     dst_pick = (target[:, None] == node_ids[None, :]).astype(BF16)
+    dst_pick_t = (target[None, :] == node_ids[:, None]).astype(BF16)
 
     step_one = jnp.where(band & 1 == 0, 1, -1)
     step_two = jnp.where(band & 2 == 0, 2, -2)
     inside = lambda place: jnp.logical_and(place >= 0, place < bands)
-    info = jnp.stack([step_one, step_two, inside(band + step_one), inside(band - step_one)])
-
-    pre_src = call(
-        src_kernel, shape((2 * edges, latent), F32),
-        grid_latent, mate_pack, src_pick, enc_src_w, row(enc_bias),
-        far_out=(0,), scratch=(edge_buf(2 * edges, F32), sem(4)),
+    info = jnp.stack([
+        step_one, step_two, inside(band + step_one), inside(band - step_one),
+        band & 1, (band & 2) // 2, inside(band + step_two), inside(band - step_two),
+    ])
+
+    src_rows = call(
+        src_kernel, shape((2 * edges, latent), BF16), grid_latent, mate_pack, src_pick, cost=0,
     )
     partial, slope = call(
         enc_kernel,
         (shape((chips, 2 * nodes, latent), BF16), shape((2 * edges, latent), BF16)),
-        pre_src, dst_pick, mesh_all, enc_dst_w,
-        far=(0,), far_out=(1,),
-        scratch=(
-            edge_buf(2 * edges, F32), edge_buf(2 * edges, BF16), edge_buf(2 * edges, BF16),
-            sem(4), sem(4),
-        ),
+        src_rows, dst_pick, dst_pick_t, mesh_all, enc_src_w, enc_dst_w, row(enc_bias),
+        far_out=(1,),
+        scratch=(pltpu.VMEM((2 * edges, 2 * latent), BF16), edge_buf(2 * edges, BF16), sem(4)),
     )
     mid, packet, enc_agg, slopes = call(
         mid_kernel,
@@ -425,10 +435,8 @@
             shape((nodes, latent), F32),
             shape((plane_nodes, latent), BF16),
         ),
-        lax.ppermute(packet, "band", near_side(1)),
-        lax.ppermute(packet, "band", far_side(1)),
-        lax.ppermute(mid, "band", near_side(2)),
-        lax.ppermute(mid, "band", far_side(2)),
+        meet(packet, near_side(1)), meet(packet, far_side(1)),
+        meet(mid, near_side(2)), meet(mid, far_side(2)),
         packet, info.astype(jnp.int32), proc_src_w, proc_dst_w, proc_out_w, row(proc_bias),
         row(proc_gain), enc_agg, row(enc_gain),
         small=(5,),

time: 104 us -> 110 us (1.058)
  the two profiles are of different devices: /device:TPU:201 before, /device:TPU:1 now
where the time goes in v6:
time: 110 us
  starting transfers between devices  37 us (34%)
  blocking collectives  29.8 us (27%)
  waiting for transfers between devices  21.8 us (20%)
  Pallas kernels  16.8 us (15%)
  local copies, waits for them, and re-layouts  2.74 us (2%)
    all_to_all x3, starting transfers between devices, exchange(): lax.all_to_all(values.reshape(chips, -1, latent), 'feat', split_axis=0, c...  27.9 us
    all_gather x4, blocking collectives, meet(): lax.all_gather(values, 'band', axis=0, tiled=True, axis_index_groups=groups)  24.1 us
    all_to_all x3, waiting for transfers between devices, exchange(): lax.all_to_all(values.reshape(chips, -1, latent), 'feat', split_axis=0, c...  21.8 us
    pallas_call x10, Pallas kernels, call(): pl.pallas_call(body, out_shape=outs[0] if single else outs, in_specs=[pl....  16.8 us
    ppermute x1, starting transfers between devices, swap(): return lax.ppermute(values, 'feat', [(i, i ^ 1) for i in range(feats)])  9.07 us
    all_gather x1, blocking collectives, per_device(): lax.all_gather(pack, 'feat', axis=0, tiled=True, axis_index_groups=[[i, i...  5.72 us
    unnamed x30, local copies, waits for them, and re-layouts  2.63 us
  transfers between devices with their start and end apart: 4, of which 3 were waited for; matrix products, arithmetic and copies ran while one was open for 1% of the time, Pallas kernels for 5%

profile of v6, /device:TPU:1, one launch (start us, length us, event | category | flops | bytes accessed | tf_op | source)
XLA Modules:
  0.0 109.8 jit_solution(3150310580210330016)
XLA Ops:
  0.6 1.4 %shard_map.195 = bf16[256,512]{1,0:T(8,128)(2,1)} custom-call(bf16[8,512]{1,0:T(8,128)(2,1)} %mesh_ref.3), custom_call_target="tpu_custom_call" | custom-call | flops 4000000000 | bytes 4194304 | tf_op jit(solution)/shard_map/pallas_call | solution.py:70
  2.1 10.5 %all-to-all-start = ((bf16[32,8,512]{2,1,0:T(8,128)(2,1)}), bf16[32,8,512]{2,1,0:T(8,128)(2,1)S(1)}, u32[]{:S(2)}, u32[]{:S(2)}) async-start(bf16[32,8,512]{2,1,0:T(8,128)(2,1)} %bitcast.9), calls=%async_computation | async-start | bytes 524288 | tf_op jit(solution)/shard_map/all_to_all | solution.py:353
  12.6 1.1 %shard_map.193 = (bf16[272,512]{1,0:T(8,128)(2,1)S(1)}, bf16[16,512]{1,0:T(8,128)(2,1)S(1)}) custom-call(bf16[256,512]{1,0:T(8,128)(2,1)} %own_ref.1, bf16[8,512]{1,0:T(8,128)(2,1)} %cotangent_ref.1, s32[1,512]{1,0:T(1,128)} %bitcast.35, s32[1,512]{1,0:T(1,128)} %bitcast.32, s32[1,512]{1,0:T(1,128)} %bitcast.34, s32[1,256]{1,0:T(1,128)} %bitcast.39, ...), custom_call_target="tpu_custom_call" | custom-call | tf_op jit(solution)/shard_map/pallas_call | solution.py:70
  13.7 5.7 %all_gather.15 = bf16[544,512]{1,0:T(8,128)(2,1)S(1)} all-gather(bf16[272,512]{1,0:T(8,128)(2,1)S(1)} %get-tuple-element.16), channel_id=1, replica_groups={{0,1},{2,3},{4,5},{6,7},{8,9},{10,11},{12,13},{14,15},{16,17},{18,19},{..., dimensions={0}, use_global_device_ids=true | all-gather | bytes 835584 | tf_op jit(solution)/shard_map/all_gather | solution.py:386
  19.5 0.0 copy-start.14
  19.5 0.7 copy-done.14
  20.2 0.2 fusion.pick_ref
  20.4 0.0 copy-start.13
  20.4 0.0 copy-start.12
  20.4 0.7 copy-done.13
  21.1 0.0 copy-done.12
  21.1 0.0 copy-done
  21.1 0.4 shard_map.194.rows_ref
  21.6 0.0 copy-start.4
  21.6 0.0 copy-start.6
  21.6 0.2 fusion.1.dst_ref
  21.8 0.1 fusion.2.dst_t_ref
  21.9 0.0 copy-start.8
  21.9 0.3 all-to-all-done
  22.3 0.4 copy-done.4
  22.6 0.2 copy-done.6
  22.8 0.0 copy-done.8
  22.8 3.4 %shard_map.196 = (bf16[32,16,512]{2,1,0:T(8,128)(2,1)}, bf16[1024,512]{1,0:T(8,128)(2,1)}) custom-call(bf16[1024,512]{1,0:T(8,128)(2,1)S(1)} %shard_map.194.rows_ref, bf16[1024,256]{1,0:T(8,128)(2,1)S(1)} %fusion.1.dst_ref, bf16[256,1024]{1,0:T(8,128)(2,1)S(1)} %fusion.2.dst_t_ref, bf16[256,512]{1,0:T(8,128)(2,1)S(1)} %bitcast.25, ...), custom_call_target="tpu_custom_call" | custom-call | flops 4000000000 | bytes 4194304 | tf_op jit(solution)/shard_map/pallas_call | solution.py:70
  26.2 0.0 copy-start.5
  26.2 9.7 %all-to-all-start.1 = ((bf16[32,16,512]{2,1,0:T(8,128)(2,1)}), bf16[32,16,512]{2,1,0:T(8,128)(2,1)S(1)}, u32[]{:S(2)}, u32[]{:S(2)}) async-start(bf16[32,16,512]{2,1,0:T(8,128)(2,1)} %get-tuple-element.17), calls=%async_computation.1 | async-start | bytes 1048576 | tf_op jit(solution)/shard_map/all_to_all | solution.py:353
  35.9 0.0 copy-start.7
  35.9 0.1 stack.51.info_ref
  36.0 14.0 %all-to-all-done.1.parts_ref = bf16[32,16,512]{2,1,0:T(8,128)(2,1)S(1)} async-done(((bf16[32,16,512]{2,1,0:T(8,128)(2,1)}), bf16[32,16,512]{2,1,0:T(8,128)(2,1)S(1)}, u32[]{:S(2)}, u32[]{:S(2)}) %all-to-all-start.1) | async-done | bytes 524320 | tf_op jit(solution)/shard_map/all_to_all | solution.py:353
  50.0 0.0 copy-start.1
  50.0 0.0 copy-start.2
  50.0 0.0 copy-start.3
  50.0 0.0 copy-start.11
  50.0 0.4 shard_map.197
  50.4 3.5 %all_gather.16.one_ref = bf16[48,512]{1,0:T(8,128)(2,1)S(1)} all-gather(bf16[24,512]{1,0:T(8,128)(2,1)S(1)} %get-tuple-element.19.own_ref), channel_id=1, replica_groups={{0,64},{128,192},{256,320},{384,448},{512,576},{640,704},{1,65},{129,19..., dimensions={0}, use_global_device_ids=true | all-gather | bytes 73728 | tf_op jit(solution)/shard_map/all_gather | solution.py:365
  53.9 11.2 %all_gather.17.two_ref = bf16[48,512]{1,0:T(8,128)(2,1)S(1)} all-gather(bf16[24,512]{1,0:T(8,128)(2,1)S(1)} %get-tuple-element.19.own_ref), channel_id=1, replica_groups={{64,128},{192,256},{320,384},{448,512},{576,640},{704,0},{65,129},{193,..., dimensions={0}, use_global_device_ids=true | all-gather | bytes 73728 | tf_op jit(solution)/shard_map/all_gather | solution.py:365
  65.1 4.1 %all_gather.18.three_ref = bf16[16,512]{1,0:T(8,128)(2,1)S(1)} all-gather(bf16[8,512]{1,0:T(8,128)(2,1)S(1)} %get-tuple-element.20), channel_id=1, replica_groups={{0,128},{64,192},{256,384},{320,448},{512,640},{576,704},{1,129},{65,19..., dimensions={0}, use_global_device_ids=true | all-gather | bytes 24576 | tf_op jit(solution)/shard_map/all_gather | solution.py:365
  69.2 5.3 %all_gather.19.four_ref = bf16[16,512]{1,0:T(8,128)(2,1)S(1)} all-gather(bf16[8,512]{1,0:T(8,128)(2,1)S(1)} %get-tuple-element.20), channel_id=1, replica_groups={{128,256},{192,320},{384,512},{448,576},{640,0},{704,64},{129,257},{193..., dimensions={0}, use_global_device_ids=true | all-gather | bytes 24576 | tf_op jit(solution)/shard_map/all_gather | solution.py:365
  74.6 0.7 copy-done.10
  75.2 3.8 %shard_map.198 = (bf16[8,512]{1,0:T(8,128)(2,1)}, f32[8,512]{1,0:T(8,128)S(1)}, bf16[256,512]{1,0:T(8,128)(2,1)}) custom-call(bf16[48,512]{1,0:T(8,128)(2,1)S(1)} %all_gather.16.one_ref, bf16[48,512]{1,0:T(8,128)(2,1)S(1)} %all_gather.17.two_ref, bf16[16,512]{1,0:T(8,128)(2,1)S(1)} %all_gather.18.three_ref, bf16[16,512]{1,0:T(8,128)(2,1)S(1)} %all_gather.19.four_ref, ...), custom_call_target="tpu_custom_call" | custom-call | flops 4000000000 | bytes 4194304 | tf_op jit(solution)/shard_map/pallas_call | solution.py:70
  79.0 7.7 %all-to-all-start.2 = ((bf16[32,8,512]{2,1,0:T(8,128)(2,1)}), bf16[32,8,512]{2,1,0:T(8,128)(2,1)S(1)}, u32[]{:S(2)}, u32[]{:S(2)}) async-start(bf16[32,8,512]{2,1,0:T(8,128)(2,1)} %bitcast.23), calls=%async_computation.2 | async-start | bytes 524288 | tf_op jit(solution)/shard_map/all_to_all | solution.py:353
  86.8 0.1 fusion.3.pick_t_ref
  86.9 2.0 %shard_map.202 = bf16[8,512]{1,0:T(8,128)(2,1)} custom-call(bf16[256,512]{1,0:T(8,128)(2,1)} %get-tuple-element.23.tiled_ref, f32[8,512]{1,0:T(8,128)S(1)} %get-tuple-element.27.slopes_ref, f32[8,512]{1,0:T(8,128)S(1)} %get-tuple-element.28.grad_ref, bf16[512,512]{1,0:T(8,128)(2,1)S(1)} %copy-done.5, bf16[512,512]{1,0:T(8,128)(2,1)S(1)} %copy-done.4), custom_call_target="tpu_custom_call" | custom-call | flops 4000000000 | bytes 4194304 | tf_op jit(solution)/shard_map/pallas_call | solution.py:70
  88.9 7.5 %all-to-all-done.2 = bf16[32,8,512]{2,1,0:T(8,128)(2,1)S(1)} async-done(((bf16[32,8,512]{2,1,0:T(8,128)(2,1)}), bf16[32,8,512]{2,1,0:T(8,128)(2,1)S(1)}, u32[]{:S(2)}, u32[]{:S(2)}) %all-to-all-start.2) | async-done | bytes 262176 | tf_op jit(solution)/shard_map/all_to_all | solution.py:353
  96.4 1.7 %shard_map.199 = (bf16[512,512]{1,0:T(8,128)(2,1)S(1)}, bf16[256,512]{1,0:T(8,128)(2,1)S(1)}) custom-call(bf16[256,512]{1,0:T(8,128)(2,1)S(1)} %bitcast.26, bf16[1024,256]{1,0:T(8,128)(2,1)S(1)} %fusion.1.dst_ref, bf16[256,1024]{1,0:T(8,128)(2,1)S(1)} %fusion.3.pick_t_ref, bf16[1024,512]{1,0:T(8,128)(2,1)} %get-tuple-element.24.slope_ref, ...), custom_call_target="tpu_custom_call" | custom-call | flops 4000000000 | bytes 4194304 | tf_op jit(solution)/shard_map/pallas_call | solution.py:70
  98.2 9.1 %collective-permute-start = (bf16[256,512]{1,0:T(8,128)(2,1)S(1)}, bf16[256,512]{1,0:T(8,128)(2,1)S(1)}, u32[]{:S(2)}, u32[]{:S(2)}) collective-permute-start(bf16[256,512]{1,0:T(8,128)(2,1)S(1)} %get-tuple-element.26), channel_id=1, source_target_pairs={{0,1},{1,0},{2,3},{3,2},{4,5},{5,4},{6,7},{7,6},{8,9},{9,8},{10,11... | collective-permute-start | bytes 786440 | tf_op jit(solution)/shard_map/ppermute | solution.py:359
  107.2 1.8 %shard_map.200.own_ref = f32[256,512]{1,0:T(8,128)S(1)} custom-call(bf16[512,512]{1,0:T(8,128)(2,1)S(1)} %get-tuple-element.25.table_ref, bf16[1024,256]{1,0:T(8,128)(2,1)S(1)} %fusion.1.dst_ref, bf16[256,1024]{1,0:T(8,128)(2,1)S(1)} %fusion.3.pick_t_ref, bf16[1024,512]{1,0:T(8,128)(2,1)} %get-tuple-element.24.slope_ref, bf16[512,512]{1,0:T(8,128)(2,1)S(1)} %copy-done.6), custom_call_target="tpu_custom_call" | custom-call | flops 4000000000 | bytes 4194304 | tf_op jit(solution)/shard_map/pallas_call | solution.py:70
  109.0 0.0 collective-permute-done.mate_ref
  109.1 0.7 shard_map.201
  (15 shorter events, 0.1 us)
Async XLA Ops:
  2.1 20.2 %all-to-all-start = ((bf16[32,8,512]{2,1,0:T(8,128)(2,1)}), bf16[32,8,512]{2,1,0:T(8,128)(2,1)S(1)}, u32[]{:S(2)}, u32[]{:S(2)}) async-start(bf16[32,8,512]{2,1,0:T(8,128)(2,1)} %bitcast.9), calls=%async_computation | async-start | bytes 524288 | tf_op jit(solution)/shard_map/all_to_all | solution.py:353
  19.5 0.7 copy-start.14
  20.2 0.9 copy-start
  20.4 0.7 copy-start.13
  20.4 0.7 copy-start.12
  21.6 1.0 copy-start.4
  21.6 1.2 %copy-start.6 = (bf16[512,512]{1,0:T(8,128)(2,1)S(1)}, bf16[512,512]{1,0:T(8,128)(2,1)}, u32[]{:S(2)}) copy-start(bf16[512,512]{1,0:T(8,128)(2,1)} %src_w_ref.7) | copy-start | bytes 1572868
  21.9 0.9 copy-start.8
  26.2 23.8 %copy-start.5 = (bf16[512,512]{1,0:T(8,128)(2,1)S(1)}, bf16[512,512]{1,0:T(8,128)(2,1)}, u32[]{:S(2)}) copy-start(bf16[512,512]{1,0:T(8,128)(2,1)} %out_w_ref.5) | copy-start | bytes 1572868
  26.2 23.8 %all-to-all-start.1 = ((bf16[32,16,512]{2,1,0:T(8,128)(2,1)}), bf16[32,16,512]{2,1,0:T(8,128)(2,1)S(1)}, u32[]{:S(2)}, u32[]{:S(2)}) async-start(bf16[32,16,512]{2,1,0:T(8,128)(2,1)} %get-tuple-element.17), calls=%async_computation.1 | async-start | bytes 1048576 | tf_op jit(solution)/shard_map/all_to_all | solution.py:353
  35.9 14.1 %copy-start.7 = (bf16[8,512]{1,0:T(8,128)(2,1)S(1)}, bf16[8,512]{1,0:T(8,128)(2,1)}, u32[]{:S(2)}) copy-start(bf16[8,512]{1,0:T(8,128)(2,1)} %mesh_ref.3) | copy-start | bytes 24580
  36.0 14.0 %copy-start.9 = (f32[512]{0:T(512)S(1)}, f32[512]{0:T(512)}, u32[]{:S(2)}) copy-start(f32[512]{0:T(512)} %param.29) | copy-start | bytes 6148
  50.0 24.6 %copy-start.1 = (bf16[512,512]{1,0:T(8,128)(2,1)S(1)}, bf16[512,512]{1,0:T(8,128)(2,1)}, u32[]{:S(2)}) copy-start(bf16[512,512]{1,0:T(8,128)(2,1)} %src_w_ref.5) | copy-start | bytes 1572868
  50.0 24.6 %copy-start.2 = (bf16[512,512]{1,0:T(8,128)(2,1)S(1)}, bf16[512,512]{1,0:T(8,128)(2,1)}, u32[]{:S(2)}) copy-start(bf16[512,512]{1,0:T(8,128)(2,1)} %dst_w_ref.4) | copy-start | bytes 1572868
  50.0 24.5 %copy-start.3 = (bf16[512,512]{1,0:T(8,128)(2,1)S(1)}, bf16[512,512]{1,0:T(8,128)(2,1)}, u32[]{:S(2)}) copy-start(bf16[512,512]{1,0:T(8,128)(2,1)} %out_w_ref.3) | copy-start | bytes 1572868
  50.0 24.5 %copy-start.11 = (f32[512]{0:T(512)S(1)}, f32[512]{0:T(512)}, u32[]{:S(2)}) copy-start(f32[512]{0:T(512)} %param.34) | copy-start | bytes 6148
  74.6 0.7 copy-start.10
  79.0 17.4 %all-to-all-start.2 = ((bf16[32,8,512]{2,1,0:T(8,128)(2,1)}), bf16[32,8,512]{2,1,0:T(8,128)(2,1)S(1)}, u32[]{:S(2)}, u32[]{:S(2)}) async-start(bf16[32,8,512]{2,1,0:T(8,128)(2,1)} %bitcast.23), calls=%async_computation.2 | async-start | bytes 524288 | tf_op jit(solution)/shard_map/all_to_all | solution.py:353
  98.2 10.9 %collective-permute-start = (bf16[256,512]{1,0:T(8,128)(2,1)S(1)}, bf16[256,512]{1,0:T(8,128)(2,1)S(1)}, u32[]{:S(2)}, u32[]{:S(2)}) collective-permute-start(bf16[256,512]{1,0:T(8,128)(2,1)S(1)} %get-tuple-element.26), channel_id=1, source_target_pairs={{0,1},{1,0},{2,3},{3,2},{4,5},{5,4},{6,7},{7,6},{8,9},{9,8},{10,11... | collective-permute-start | bytes 786440 | tf_op jit(solution)/shard_map/ppermute | solution.py:359

commit v7 on v6

--- a/solution.py
+++ b/solution.py
@@ -27,14 +27,6 @@
     high, low = split(values)
     both = product(jnp.concatenate([high.astype(F32), low.astype(F32)], axis=0).astype(BF16), weight)
     return both[:rows] + both[rows:]
-
-
-def thirds(values):
-    high, rest = values.astype(BF16), values
-    rest = rest - high.astype(F32)
-    mid = rest.astype(BF16).astype(F32)
-    low = (rest - mid).astype(BF16).astype(F32)
-    return jnp.concatenate([high.astype(F32), mid, low], axis=0).astype(BF16)
 
 
 def layer_norm(values, gain):
@@ -219,24 +211,12 @@
     )
 
 
-def partner_rows(ref, first, valid):
-    rows = ref[...].astype(F32)
-    half = rows.shape[0] // 2
-    return jnp.where(first == 0, rows[half:], rows[:half]) * valid.astype(F32)
-
-
 def proc_kernel(
     one_ref, two_ref, three_ref, four_ref, own_ref, info_ref, src_w_ref, dst_w_ref, out_w_ref,
     bias_ref, gain_ref, enc_agg_ref, enc_gain_ref, out_ref, grad_ref, tiled_ref,
 ):
     count = out_ref.shape[0]
-    packets = [
-        partner_rows(one_ref, info_ref[4], info_ref[2]),
-        partner_rows(two_ref, 1 - info_ref[4], info_ref[3]),
-        own_ref[...].astype(F32),
-    ]
-    three = partner_rows(three_ref, info_ref[5], info_ref[6])
-    four = partner_rows(four_ref, 1 - info_ref[5], info_ref[7])
+    packets = [ref[...].astype(F32) for ref in (one_ref, two_ref, own_ref)]
     one, two, mid = (packet[:count] for packet in packets)
     upstreams = jnp.concatenate([packet[count : 2 * count] for packet in packets], axis=0)
     index = [packet[2 * count : 2 * count + 1].astype(jnp.int32) for packet in packets]
@@ -250,15 +230,15 @@
     ids = lax.broadcasted_iota(jnp.int32, (8 * count, sender.shape[1]), 0)
     chosen = jnp.where(jnp.logical_or(ids == sender, ids == receiver), 1.0, 0.0)
     pick_t = chosen.astype(BF16)
-    pick = jnp.concatenate([chosen] * 3, axis=0).astype(BF16)
-
-    rows = [one, two, three, four, mid]
+    pick = jnp.concatenate([chosen] * 2, axis=0).astype(BF16)
+
+    rows = [one, two, three_ref[...].astype(F32), four_ref[...].astype(F32), mid]
     senders = jnp.concatenate(rows, axis=0).astype(BF16)
     receivers = jnp.concatenate([one, two, mid], axis=0).astype(BF16)
     table = jnp.concatenate(
         [dot(senders, src_w_ref[...]), dot(receivers, dst_w_ref[...]) + bias_ref[...]], axis=0
     )
-    hidden, slope = silu_parts(dot_first(pick, thirds(table)))
+    hidden, slope = silu_parts(dot_first(pick, stack_split(table)))
     summed = dot(pick_t, hidden)[5 * count :]
     agg = wide_dot(summed, out_w_ref[...], dot)
     shifted, normed, inv_std = layer_norm(agg, gain_ref[...])
@@ -266,7 +246,7 @@
     grad_agg = norm_back(normed, inv_std, gain_ref[...], upstreams).astype(BF16)
     back = dot_t(grad_agg, out_w_ref[...])
     blank = jnp.zeros((5 * count, back.shape[1]), F32)
-    spread = dot_first(pick, thirds(jnp.concatenate([blank, back], axis=0)))
+    spread = dot_first(pick, stack_split(jnp.concatenate([blank, back], axis=0)))
     sums = dot(pick_t, (spread * slope).astype(BF16))
     sender_sum = wide_dot(sums[4 * count : 5 * count], src_w_ref[...], dot_t)
     receiver_sum = wide_dot(sums[7 * count :], dst_w_ref[...], dot_t)
@@ -358,11 +338,16 @@
     def swap(values):
         return lax.ppermute(values, "feat", [(i, i ^ 1) for i in range(feats)])
 
-    near_side = lambda step: [[i, i + step] for i in range(bands) if not i & step]
-    far_side = lambda step: [[i, (i + step) % bands] for i in range(bands) if i & step]
-
-    def meet(values, groups):
-        return lax.all_gather(values, "band", axis=0, tiled=True, axis_index_groups=groups)
+    near_side = lambda step: [(i, i ^ step) for i in range(bands)]
+    far_side = lambda step: [
+        pair
+        for i in range(bands - step)
+        if i & step
+        for pair in ((i, i + step), (i + step, i))
+    ]
+
+    def meet(values, pairs):
+        return lax.ppermute(values, "band", pairs)
 
     line = lambda index: index.reshape(1, edges)
 
@@ -403,10 +388,7 @@
     step_one = jnp.where(band & 1 == 0, 1, -1)
     step_two = jnp.where(band & 2 == 0, 2, -2)
     inside = lambda place: jnp.logical_and(place >= 0, place < bands)
-    info = jnp.stack([
-        step_one, step_two, inside(band + step_one), inside(band - step_one),
-        band & 1, (band & 2) // 2, inside(band + step_two), inside(band - step_two),
-    ])
+    info = jnp.stack([step_one, step_two, inside(band + step_one), inside(band - step_one)])
 
     src_rows = call(
         src_kernel, shape((2 * edges, latent), BF16), grid_latent, mate_pack, src_pick, cost=0,

time: 110 us -> 100 us (0.909)
  the two profiles are of different devices: /device:TPU:1 before, /device:TPU:201 now
where the time goes in v7:
time: 100 us; the launch traced here: 99.6 us
  starting transfers between devices  46.2 us (46%)
  waiting for transfers between devices  29.7 us (30%)
  Pallas kernels  16.8 us (17%)
  blocking collectives  3.07 us (3%)
  local copies, waits for them, and re-layouts  2.11 us (2%)
  between operations  1 us (1%)
    all_to_all x3, waiting for transfers between devices, exchange(): lax.all_to_all(values.reshape(chips, -1, latent), 'feat', split_axis=0, c...  28.7 us
    all_to_all x3, starting transfers between devices, exchange(): lax.all_to_all(values.reshape(chips, -1, latent), 'feat', split_axis=0, c...  20.8 us
    ppermute x4, starting transfers between devices, meet(): return lax.ppermute(values, 'band', pairs)  18.9 us
    pallas_call x10, Pallas kernels, call(): pl.pallas_call(body, out_shape=outs[0] if single else outs, in_specs=[pl....  16.8 us
    ppermute x1, starting transfers between devices, swap(): return lax.ppermute(values, 'feat', [(i, i ^ 1) for i in range(feats)])  6.51 us
    all_gather x1, blocking collectives, per_device(): lax.all_gather(pack, 'feat', axis=0, tiled=True, axis_index_groups=[[i, i...  3.07 us
    unnamed x30, local copies, waits for them, and re-layouts  2.08 us
  transfers between devices with their start and end apart: 8, of which 4 were waited for; matrix products, arithmetic and copies ran while one was open for 1% of the time, Pallas kernels for 5%

profile of v7, /device:TPU:201, one launch (start us, length us, event | category | flops | bytes accessed | tf_op | source)
XLA Modules:
  0.0 99.6 jit_solution(13354069246118876867)
XLA Ops:
  0.6 1.4 %shard_map.195 = bf16[256,512]{1,0:T(8,128)(2,1)} custom-call(bf16[8,512]{1,0:T(8,128)(2,1)} %mesh_ref.3), custom_call_target="tpu_custom_call" | custom-call | flops 4000000000 | bytes 4194304 | tf_op jit(solution)/shard_map/pallas_call | solution.py:62
  2.1 9.6 %all-to-all-start = ((bf16[32,8,512]{2,1,0:T(8,128)(2,1)}), bf16[32,8,512]{2,1,0:T(8,128)(2,1)S(1)}, u32[]{:S(2)}, u32[]{:S(2)}) async-start(bf16[32,8,512]{2,1,0:T(8,128)(2,1)} %bitcast.9), calls=%async_computation | async-start | bytes 524288 | tf_op jit(solution)/shard_map/all_to_all | solution.py:333
  11.7 1.1 %shard_map.193 = (bf16[272,512]{1,0:T(8,128)(2,1)S(1)}, bf16[16,512]{1,0:T(8,128)(2,1)S(1)}) custom-call(bf16[256,512]{1,0:T(8,128)(2,1)} %own_ref.1, bf16[8,512]{1,0:T(8,128)(2,1)} %cotangent_ref.1, s32[1,512]{1,0:T(1,128)} %bitcast.31, s32[1,512]{1,0:T(1,128)} %bitcast.28, s32[1,512]{1,0:T(1,128)} %bitcast.30, s32[1,256]{1,0:T(1,128)} %bitcast.35, ...), custom_call_target="tpu_custom_call" | custom-call | tf_op jit(solution)/shard_map/pallas_call | solution.py:62
  12.8 3.1 %all_gather.3 = bf16[544,512]{1,0:T(8,128)(2,1)S(1)} all-gather(bf16[272,512]{1,0:T(8,128)(2,1)S(1)} %get-tuple-element.16), channel_id=1, replica_groups={{0,1},{2,3},{4,5},{6,7},{8,9},{10,11},{12,13},{14,15},{16,17},{18,19},{..., dimensions={0}, use_global_device_ids=true | all-gather | bytes 835584 | tf_op jit(solution)/shard_map/all_gather | solution.py:371
  15.9 0.0 copy-start.14
  16.0 0.7 copy-done.14
  16.6 0.2 fusion.pick_ref
  16.9 0.0 copy-start.13
  16.9 0.0 copy-start.12
  16.9 0.7 copy-done.13
  17.5 0.0 copy-done.12
  17.6 0.0 copy-done
  17.6 0.4 shard_map.194.rows_ref
  18.0 0.0 copy-start.4
  18.0 0.0 copy-start.6
  18.1 0.2 fusion.1.dst_ref
  18.3 0.1 fusion.2.dst_t_ref
  18.4 0.0 copy-start.8
  18.4 4.9 %all-to-all-done = bf16[32,8,512]{2,1,0:T(8,128)(2,1)S(1)} async-done(((bf16[32,8,512]{2,1,0:T(8,128)(2,1)}), bf16[32,8,512]{2,1,0:T(8,128)(2,1)S(1)}, u32[]{:S(2)}, u32[]{:S(2)}) %all-to-all-start) | async-done | bytes 262176 | tf_op jit(solution)/shard_map/all_to_all | solution.py:333
  23.3 3.4 %shard_map.196 = (bf16[32,16,512]{2,1,0:T(8,128)(2,1)}, bf16[1024,512]{1,0:T(8,128)(2,1)}) custom-call(bf16[1024,512]{1,0:T(8,128)(2,1)S(1)} %shard_map.194.rows_ref, bf16[1024,256]{1,0:T(8,128)(2,1)S(1)} %fusion.1.dst_ref, bf16[256,1024]{1,0:T(8,128)(2,1)S(1)} %fusion.2.dst_t_ref, bf16[256,512]{1,0:T(8,128)(2,1)S(1)} %bitcast.21, ...), custom_call_target="tpu_custom_call" | custom-call | flops 4000000000 | bytes 4194304 | tf_op jit(solution)/shard_map/pallas_call | solution.py:62
  26.7 0.0 copy-start.5
  26.7 5.3 %all-to-all-start.1 = ((bf16[32,16,512]{2,1,0:T(8,128)(2,1)}), bf16[32,16,512]{2,1,0:T(8,128)(2,1)S(1)}, u32[]{:S(2)}, u32[]{:S(2)}) async-start(bf16[32,16,512]{2,1,0:T(8,128)(2,1)} %get-tuple-element.17), calls=%async_computation.1 | async-start | bytes 1048576 | tf_op jit(solution)/shard_map/all_to_all | solution.py:333
  32.1 0.0 copy-start.7
  32.1 0.0 copy-start.9
  32.1 15.8 %all-to-all-done.1.parts_ref = bf16[32,16,512]{2,1,0:T(8,128)(2,1)S(1)} async-done(((bf16[32,16,512]{2,1,0:T(8,128)(2,1)}), bf16[32,16,512]{2,1,0:T(8,128)(2,1)S(1)}, u32[]{:S(2)}, u32[]{:S(2)}) %all-to-all-start.1) | async-done | bytes 524320 | tf_op jit(solution)/shard_map/all_to_all | solution.py:333
  47.9 0.0 copy-start.1
  47.9 0.0 copy-start.2
  47.9 0.0 copy-start.3
  47.9 0.0 copy-start.11
  48.0 0.4 shard_map.197
  48.4 2.0 %collective-permute-start = (bf16[24,512]{1,0:T(8,128)(2,1)S(1)}, bf16[24,512]{1,0:T(8,128)(2,1)S(1)}, u32[]{:S(2)}, u32[]{:S(2)}) collective-permute-start(bf16[24,512]{1,0:T(8,128)(2,1)S(1)} %get-tuple-element.19.own_ref), channel_id=1, source_target_pairs={{0,64},{64,0},{128,192},{192,128},{256,320},{320,256},{384,448},{4... | collective-permute-start | bytes 73736 | tf_op jit(solution)/shard_map/ppermute | solution.py:350
  50.4 7.3 %collective-permute-start.1 = (bf16[24,512]{1,0:T(8,128)(2,1)S(1)}, bf16[24,512]{1,0:T(8,128)(2,1)S(1)}, u32[]{:S(2)}, u32[]{:S(2)}) collective-permute-start(bf16[24,512]{1,0:T(8,128)(2,1)S(1)} %get-tuple-element.19.own_ref), channel_id=1, source_target_pairs={{64,128},{128,64},{192,256},{256,192},{320,384},{384,320},{448,512... | collective-permute-start | bytes 73736 | tf_op jit(solution)/shard_map/ppermute | solution.py:350
  57.7 1.9 %collective-permute-start.2 = (bf16[8,512]{1,0:T(8,128)(2,1)S(1)}, bf16[8,512]{1,0:T(8,128)(2,1)S(1)}, u32[]{:S(2)}, u32[]{:S(2)}) collective-permute-start(bf16[8,512]{1,0:T(8,128)(2,1)S(1)} %get-tuple-element.20), channel_id=1, source_target_pairs={{0,128},{64,192},{128,0},{192,64},{256,384},{320,448},{384,256},{4... | collective-permute-start | bytes 24584 | tf_op jit(solution)/shard_map/ppermute | solution.py:350
  59.6 7.6 %collective-permute-start.3 = (bf16[8,512]{1,0:T(8,128)(2,1)S(1)}, bf16[8,512]{1,0:T(8,128)(2,1)S(1)}, u32[]{:S(2)}, u32[]{:S(2)}) collective-permute-start(bf16[8,512]{1,0:T(8,128)(2,1)S(1)} %get-tuple-element.20), channel_id=1, source_target_pairs={{128,256},{256,128},{192,320},{320,192},{384,512},{512,384},{448,5... | collective-permute-start | bytes 24584 | tf_op jit(solution)/shard_map/ppermute | solution.py:350
  67.2 0.1 pad_add_fusion.2.info_ref
  67.3 0.9 collective-permute-done.3.four_ref
  68.3 0.0 collective-permute-done.one_ref
  68.3 0.6 copy-done.10
  69.0 3.7 %shard_map.198 = (bf16[8,512]{1,0:T(8,128)(2,1)}, f32[8,512]{1,0:T(8,128)S(1)}, bf16[256,512]{1,0:T(8,128)(2,1)}) custom-call(bf16[24,512]{1,0:T(8,128)(2,1)S(1)} %collective-permute-done.one_ref, bf16[24,512]{1,0:T(8,128)(2,1)S(1)} %collective-permute-done.1.two_ref, bf16[8,512]{1,0:T(8,128)(2,1)S(1)} %collective-permute-done.2.three_ref, ...), custom_call_target="tpu_custom_call" | custom-call | flops 4000000000 | bytes 4194304 | tf_op jit(solution)/shard_map/pallas_call | solution.py:62
  72.7 5.9 %all-to-all-start.2 = ((bf16[32,8,512]{2,1,0:T(8,128)(2,1)}), bf16[32,8,512]{2,1,0:T(8,128)(2,1)S(1)}, u32[]{:S(2)}, u32[]{:S(2)}) async-start(bf16[32,8,512]{2,1,0:T(8,128)(2,1)} %bitcast.19), calls=%async_computation.2 | async-start | bytes 524288 | tf_op jit(solution)/shard_map/all_to_all | solution.py:333
  78.6 0.1 fusion.3.pick_t_ref
  78.7 2.0 %shard_map.202 = bf16[8,512]{1,0:T(8,128)(2,1)} custom-call(bf16[256,512]{1,0:T(8,128)(2,1)} %get-tuple-element.23.tiled_ref, f32[8,512]{1,0:T(8,128)S(1)} %get-tuple-element.27.slopes_ref, f32[8,512]{1,0:T(8,128)S(1)} %get-tuple-element.28.grad_ref, bf16[512,512]{1,0:T(8,128)(2,1)S(1)} %copy-done.5, bf16[512,512]{1,0:T(8,128)(2,1)S(1)} %copy-done.4), custom_call_target="tpu_custom_call" | custom-call | flops 4000000000 | bytes 4194304 | tf_op jit(solution)/shard_map/pallas_call | solution.py:62
  80.7 8.0 %all-to-all-done.2 = bf16[32,8,512]{2,1,0:T(8,128)(2,1)S(1)} async-done(((bf16[32,8,512]{2,1,0:T(8,128)(2,1)}), bf16[32,8,512]{2,1,0:T(8,128)(2,1)S(1)}, u32[]{:S(2)}, u32[]{:S(2)}) %all-to-all-start.2) | async-done | bytes 262176 | tf_op jit(solution)/shard_map/all_to_all | solution.py:333
  88.7 1.7 %shard_map.199 = (bf16[512,512]{1,0:T(8,128)(2,1)S(1)}, bf16[256,512]{1,0:T(8,128)(2,1)S(1)}) custom-call(bf16[256,512]{1,0:T(8,128)(2,1)S(1)} %bitcast.22, bf16[1024,256]{1,0:T(8,128)(2,1)S(1)} %fusion.1.dst_ref, bf16[256,1024]{1,0:T(8,128)(2,1)S(1)} %fusion.3.pick_t_ref, bf16[1024,512]{1,0:T(8,128)(2,1)} %get-tuple-element.24.slope_ref, ...), custom_call_target="tpu_custom_call" | custom-call | flops 4000000000 | bytes 4194304 | tf_op jit(solution)/shard_map/pallas_call | solution.py:62
  90.5 6.5 %collective-permute-start.4 = (bf16[256,512]{1,0:T(8,128)(2,1)S(1)}, bf16[256,512]{1,0:T(8,128)(2,1)S(1)}, u32[]{:S(2)}, u32[]{:S(2)}) collective-permute-start(bf16[256,512]{1,0:T(8,128)(2,1)S(1)} %get-tuple-element.26), channel_id=1, source_target_pairs={{0,1},{1,0},{2,3},{3,2},{4,5},{5,4},{6,7},{7,6},{8,9},{9,8},{10,11... | collective-permute-start | bytes 786440 | tf_op jit(solution)/shard_map/ppermute | solution.py:339
  97.0 1.8 %shard_map.200.own_ref = f32[256,512]{1,0:T(8,128)S(1)} custom-call(bf16[512,512]{1,0:T(8,128)(2,1)S(1)} %get-tuple-element.25.table_ref, bf16[1024,256]{1,0:T(8,128)(2,1)S(1)} %fusion.1.dst_ref, bf16[256,1024]{1,0:T(8,128)(2,1)S(1)} %fusion.3.pick_t_ref, bf16[1024,512]{1,0:T(8,128)(2,1)} %get-tuple-element.24.slope_ref, bf16[512,512]{1,0:T(8,128)(2,1)S(1)} %copy-done.6), custom_call_target="tpu_custom_call" | custom-call | flops 4000000000 | bytes 4194304 | tf_op jit(solution)/shard_map/pallas_call | solution.py:62
  98.8 0.0 collective-permute-done.4.mate_ref
  98.8 0.7 shard_map.201
  (19 shorter events, 0.1 us)
Async XLA Ops:
  2.1 21.2 %all-to-all-start = ((bf16[32,8,512]{2,1,0:T(8,128)(2,1)}), bf16[32,8,512]{2,1,0:T(8,128)(2,1)S(1)}, u32[]{:S(2)}, u32[]{:S(2)}) async-start(bf16[32,8,512]{2,1,0:T(8,128)(2,1)} %bitcast.9), calls=%async_computation | async-start | bytes 524288 | tf_op jit(solution)/shard_map/all_to_all | solution.py:333
  15.9 0.7 copy-start.14
  16.6 0.9 copy-start
  16.9 0.7 copy-start.13
  16.9 0.7 copy-start.12
  18.0 5.3 %copy-start.4 = (bf16[512,512]{1,0:T(8,128)(2,1)S(1)}, bf16[512,512]{1,0:T(8,128)(2,1)}, u32[]{:S(2)}) copy-start(bf16[512,512]{1,0:T(8,128)(2,1)} %dst_w_ref.5) | copy-start | bytes 1572868
  18.0 5.2 %copy-start.6 = (bf16[512,512]{1,0:T(8,128)(2,1)S(1)}, bf16[512,512]{1,0:T(8,128)(2,1)}, u32[]{:S(2)}) copy-start(bf16[512,512]{1,0:T(8,128)(2,1)} %src_w_ref.7) | copy-start | bytes 1572868
  18.4 4.9 %copy-start.8 = (f32[512]{0:T(512)S(1)}, f32[512]{0:T(512)}, u32[]{:S(2)}) copy-start(f32[512]{0:T(512)} %param.28) | copy-start | bytes 6148
  26.7 21.2 %copy-start.5 = (bf16[512,512]{1,0:T(8,128)(2,1)S(1)}, bf16[512,512]{1,0:T(8,128)(2,1)}, u32[]{:S(2)}) copy-start(bf16[512,512]{1,0:T(8,128)(2,1)} %out_w_ref.5) | copy-start | bytes 1572868
  26.7 21.2 %all-to-all-start.1 = ((bf16[32,16,512]{2,1,0:T(8,128)(2,1)}), bf16[32,16,512]{2,1,0:T(8,128)(2,1)S(1)}, u32[]{:S(2)}, u32[]{:S(2)}) async-start(bf16[32,16,512]{2,1,0:T(8,128)(2,1)} %get-tuple-element.17), calls=%async_computation.1 | async-start | bytes 1048576 | tf_op jit(solution)/shard_map/all_to_all | solution.py:333
  32.1 15.8 %copy-start.7 = (bf16[8,512]{1,0:T(8,128)(2,1)S(1)}, bf16[8,512]{1,0:T(8,128)(2,1)}, u32[]{:S(2)}) copy-start(bf16[8,512]{1,0:T(8,128)(2,1)} %mesh_ref.3) | copy-start | bytes 24580
  32.1 15.8 %copy-start.9 = (f32[512]{0:T(512)S(1)}, f32[512]{0:T(512)}, u32[]{:S(2)}) copy-start(f32[512]{0:T(512)} %param.29) | copy-start | bytes 6148
  47.9 20.4 %copy-start.1 = (bf16[512,512]{1,0:T(8,128)(2,1)S(1)}, bf16[512,512]{1,0:T(8,128)(2,1)}, u32[]{:S(2)}) copy-start(bf16[512,512]{1,0:T(8,128)(2,1)} %src_w_ref.5) | copy-start | bytes 1572868
  47.9 20.4 %copy-start.2 = (bf16[512,512]{1,0:T(8,128)(2,1)S(1)}, bf16[512,512]{1,0:T(8,128)(2,1)}, u32[]{:S(2)}) copy-start(bf16[512,512]{1,0:T(8,128)(2,1)} %dst_w_ref.4) | copy-start | bytes 1572868
  47.9 20.4 %copy-start.3 = (bf16[512,512]{1,0:T(8,128)(2,1)S(1)}, bf16[512,512]{1,0:T(8,128)(2,1)}, u32[]{:S(2)}) copy-start(bf16[512,512]{1,0:T(8,128)(2,1)} %out_w_ref.3) | copy-start | bytes 1572868
  47.9 20.4 %copy-start.11 = (f32[512]{0:T(512)S(1)}, f32[512]{0:T(512)}, u32[]{:S(2)}) copy-start(f32[512]{0:T(512)} %param.34) | copy-start | bytes 6148
  48.4 19.9 %collective-permute-start = (bf16[24,512]{1,0:T(8,128)(2,1)S(1)}, bf16[24,512]{1,0:T(8,128)(2,1)S(1)}, u32[]{:S(2)}, u32[]{:S(2)}) collective-permute-start(bf16[24,512]{1,0:T(8,128)(2,1)S(1)} %get-tuple-element.19.own_ref), channel_id=1, source_target_pairs={{0,64},{64,0},{128,192},{192,128},{256,320},{320,256},{384,448},{4... | collective-permute-start | bytes 73736 | tf_op jit(solution)/shard_map/ppermute | solution.py:350
  50.4 17.9 %collective-permute-start.1 = (bf16[24,512]{1,0:T(8,128)(2,1)S(1)}, bf16[24,512]{1,0:T(8,128)(2,1)S(1)}, u32[]{:S(2)}, u32[]{:S(2)}) collective-permute-start(bf16[24,512]{1,0:T(8,128)(2,1)S(1)} %get-tuple-element.19.own_ref), channel_id=1, source_target_pairs={{64,128},{128,64},{192,256},{256,192},{320,384},{384,320},{448,512... | collective-permute-start | bytes 73736 | tf_op jit(solution)/shard_map/ppermute | solution.py:350
  57.7 9.6 %collective-permute-start.2 = (bf16[8,512]{1,0:T(8,128)(2,1)S(1)}, bf16[8,512]{1,0:T(8,128)(2,1)S(1)}, u32[]{:S(2)}, u32[]{:S(2)}) collective-permute-start(bf16[8,512]{1,0:T(8,128)(2,1)S(1)} %get-tuple-element.20), channel_id=1, source_target_pairs={{0,128},{64,192},{128,0},{192,64},{256,384},{320,448},{384,256},{4... | collective-permute-start | bytes 24584 | tf_op jit(solution)/shard_map/ppermute | solution.py:350
  59.6 8.6 %collective-permute-start.3 = (bf16[8,512]{1,0:T(8,128)(2,1)S(1)}, bf16[8,512]{1,0:T(8,128)(2,1)S(1)}, u32[]{:S(2)}, u32[]{:S(2)}) collective-permute-start(bf16[8,512]{1,0:T(8,128)(2,1)S(1)} %get-tuple-element.20), channel_id=1, source_target_pairs={{128,256},{256,128},{192,320},{320,192},{384,512},{512,384},{448,5... | collective-permute-start | bytes 24584 | tf_op jit(solution)/shard_map/ppermute | solution.py:350
  68.3 0.7 copy-start.10
  72.7 16.0 %all-to-all-start.2 = ((bf16[32,8,512]{2,1,0:T(8,128)(2,1)}), bf16[32,8,512]{2,1,0:T(8,128)(2,1)S(1)}, u32[]{:S(2)}, u32[]{:S(2)}) async-start(bf16[32,8,512]{2,1,0:T(8,128)(2,1)} %bitcast.19), calls=%async_computation.2 | async-start | bytes 524288 | tf_op jit(solution)/shard_map/all_to_all | solution.py:333
  90.5 8.3 %collective-permute-start.4 = (bf16[256,512]{1,0:T(8,128)(2,1)S(1)}, bf16[256,512]{1,0:T(8,128)(2,1)S(1)}, u32[]{:S(2)}, u32[]{:S(2)}) collective-permute-start(bf16[256,512]{1,0:T(8,128)(2,1)S(1)} %get-tuple-element.26), channel_id=1, source_target_pairs={{0,1},{1,0},{2,3},{3,2},{4,5},{5,4},{6,7},{7,6},{8,9},{9,8},{10,11... | collective-permute-start | bytes 786440 | tf_op jit(solution)/shard_map/ppermute | solution.py:339

commit v8 on v7

--- a/solution.py
+++ b/solution.py
@@ -180,7 +180,7 @@
 
 
 def mid_kernel(
-    parts_ref, weight_ref, gain_ref, mesh_ref, near_ref, mid_ref, packet_ref, agg_ref, slopes_ref
+    parts_ref, weight_ref, gain_ref, mesh_ref, near_ref, packet_ref, agg_ref, slopes_ref
 ):
     count = mesh_ref.shape[0]
     summed = jnp.sum(parts_ref[...].astype(F32), axis=0)
@@ -188,7 +188,6 @@
     slopes_ref[...] = summed[count:]
     agg_ref[...] = agg
     mid = mesh_ref[...].astype(F32) + layer_norm(agg, gain_ref[...])[0]
-    mid_ref[...] = mid.astype(BF16)
     packet_ref[...] = jnp.concatenate([mid, near_ref[...].astype(F32)], axis=0).astype(BF16)
 
 
@@ -212,11 +211,18 @@
 
 
 def proc_kernel(
-    one_ref, two_ref, three_ref, four_ref, own_ref, info_ref, src_w_ref, dst_w_ref, out_w_ref,
+    halo_ref, own_ref, info_ref, src_w_ref, dst_w_ref, out_w_ref,
     bias_ref, gain_ref, enc_agg_ref, enc_gain_ref, out_ref, grad_ref, tiled_ref,
 ):
     count = out_ref.shape[0]
-    packets = [ref[...].astype(F32) for ref in (one_ref, two_ref, own_ref)]
+    own = own_ref[...].astype(F32)
+    halo = halo_ref[...].astype(F32)
+    size = own.shape[0]
+    met = [
+        jnp.where(info_ref[4] == 0, halo[start : start + size], halo[start + size : start + 2 * size])
+        for start in range(0, 8 * size, 2 * size)
+    ]
+    packets = [met[0], met[1], own]
     one, two, mid = (packet[:count] for packet in packets)
     upstreams = jnp.concatenate([packet[count : 2 * count] for packet in packets], axis=0)
     index = [packet[2 * count : 2 * count + 1].astype(jnp.int32) for packet in packets]
@@ -232,7 +238,7 @@
     pick_t = chosen.astype(BF16)
     pick = jnp.concatenate([chosen] * 2, axis=0).astype(BF16)
 
-    rows = [one, two, three_ref[...].astype(F32), four_ref[...].astype(F32), mid]
+    rows = [one, two, met[2][:count], met[3][:count], mid]
     senders = jnp.concatenate(rows, axis=0).astype(BF16)
     receivers = jnp.concatenate([one, two, mid], axis=0).astype(BF16)
     table = jnp.concatenate(
@@ -346,8 +352,19 @@
         for pair in ((i, i + step), (i + step, i))
     ]
 
-    def meet(values, pairs):
-        return lax.ppermute(values, "band", pairs)
+    def meet(values, *sides):
+        pairs = [
+            (source * feats + feat, target * feats + feat)
+            for feat in range(feats)
+            for source, target in sides[feat % 2]
+        ]
+        return lax.ppermute(values, ("band", "feat"), pairs)
+
+    def both_cores(values):
+        return lax.all_gather(
+            values, "feat", axis=0, tiled=True,
+            axis_index_groups=[[i, i + 1] for i in range(0, feats, 2)],
+        )
 
     line = lambda index: index.reshape(1, edges)
 
@@ -368,9 +385,7 @@
             sem(7),
         ),
     )
-    packs = lax.all_gather(
-        pack, "feat", axis=0, tiled=True, axis_index_groups=[[i, i + 1] for i in range(0, feats, 2)]
-    )
+    packs = both_cores(pack)
     mate_pack = lax.dynamic_slice_in_dim(packs, (1 - core) * pack.shape[0], pack.shape[0])
     mesh_all = exchange(tiled_mesh).reshape(plane_nodes, latent)
 
@@ -388,7 +403,7 @@
     step_one = jnp.where(band & 1 == 0, 1, -1)
     step_two = jnp.where(band & 2 == 0, 2, -2)
     inside = lambda place: jnp.logical_and(place >= 0, place < bands)
-    info = jnp.stack([step_one, step_two, inside(band + step_one), inside(band - step_one)])
+    info = jnp.stack([step_one, step_two, inside(band + step_one), inside(band - step_one), core])
 
     src_rows = call(
         src_kernel, shape((2 * edges, latent), BF16), grid_latent, mate_pack, src_pick, cost=0,
@@ -400,15 +415,24 @@
         far_out=(1,),
         scratch=(pltpu.VMEM((2 * edges, 2 * latent), BF16), edge_buf(2 * edges, BF16), sem(4)),
     )
-    mid, packet, enc_agg, slopes = call(
+    packet, enc_agg, slopes = call(
         mid_kernel,
         (
-            shape((nodes, latent), BF16),
             shape((3 * nodes, latent), BF16),
             shape((nodes, latent), F32),
             shape((nodes, latent), F32),
         ),
         exchange(partial), enc_out_w, row(enc_gain), mesh_latent, near,
+    )
+    packets = both_cores(packet)
+    halo = both_cores(
+        jnp.concatenate(
+            [
+                meet(packets, near_side(1), near_side(2)),
+                meet(packets, far_side(1), far_side(2)),
+            ],
+            axis=0,
+        )
     )
     mesh_out, grad_mid, tiled = call(
         proc_kernel,
@@ -417,11 +441,9 @@
             shape((nodes, latent), F32),
             shape((plane_nodes, latent), BF16),
         ),
-        meet(packet, near_side(1)), meet(packet, far_side(1)),
-        meet(mid, near_side(2)), meet(mid, far_side(2)),
-        packet, info.astype(jnp.int32), proc_src_w, proc_dst_w, proc_out_w, row(proc_bias),
+        halo, packet, info.astype(jnp.int32), proc_src_w, proc_dst_w, proc_out_w, row(proc_bias),
         row(proc_gain), enc_agg, row(enc_gain),
-        small=(5,),
+        small=(2,),
     )
     grad_all = exchange(tiled).reshape(plane_nodes, latent)
     grad_mesh = call(

time: 100 us -> 99.1 us (level)
  the two profiles are of different devices: /device:TPU:201 before, /device:TPU:137 now
where the time goes in v8:
time: 99.1 us; the launch traced here: 98.3 us
  blocking collectives  30.5 us (31%)
  starting transfers between devices  30.1 us (30%)
  waiting for transfers between devices  16.2 us (16%)
  Pallas kernels  16 us (16%)
  local copies, waits for them, and re-layouts  3.92 us (4%)
    all_to_all x1, blocking collectives, exchange(): lax.all_to_all(values.reshape(chips, -1, latent), 'feat', split_axis=0, c...  20.6 us
    pallas_call x10, Pallas kernels, call(): pl.pallas_call(body, out_shape=outs[0] if single else outs, in_specs=[pl....  16 us
    all_to_all x2, waiting for transfers between devices, exchange(): lax.all_to_all(values.reshape(chips, -1, latent), 'feat', split_axis=0, c...  14.9 us
    all_to_all x2, starting transfers between devices, exchange(): lax.all_to_all(values.reshape(chips, -1, latent), 'feat', split_axis=0, c...  14 us
    ppermute x2, starting transfers between devices, meet(): return lax.ppermute(values, ('band', 'feat'), pairs)  12.8 us
    all_gather x3, blocking collectives, both_cores(): lax.all_gather(values, 'feat', axis=0, tiled=True, axis_index_groups=[[i,...  9.88 us
    unnamed x34, local copies, waits for them, and re-layouts  3.81 us
    ppermute x1, starting transfers between devices, swap(): return lax.ppermute(values, 'feat', [(i, i ^ 1) for i in range(feats)])  3.28 us
  transfers between devices with their start and end apart: 5, of which 3 were waited for; matrix products, arithmetic and copies ran while one was open for 1% of the time, Pallas kernels for 5%

profile of v8, /device:TPU:137, one launch (start us, length us, event | category | flops | bytes accessed | tf_op | source)
XLA Modules:
  0.0 98.3 jit_solution(3513114064805728551)
XLA Ops:
  0.6 1.4 %shard_map.195 = bf16[256,512]{1,0:T(8,128)(2,1)} custom-call(bf16[8,512]{1,0:T(8,128)(2,1)} %mesh_ref.3), custom_call_target="tpu_custom_call" | custom-call | flops 4000000000 | bytes 4194304 | tf_op jit(solution)/shard_map/pallas_call | solution.py:62
  2.1 9.6 %all-to-all-start = ((bf16[32,8,512]{2,1,0:T(8,128)(2,1)}), bf16[32,8,512]{2,1,0:T(8,128)(2,1)S(1)}, u32[]{:S(2)}, u32[]{:S(2)}) async-start(bf16[32,8,512]{2,1,0:T(8,128)(2,1)} %bitcast.9), calls=%async_computation | async-start | bytes 524288 | tf_op jit(solution)/shard_map/all_to_all | solution.py:339
  11.7 1.1 %shard_map.193 = (bf16[272,512]{1,0:T(8,128)(2,1)S(1)}, bf16[16,512]{1,0:T(8,128)(2,1)S(1)}) custom-call(bf16[256,512]{1,0:T(8,128)(2,1)} %own_ref.1, bf16[8,512]{1,0:T(8,128)(2,1)} %cotangent_ref.1, s32[1,512]{1,0:T(1,128)} %bitcast.32, s32[1,512]{1,0:T(1,128)} %bitcast.29, s32[1,512]{1,0:T(1,128)} %bitcast.31, s32[1,256]{1,0:T(1,128)} %bitcast.36, ...), custom_call_target="tpu_custom_call" | custom-call | tf_op jit(solution)/shard_map/pallas_call | solution.py:62
  12.8 3.1 %all_gather.9 = bf16[544,512]{1,0:T(8,128)(2,1)S(1)} all-gather(bf16[272,512]{1,0:T(8,128)(2,1)S(1)} %get-tuple-element.15), channel_id=1, replica_groups={{0,1},{2,3},{4,5},{6,7},{8,9},{10,11},{12,13},{14,15},{16,17},{18,19},{..., dimensions={0}, use_global_device_ids=true | all-gather | bytes 835584 | tf_op jit(solution)/shard_map/all_gather | solution.py:364
  15.9 0.0 copy-start.16
  16.0 0.7 copy-done.16
  16.6 0.2 fusion.pick_ref
  16.9 0.0 copy-start.15
  16.9 0.0 copy-start.14
  16.9 0.7 copy-done.15
  17.5 0.0 copy-done.14
  17.6 0.0 copy-done
  17.6 0.4 shard_map.194.rows_ref
  18.0 0.0 copy-start.4
  18.0 0.2 fusion.1.dst_ref
  18.3 0.1 fusion.2.dst_t_ref
  18.4 0.0 copy-start.10
  18.4 4.9 %all-to-all-done = bf16[32,8,512]{2,1,0:T(8,128)(2,1)S(1)} async-done(((bf16[32,8,512]{2,1,0:T(8,128)(2,1)}), bf16[32,8,512]{2,1,0:T(8,128)(2,1)S(1)}, u32[]{:S(2)}, u32[]{:S(2)}) %all-to-all-start) | async-done | bytes 262176 | tf_op jit(solution)/shard_map/all_to_all | solution.py:339
  23.3 1.0 %copy-done.7 = bf16[512,512]{1,0:T(8,128)(2,1)S(1)} copy-done((bf16[512,512]{1,0:T(8,128)(2,1)S(1)}, bf16[512,512]{1,0:T(8,128)(2,1)}, u32[]{:S(2)}) %copy-start.7) | copy-done | bytes 524312
  24.3 2.6 %shard_map.196 = (bf16[32,16,512]{2,1,0:T(8,128)(2,1)S(1)}, bf16[1024,512]{1,0:T(8,128)(2,1)}) custom-call(bf16[1024,512]{1,0:T(8,128)(2,1)S(1)} %shard_map.194.rows_ref, bf16[1024,256]{1,0:T(8,128)(2,1)S(1)} %fusion.1.dst_ref, bf16[256,1024]{1,0:T(8,128)(2,1)S(1)} %fusion.2.dst_t_ref, bf16[256,512]{1,0:T(8,128)(2,1)S(1)} %bitcast.22, ...), custom_call_target="tpu_custom_call" | custom-call | flops 4000000000 | bytes 4194304 | tf_op jit(solution)/shard_map/pallas_call | solution.py:62
  26.9 0.0 copy-start.5
  26.9 0.0 copy-start.9
  27.0 20.6 %all_to_all.15.parts_ref = bf16[32,16,512]{2,1,0:T(8,128)(2,1)S(1)} all-to-all(bf16[32,16,512]{2,1,0:T(8,128)(2,1)S(1)} %get-tuple-element.16), channel_id=1, replica_groups={{0,2,4,6,8,10,12,14,16,18,20,22,24,26,28,30,32,34,36,38,40,42,44,46,48,..., dimensions={0} | all-to-all | bytes 1048576 | tf_op jit(solution)/shard_map/all_to_all | solution.py:339
  47.5 0.0 copy-done.9
  47.5 0.7 copy-done.11
  48.2 0.4 shard_map.197
  48.6 4.9 %all_gather.10 = bf16[48,512]{1,0:T(8,128)(2,1)S(1)} all-gather(bf16[24,512]{1,0:T(8,128)(2,1)S(1)} %get-tuple-element.18.own_ref), channel_id=1, replica_groups={{0,1},{2,3},{4,5},{6,7},{8,9},{10,11},{12,13},{14,15},{16,17},{18,19},{..., dimensions={0}, use_global_device_ids=true | all-gather | bytes 73728 | tf_op jit(solution)/shard_map/all_gather | solution.py:364
  53.5 3.3 %collective-permute-start = (bf16[48,512]{1,0:T(8,128)(2,1)S(1)}, bf16[48,512]{1,0:T(8,128)(2,1)S(1)}, u32[]{:S(2)}, u32[]{:S(2)}) collective-permute-start(bf16[48,512]{1,0:T(8,128)(2,1)S(1)} %all_gather.10), channel_id=1, source_target_pairs={{0,64},{64,0},{128,192},{192,128},{256,320},{320,256},{384,448},{4... | collective-permute-start | bytes 147464 | tf_op jit(solution)/shard_map/ppermute | solution.py:361
  56.8 9.5 %collective-permute-start.1 = (bf16[48,512]{1,0:T(8,128)(2,1)S(1)}, bf16[48,512]{1,0:T(8,128)(2,1)S(1)}, u32[]{:S(2)}, u32[]{:S(2)}) collective-permute-start(bf16[48,512]{1,0:T(8,128)(2,1)S(1)} %all_gather.10), channel_id=1, source_target_pairs={{64,128},{128,64},{192,256},{256,192},{320,384},{384,320},{448,512... | collective-permute-start | bytes 147464 | tf_op jit(solution)/shard_map/ppermute | solution.py:361
  66.3 0.0 copy-start.13
  66.4 0.1 stack.31.info_ref
  66.4 0.0 collective-permute-done
  66.4 1.3 %collective-permute-done.1 = bf16[48,512]{1,0:T(8,128)(2,1)S(1)} collective-permute-done((bf16[48,512]{1,0:T(8,128)(2,1)S(1)}, bf16[48,512]{1,0:T(8,128)(2,1)S(1)}, u32[]{:S(2)}, u32[]{:S(2)}) %collective-permute-start.1) | collective-permute-done | bytes 49184 | tf_op jit(solution)/shard_map/ppermute | solution.py:361
  67.8 1.9 %all_gather.11.halo_ref = bf16[192,512]{1,0:T(8,128)(2,1)S(1)} all-gather(bf16[96,512]{1,0:T(8,128)(2,1)S(1)} %pad_maximum_fusion), channel_id=1, replica_groups={{0,1},{2,3},{4,5},{6,7},{8,9},{10,11},{12,13},{14,15},{16,17},{18,19},{..., dimensions={0}, use_global_device_ids=true | all-gather | bytes 294912 | tf_op jit(solution)/shard_map/all_gather | solution.py:364
  69.7 0.0 copy-done.3
  69.8 0.0 copy-done.13
  69.8 0.7 copy-done.12
  70.4 3.7 %shard_map.198 = (bf16[8,512]{1,0:T(8,128)(2,1)}, f32[8,512]{1,0:T(8,128)S(1)}, bf16[256,512]{1,0:T(8,128)(2,1)}) custom-call(bf16[192,512]{1,0:T(8,128)(2,1)S(1)} %all_gather.11.halo_ref, bf16[24,512]{1,0:T(8,128)(2,1)S(1)} %get-tuple-element.18.own_ref, s32[5]{0:T(128)S(1)} %stack.31.info_ref, bf16[512,512]{1,0:T(8,128)(2,1)S(1)} %copy-done.1, ...), custom_call_target="tpu_custom_call" | custom-call | flops 4000000000 | bytes 4194304 | tf_op jit(solution)/shard_map/pallas_call | solution.py:62
  74.2 4.4 %all-to-all-start.2 = ((bf16[32,8,512]{2,1,0:T(8,128)(2,1)}), bf16[32,8,512]{2,1,0:T(8,128)(2,1)S(1)}, u32[]{:S(2)}, u32[]{:S(2)}) async-start(bf16[32,8,512]{2,1,0:T(8,128)(2,1)} %bitcast.20), calls=%async_computation.2 | async-start | bytes 524288 | tf_op jit(solution)/shard_map/all_to_all | solution.py:339
  78.6 0.1 fusion.3.pick_t_ref
  78.7 0.0 copy-start.8
  78.7 2.0 %shard_map.202 = bf16[8,512]{1,0:T(8,128)(2,1)} custom-call(bf16[256,512]{1,0:T(8,128)(2,1)} %get-tuple-element.21.tiled_ref, f32[8,512]{1,0:T(8,128)S(1)} %get-tuple-element.25.slopes_ref, f32[8,512]{1,0:T(8,128)S(1)} %get-tuple-element.26.grad_ref, bf16[512,512]{1,0:T(8,128)(2,1)S(1)} %copy-done.6, bf16[512,512]{1,0:T(8,128)(2,1)S(1)} %copy-done.4), custom_call_target="tpu_custom_call" | custom-call | flops 4000000000 | bytes 4194304 | tf_op jit(solution)/shard_map/pallas_call | solution.py:62
  80.8 10.0 %all-to-all-done.2 = bf16[32,8,512]{2,1,0:T(8,128)(2,1)S(1)} async-done(((bf16[32,8,512]{2,1,0:T(8,128)(2,1)}), bf16[32,8,512]{2,1,0:T(8,128)(2,1)S(1)}, u32[]{:S(2)}, u32[]{:S(2)}) %all-to-all-start.2) | async-done | bytes 262176 | tf_op jit(solution)/shard_map/all_to_all | solution.py:339
  90.7 1.7 %shard_map.199 = (bf16[512,512]{1,0:T(8,128)(2,1)S(1)}, bf16[256,512]{1,0:T(8,128)(2,1)S(1)}) custom-call(bf16[256,512]{1,0:T(8,128)(2,1)S(1)} %bitcast.23, bf16[1024,256]{1,0:T(8,128)(2,1)S(1)} %fusion.1.dst_ref, bf16[256,1024]{1,0:T(8,128)(2,1)S(1)} %fusion.3.pick_t_ref, bf16[1024,512]{1,0:T(8,128)(2,1)} %get-tuple-element.22.slope_ref, ...), custom_call_target="tpu_custom_call" | custom-call | flops 4000000000 | bytes 4194304 | tf_op jit(solution)/shard_map/pallas_call | solution.py:62
  92.5 3.3 %collective-permute-start.2 = (bf16[256,512]{1,0:T(8,128)(2,1)S(1)}, bf16[256,512]{1,0:T(8,128)(2,1)S(1)}, u32[]{:S(2)}, u32[]{:S(2)}) collective-permute-start(bf16[256,512]{1,0:T(8,128)(2,1)S(1)} %get-tuple-element.24), channel_id=1, source_target_pairs={{0,1},{1,0},{2,3},{3,2},{4,5},{5,4},{6,7},{7,6},{8,9},{9,8},{10,11... | collective-permute-start | bytes 786440 | tf_op jit(solution)/shard_map/ppermute | solution.py:345
  95.8 1.8 %shard_map.200.own_ref = f32[256,512]{1,0:T(8,128)S(1)} custom-call(bf16[512,512]{1,0:T(8,128)(2,1)S(1)} %get-tuple-element.23.table_ref, bf16[1024,256]{1,0:T(8,128)(2,1)S(1)} %fusion.1.dst_ref, bf16[256,1024]{1,0:T(8,128)(2,1)S(1)} %fusion.3.pick_t_ref, bf16[1024,512]{1,0:T(8,128)(2,1)} %get-tuple-element.22.slope_ref, bf16[512,512]{1,0:T(8,128)(2,1)S(1)} %copy-done.8), custom_call_target="tpu_custom_call" | custom-call | flops 4000000000 | bytes 4194304 | tf_op jit(solution)/shard_map/pallas_call | solution.py:62
  97.6 0.0 collective-permute-done.2.mate_ref
  97.6 0.7 shard_map.201
  (21 shorter events, 0.1 us)
Async XLA Ops:
  2.1 21.2 %all-to-all-start = ((bf16[32,8,512]{2,1,0:T(8,128)(2,1)}), bf16[32,8,512]{2,1,0:T(8,128)(2,1)S(1)}, u32[]{:S(2)}, u32[]{:S(2)}) async-start(bf16[32,8,512]{2,1,0:T(8,128)(2,1)} %bitcast.9), calls=%async_computation | async-start | bytes 524288 | tf_op jit(solution)/shard_map/all_to_all | solution.py:339
  15.9 0.7 copy-start.16
  16.6 0.9 copy-start
  16.9 0.7 copy-start.15
  16.9 0.7 copy-start.14
  18.0 5.3 %copy-start.4 = (bf16[512,512]{1,0:T(8,128)(2,1)S(1)}, bf16[512,512]{1,0:T(8,128)(2,1)}, u32[]{:S(2)}) copy-start(bf16[512,512]{1,0:T(8,128)(2,1)} %dst_w_ref.5) | copy-start | bytes 1572868
  18.4 4.9 %copy-start.10 = (f32[512]{0:T(512)S(1)}, f32[512]{0:T(512)}, u32[]{:S(2)}) copy-start(f32[512]{0:T(512)} %param.28) | copy-start | bytes 6148
  23.3 1.0 %copy-start.7 = (bf16[512,512]{1,0:T(8,128)(2,1)S(1)}, bf16[512,512]{1,0:T(8,128)(2,1)}, u32[]{:S(2)}) copy-start(bf16[512,512]{1,0:T(8,128)(2,1)} %src_w_ref.7) | copy-start | bytes 1572868
  26.9 20.6 %copy-start.5 = (bf16[512,512]{1,0:T(8,128)(2,1)S(1)}, bf16[512,512]{1,0:T(8,128)(2,1)}, u32[]{:S(2)}) copy-start(bf16[512,512]{1,0:T(8,128)(2,1)} %out_w_ref.5) | copy-start | bytes 1572868
  26.9 20.6 %copy-start.9 = (bf16[8,512]{1,0:T(8,128)(2,1)S(1)}, bf16[8,512]{1,0:T(8,128)(2,1)}, u32[]{:S(2)}) copy-start(bf16[8,512]{1,0:T(8,128)(2,1)} %mesh_ref.3) | copy-start | bytes 24580
  47.5 0.7 copy-start.11
  48.2 21.5 %copy-start.2 = (bf16[512,512]{1,0:T(8,128)(2,1)S(1)}, bf16[512,512]{1,0:T(8,128)(2,1)}, u32[]{:S(2)}) copy-start(bf16[512,512]{1,0:T(8,128)(2,1)} %dst_w_ref.4) | copy-start | bytes 1572868
  48.2 21.5 %copy-start.3 = (bf16[512,512]{1,0:T(8,128)(2,1)S(1)}, bf16[512,512]{1,0:T(8,128)(2,1)}, u32[]{:S(2)}) copy-start(bf16[512,512]{1,0:T(8,128)(2,1)} %out_w_ref.3) | copy-start | bytes 1572868
  48.6 21.1 %copy-start.1 = (bf16[512,512]{1,0:T(8,128)(2,1)S(1)}, bf16[512,512]{1,0:T(8,128)(2,1)}, u32[]{:S(2)}) copy-start(bf16[512,512]{1,0:T(8,128)(2,1)} %src_w_ref.5) | copy-start | bytes 1572868
  53.5 13.0 %collective-permute-start = (bf16[48,512]{1,0:T(8,128)(2,1)S(1)}, bf16[48,512]{1,0:T(8,128)(2,1)S(1)}, u32[]{:S(2)}, u32[]{:S(2)}) collective-permute-start(bf16[48,512]{1,0:T(8,128)(2,1)S(1)} %all_gather.10), channel_id=1, source_target_pairs={{0,64},{64,0},{128,192},{192,128},{256,320},{320,256},{384,448},{4... | collective-permute-start | bytes 147464 | tf_op jit(solution)/shard_map/ppermute | solution.py:361
  56.8 11.0 %collective-permute-start.1 = (bf16[48,512]{1,0:T(8,128)(2,1)S(1)}, bf16[48,512]{1,0:T(8,128)(2,1)S(1)}, u32[]{:S(2)}, u32[]{:S(2)}) collective-permute-start(bf16[48,512]{1,0:T(8,128)(2,1)S(1)} %all_gather.10), channel_id=1, source_target_pairs={{64,128},{128,64},{192,256},{256,192},{320,384},{384,320},{448,512... | collective-permute-start | bytes 147464 | tf_op jit(solution)/shard_map/ppermute | solution.py:361
  66.3 3.4 %copy-start.13 = (f32[512]{0:T(512)S(1)}, f32[512]{0:T(512)}, u32[]{:S(2)}) copy-start(f32[512]{0:T(512)} %param.34) | copy-start | bytes 6148
  69.7 0.7 copy-start.12
  74.2 4.5 %copy-start.6 = (bf16[512,512]{1,0:T(8,128)(2,1)S(1)}, bf16[512,512]{1,0:T(8,128)(2,1)}, u32[]{:S(2)}) copy-start(bf16[512,512]{1,0:T(8,128)(2,1)} %out_w_ref.5) | copy-start | bytes 1572868
  74.2 16.6 %all-to-all-start.2 = ((bf16[32,8,512]{2,1,0:T(8,128)(2,1)}), bf16[32,8,512]{2,1,0:T(8,128)(2,1)S(1)}, u32[]{:S(2)}, u32[]{:S(2)}) async-start(bf16[32,8,512]{2,1,0:T(8,128)(2,1)} %bitcast.20), calls=%async_computation.2 | async-start | bytes 524288 | tf_op jit(solution)/shard_map/all_to_all | solution.py:339
  78.7 12.0 %copy-start.8 = (bf16[512,512]{1,0:T(8,128)(2,1)S(1)}, bf16[512,512]{1,0:T(8,128)(2,1)}, u32[]{:S(2)}) copy-start(bf16[512,512]{1,0:T(8,128)(2,1)} %src_w_ref.7) | copy-start | bytes 1572868
  92.5 5.1 %collective-permute-start.2 = (bf16[256,512]{1,0:T(8,128)(2,1)S(1)}, bf16[256,512]{1,0:T(8,128)(2,1)S(1)}, u32[]{:S(2)}, u32[]{:S(2)}) collective-permute-start(bf16[256,512]{1,0:T(8,128)(2,1)S(1)} %get-tuple-element.24), channel_id=1, source_target_pairs={{0,1},{1,0},{2,3},{3,2},{4,5},{5,4},{6,7},{7,6},{8,9},{9,8},{10,11... | collective-permute-start | bytes 786440 | tf_op jit(solution)/shard_map/ppermute | solution.py:345

commit v9 on v8

--- a/solution.py
+++ b/solution.py
@@ -406,7 +406,7 @@
     info = jnp.stack([step_one, step_two, inside(band + step_one), inside(band - step_one), core])
 
     src_rows = call(
-        src_kernel, shape((2 * edges, latent), BF16), grid_latent, mate_pack, src_pick, cost=0,
+        src_kernel, shape((2 * edges, latent), BF16), grid_latent, mate_pack, src_pick,
     )
     partial, slope = call(
         enc_kernel,

time: 99.1 us -> 101 us (1.019)
  local copies, waits for them, and re-layouts: 3.92 us -> 5.97 us
  waiting for transfers between devices: 16.2 us -> 14.4 us
  blocking collectives: 30.5 us -> 32.3 us
    all_to_all x1, blocking collectives: 20.6 us -> 23 us  [exchange(): lax.all_to_all(values.reshape(chips, -1, latent), 'feat', split_axis=0, c...]
    unnamed x34 -> x36, local copies, waits for them, and re-layouts: 3.81 us -> 5.85 us
    all_to_all x2, waiting for transfers between devices: 14.9 us -> 13 us  [exchange(): lax.all_to_all(values.reshape(chips, -1, latent), 'feat', split_axis=0, c...]
where the time goes in v9:
time: 101 us; the launch traced here: 100 us
  blocking collectives  32.3 us (32%)
  starting transfers between devices  30 us (30%)
  Pallas kernels  16 us (16%)
  waiting for transfers between devices  14.4 us (14%)
  local copies, waits for them, and re-layouts  5.97 us (6%)
    all_to_all x1, blocking collectives, exchange(): lax.all_to_all(values.reshape(chips, -1, latent), 'feat', split_axis=0, c...  23 us
    pallas_call x10, Pallas kernels, call(): pl.pallas_call(body, out_shape=outs[0] if single else outs, in_specs=[pl....  16 us
    all_to_all x2, starting transfers between devices, exchange(): lax.all_to_all(values.reshape(chips, -1, latent), 'feat', split_axis=0, c...  13.9 us
    all_to_all x2, waiting for transfers between devices, exchange(): lax.all_to_all(values.reshape(chips, -1, latent), 'feat', split_axis=0, c...  13 us
    ppermute x2, starting transfers between devices, meet(): return lax.ppermute(values, ('band', 'feat'), pairs)  12.8 us
    all_gather x3, blocking collectives, both_cores(): lax.all_gather(values, 'feat', axis=0, tiled=True, axis_index_groups=[[i,...  9.25 us
    unnamed x36, local copies, waits for them, and re-layouts  5.85 us
    ppermute x1, starting transfers between devices, swap(): return lax.ppermute(values, 'feat', [(i, i ^ 1) for i in range(feats)])  3.28 us
  transfers between devices with their start and end apart: 5, of which 3 were waited for; matrix products, arithmetic and copies ran while one was open for 1% of the time, Pallas kernels for 5%

profile of v9, /device:TPU:137, one launch (start us, length us, event | category | flops | bytes accessed | tf_op | source)
XLA Modules:
  0.0 100.2 jit_solution(14063997944732885268)
XLA Ops:
  0.6 1.4 %shard_map.195 = bf16[256,512]{1,0:T(8,128)(2,1)} custom-call(bf16[8,512]{1,0:T(8,128)(2,1)} %mesh_ref.3), custom_call_target="tpu_custom_call" | custom-call | flops 4000000000 | bytes 4194304 | tf_op jit(solution)/shard_map/pallas_call | solution.py:62
  2.1 9.6 %all-to-all-start = ((bf16[32,8,512]{2,1,0:T(8,128)(2,1)}), bf16[32,8,512]{2,1,0:T(8,128)(2,1)S(1)}, u32[]{:S(2)}, u32[]{:S(2)}) async-start(bf16[32,8,512]{2,1,0:T(8,128)(2,1)} %bitcast.9), calls=%async_computation | async-start | bytes 524288 | tf_op jit(solution)/shard_map/all_to_all | solution.py:339
  11.7 1.1 %shard_map.193 = (bf16[272,512]{1,0:T(8,128)(2,1)S(1)}, bf16[16,512]{1,0:T(8,128)(2,1)S(1)}) custom-call(bf16[256,512]{1,0:T(8,128)(2,1)} %own_ref.1, bf16[8,512]{1,0:T(8,128)(2,1)} %cotangent_ref.1, s32[1,512]{1,0:T(1,128)} %bitcast.32, s32[1,512]{1,0:T(1,128)} %bitcast.29, s32[1,512]{1,0:T(1,128)} %bitcast.31, s32[1,256]{1,0:T(1,128)} %bitcast.36, ...), custom_call_target="tpu_custom_call" | custom-call | tf_op jit(solution)/shard_map/pallas_call | solution.py:62
  12.8 3.1 %all_gather.9 = bf16[544,512]{1,0:T(8,128)(2,1)S(1)} all-gather(bf16[272,512]{1,0:T(8,128)(2,1)S(1)} %get-tuple-element.15), channel_id=1, replica_groups={{0,1},{2,3},{4,5},{6,7},{8,9},{10,11},{12,13},{14,15},{16,17},{18,19},{..., dimensions={0}, use_global_device_ids=true | all-gather | bytes 835584 | tf_op jit(solution)/shard_map/all_gather | solution.py:364
  15.9 0.0 copy-start.15
  15.9 0.7 copy-done.16
  16.6 0.0 copy-done.15
  16.6 0.2 fusion.1.dst_ref
  16.8 0.1 fusion.2.dst_t_ref
  17.0 0.0 copy-start.17
  17.0 0.7 copy-done.17
  17.6 0.2 fusion.pick_ref
  17.9 0.0 copy-start
  17.9 0.9 copy-done
  18.8 0.4 shard_map.194.rows_ref
  19.3 0.0 copy-start.13
  19.3 1.0 copy-done.13
  20.2 3.0 %all-to-all-done = bf16[32,8,512]{2,1,0:T(8,128)(2,1)S(1)} async-done(((bf16[32,8,512]{2,1,0:T(8,128)(2,1)}), bf16[32,8,512]{2,1,0:T(8,128)(2,1)S(1)}, u32[]{:S(2)}, u32[]{:S(2)}) %all-to-all-start) | async-done | bytes 262176 | tf_op jit(solution)/shard_map/all_to_all | solution.py:339
  23.3 0.0 copy-done.4
  23.3 0.0 copy-done.6
  23.3 0.0 copy-done.9
  23.3 1.2 %copy-done.14 = bf16[1024,512]{1,0:T(8,128)(2,1)S(1)} copy-done((bf16[1024,512]{1,0:T(8,128)(2,1)S(1)}, bf16[1024,512]{1,0:T(8,128)(2,1)}, u32[]{:S(2)}) %copy-start.14) | copy-done | bytes 1048600
  24.5 2.6 %shard_map.196 = (bf16[32,16,512]{2,1,0:T(8,128)(2,1)S(1)}, bf16[1024,512]{1,0:T(8,128)(2,1)}) custom-call(bf16[1024,512]{1,0:T(8,128)(2,1)S(1)} %copy-done.14, bf16[1024,256]{1,0:T(8,128)(2,1)S(1)} %fusion.1.dst_ref, bf16[256,1024]{1,0:T(8,128)(2,1)S(1)} %fusion.2.dst_t_ref, bf16[256,512]{1,0:T(8,128)(2,1)S(1)} %bitcast.22, bf16[512,512]{1,0:T(8,128)(2,1)S(1)} %copy-done.6, ...), custom_call_target="tpu_custom_call" | custom-call | flops 4000000000 | bytes 4194304 | tf_op jit(solution)/shard_map/pallas_call | solution.py:62
  27.1 0.0 copy-start.5
  27.1 0.0 copy-start.8
  27.2 23.0 %all_to_all.15.parts_ref = bf16[32,16,512]{2,1,0:T(8,128)(2,1)S(1)} all-to-all(bf16[32,16,512]{2,1,0:T(8,128)(2,1)S(1)} %get-tuple-element.16), channel_id=1, replica_groups={{0,2,4,6,8,10,12,14,16,18,20,22,24,26,28,30,32,34,36,38,40,42,44,46,48,..., dimensions={0} | all-to-all | bytes 1048576 | tf_op jit(solution)/shard_map/all_to_all | solution.py:339
  50.2 0.7 copy-done.10
  50.9 0.4 shard_map.197
  51.3 4.2 %all_gather.10 = bf16[48,512]{1,0:T(8,128)(2,1)S(1)} all-gather(bf16[24,512]{1,0:T(8,128)(2,1)S(1)} %get-tuple-element.18.own_ref), channel_id=1, replica_groups={{0,1},{2,3},{4,5},{6,7},{8,9},{10,11},{12,13},{14,15},{16,17},{18,19},{..., dimensions={0}, use_global_device_ids=true | all-gather | bytes 73728 | tf_op jit(solution)/shard_map/all_gather | solution.py:364
  55.5 3.3 %collective-permute-start = (bf16[48,512]{1,0:T(8,128)(2,1)S(1)}, bf16[48,512]{1,0:T(8,128)(2,1)S(1)}, u32[]{:S(2)}, u32[]{:S(2)}) collective-permute-start(bf16[48,512]{1,0:T(8,128)(2,1)S(1)} %all_gather.10), channel_id=1, source_target_pairs={{0,64},{64,0},{128,192},{192,128},{256,320},{320,256},{384,448},{4... | collective-permute-start | bytes 147464 | tf_op jit(solution)/shard_map/ppermute | solution.py:361
  58.8 9.5 %collective-permute-start.1 = (bf16[48,512]{1,0:T(8,128)(2,1)S(1)}, bf16[48,512]{1,0:T(8,128)(2,1)S(1)}, u32[]{:S(2)}, u32[]{:S(2)}) collective-permute-start(bf16[48,512]{1,0:T(8,128)(2,1)S(1)} %all_gather.10), channel_id=1, source_target_pairs={{64,128},{128,64},{192,256},{256,192},{320,384},{384,320},{448,512... | collective-permute-start | bytes 147464 | tf_op jit(solution)/shard_map/ppermute | solution.py:361
  68.4 0.1 stack.31.info_ref
  68.5 0.0 collective-permute-done
  68.5 1.3 %collective-permute-done.1 = bf16[48,512]{1,0:T(8,128)(2,1)S(1)} collective-permute-done((bf16[48,512]{1,0:T(8,128)(2,1)S(1)}, bf16[48,512]{1,0:T(8,128)(2,1)S(1)}, u32[]{:S(2)}, u32[]{:S(2)}) %collective-permute-start.1) | collective-permute-done | bytes 49184 | tf_op jit(solution)/shard_map/ppermute | solution.py:361
  69.8 1.9 %all_gather.11.halo_ref = bf16[192,512]{1,0:T(8,128)(2,1)S(1)} all-gather(bf16[96,512]{1,0:T(8,128)(2,1)S(1)} %pad_maximum_fusion), channel_id=1, replica_groups={{0,1},{2,3},{4,5},{6,7},{8,9},{10,11},{12,13},{14,15},{16,17},{18,19},{..., dimensions={0}, use_global_device_ids=true | all-gather | bytes 294912 | tf_op jit(solution)/shard_map/all_gather | solution.py:364
  71.8 0.0 copy-done.1
  71.8 0.7 copy-done.11
  72.5 3.7 %shard_map.198 = (bf16[8,512]{1,0:T(8,128)(2,1)}, f32[8,512]{1,0:T(8,128)S(1)}, bf16[256,512]{1,0:T(8,128)(2,1)}) custom-call(bf16[192,512]{1,0:T(8,128)(2,1)S(1)} %all_gather.11.halo_ref, bf16[24,512]{1,0:T(8,128)(2,1)S(1)} %get-tuple-element.18.own_ref, s32[5]{0:T(128)S(1)} %stack.31.info_ref, bf16[512,512]{1,0:T(8,128)(2,1)S(1)} %copy-done.1, ...), custom_call_target="tpu_custom_call" | custom-call | flops 4000000000 | bytes 4194304 | tf_op jit(solution)/shard_map/pallas_call | solution.py:62
  76.2 4.3 %all-to-all-start.2 = ((bf16[32,8,512]{2,1,0:T(8,128)(2,1)}), bf16[32,8,512]{2,1,0:T(8,128)(2,1)S(1)}, u32[]{:S(2)}, u32[]{:S(2)}) async-start(bf16[32,8,512]{2,1,0:T(8,128)(2,1)} %bitcast.20), calls=%async_computation.2 | async-start | bytes 524288 | tf_op jit(solution)/shard_map/all_to_all | solution.py:339
  80.5 0.1 fusion.3.pick_t_ref
  80.6 0.0 copy-start.7
  80.6 2.0 %shard_map.202 = bf16[8,512]{1,0:T(8,128)(2,1)} custom-call(bf16[256,512]{1,0:T(8,128)(2,1)} %get-tuple-element.21.tiled_ref, f32[8,512]{1,0:T(8,128)S(1)} %get-tuple-element.25.slopes_ref, f32[8,512]{1,0:T(8,128)S(1)} %get-tuple-element.26.grad_ref, bf16[512,512]{1,0:T(8,128)(2,1)S(1)} %copy-done.5, bf16[512,512]{1,0:T(8,128)(2,1)S(1)} %copy-done.4), custom_call_target="tpu_custom_call" | custom-call | flops 4000000000 | bytes 4194304 | tf_op jit(solution)/shard_map/pallas_call | solution.py:62
  82.7 10.0 %all-to-all-done.2 = bf16[32,8,512]{2,1,0:T(8,128)(2,1)S(1)} async-done(((bf16[32,8,512]{2,1,0:T(8,128)(2,1)}), bf16[32,8,512]{2,1,0:T(8,128)(2,1)S(1)}, u32[]{:S(2)}, u32[]{:S(2)}) %all-to-all-start.2) | async-done | bytes 262176 | tf_op jit(solution)/shard_map/all_to_all | solution.py:339
  92.7 1.7 %shard_map.199 = (bf16[512,512]{1,0:T(8,128)(2,1)S(1)}, bf16[256,512]{1,0:T(8,128)(2,1)S(1)}) custom-call(bf16[256,512]{1,0:T(8,128)(2,1)S(1)} %bitcast.23, bf16[1024,256]{1,0:T(8,128)(2,1)S(1)} %fusion.1.dst_ref, bf16[256,1024]{1,0:T(8,128)(2,1)S(1)} %fusion.3.pick_t_ref, bf16[1024,512]{1,0:T(8,128)(2,1)} %get-tuple-element.22.slope_ref, ...), custom_call_target="tpu_custom_call" | custom-call | flops 4000000000 | bytes 4194304 | tf_op jit(solution)/shard_map/pallas_call | solution.py:62
  94.4 3.3 %collective-permute-start.2 = (bf16[256,512]{1,0:T(8,128)(2,1)S(1)}, bf16[256,512]{1,0:T(8,128)(2,1)S(1)}, u32[]{:S(2)}, u32[]{:S(2)}) collective-permute-start(bf16[256,512]{1,0:T(8,128)(2,1)S(1)} %get-tuple-element.24), channel_id=1, source_target_pairs={{0,1},{1,0},{2,3},{3,2},{4,5},{5,4},{6,7},{7,6},{8,9},{9,8},{10,11... | collective-permute-start | bytes 786440 | tf_op jit(solution)/shard_map/ppermute | solution.py:345
  97.7 1.8 %shard_map.200.own_ref = f32[256,512]{1,0:T(8,128)S(1)} custom-call(bf16[512,512]{1,0:T(8,128)(2,1)S(1)} %get-tuple-element.23.table_ref, bf16[1024,256]{1,0:T(8,128)(2,1)S(1)} %fusion.1.dst_ref, bf16[256,1024]{1,0:T(8,128)(2,1)S(1)} %fusion.3.pick_t_ref, bf16[1024,512]{1,0:T(8,128)(2,1)} %get-tuple-element.22.slope_ref, bf16[512,512]{1,0:T(8,128)(2,1)S(1)} %copy-done.7), custom_call_target="tpu_custom_call" | custom-call | flops 4000000000 | bytes 4194304 | tf_op jit(solution)/shard_map/pallas_call | solution.py:62
  99.5 0.0 collective-permute-done.2.mate_ref
  99.5 0.7 shard_map.201
  (23 shorter events, 0.1 us)
Async XLA Ops:
  2.1 21.2 %all-to-all-start = ((bf16[32,8,512]{2,1,0:T(8,128)(2,1)}), bf16[32,8,512]{2,1,0:T(8,128)(2,1)S(1)}, u32[]{:S(2)}, u32[]{:S(2)}) async-start(bf16[32,8,512]{2,1,0:T(8,128)(2,1)} %bitcast.9), calls=%async_computation | async-start | bytes 524288 | tf_op jit(solution)/shard_map/all_to_all | solution.py:339
  15.9 0.7 copy-start.16
  15.9 0.7 copy-start.15
  17.0 0.7 copy-start.17
  17.9 1.0 copy-start
  18.8 4.5 %copy-start.4 = (bf16[512,512]{1,0:T(8,128)(2,1)S(1)}, bf16[512,512]{1,0:T(8,128)(2,1)}, u32[]{:S(2)}) copy-start(bf16[512,512]{1,0:T(8,128)(2,1)} %dst_w_ref.5) | copy-start | bytes 1572868
  18.8 4.5 %copy-start.6 = (bf16[512,512]{1,0:T(8,128)(2,1)S(1)}, bf16[512,512]{1,0:T(8,128)(2,1)}, u32[]{:S(2)}) copy-start(bf16[512,512]{1,0:T(8,128)(2,1)} %src_w_ref.7) | copy-start | bytes 1572868
  19.3 1.0 copy-start.13
  20.2 3.0 %copy-start.9 = (f32[512]{0:T(512)S(1)}, f32[512]{0:T(512)}, u32[]{:S(2)}) copy-start(f32[512]{0:T(512)} %param.28) | copy-start | bytes 6148
  23.3 1.2 %copy-start.14 = (bf16[1024,512]{1,0:T(8,128)(2,1)S(1)}, bf16[1024,512]{1,0:T(8,128)(2,1)}, u32[]{:S(2)}) copy-start(bf16[1024,512]{1,0:T(8,128)(2,1)} %copy-done.13) | copy-start | bytes 3145732
  27.1 23.1 %copy-start.5 = (bf16[512,512]{1,0:T(8,128)(2,1)S(1)}, bf16[512,512]{1,0:T(8,128)(2,1)}, u32[]{:S(2)}) copy-start(bf16[512,512]{1,0:T(8,128)(2,1)} %out_w_ref.5) | copy-start | bytes 1572868
  27.1 23.1 %copy-start.8 = (bf16[8,512]{1,0:T(8,128)(2,1)S(1)}, bf16[8,512]{1,0:T(8,128)(2,1)}, u32[]{:S(2)}) copy-start(bf16[8,512]{1,0:T(8,128)(2,1)} %mesh_ref.3) | copy-start | bytes 24580
  50.2 0.7 copy-start.10
  50.9 20.9 %copy-start.2 = (bf16[512,512]{1,0:T(8,128)(2,1)S(1)}, bf16[512,512]{1,0:T(8,128)(2,1)}, u32[]{:S(2)}) copy-start(bf16[512,512]{1,0:T(8,128)(2,1)} %dst_w_ref.4) | copy-start | bytes 1572868
  50.9 20.9 %copy-start.3 = (bf16[512,512]{1,0:T(8,128)(2,1)S(1)}, bf16[512,512]{1,0:T(8,128)(2,1)}, u32[]{:S(2)}) copy-start(bf16[512,512]{1,0:T(8,128)(2,1)} %out_w_ref.3) | copy-start | bytes 1572868
  50.9 20.9 %copy-start.12 = (f32[512]{0:T(512)S(1)}, f32[512]{0:T(512)}, u32[]{:S(2)}) copy-start(f32[512]{0:T(512)} %param.34) | copy-start | bytes 6148
  51.3 20.5 %copy-start.1 = (bf16[512,512]{1,0:T(8,128)(2,1)S(1)}, bf16[512,512]{1,0:T(8,128)(2,1)}, u32[]{:S(2)}) copy-start(bf16[512,512]{1,0:T(8,128)(2,1)} %src_w_ref.5) | copy-start | bytes 1572868
  55.5 13.0 %collective-permute-start = (bf16[48,512]{1,0:T(8,128)(2,1)S(1)}, bf16[48,512]{1,0:T(8,128)(2,1)S(1)}, u32[]{:S(2)}, u32[]{:S(2)}) collective-permute-start(bf16[48,512]{1,0:T(8,128)(2,1)S(1)} %all_gather.10), channel_id=1, source_target_pairs={{0,64},{64,0},{128,192},{192,128},{256,320},{320,256},{384,448},{4... | collective-permute-start | bytes 147464 | tf_op jit(solution)/shard_map/ppermute | solution.py:361
  58.8 11.0 %collective-permute-start.1 = (bf16[48,512]{1,0:T(8,128)(2,1)S(1)}, bf16[48,512]{1,0:T(8,128)(2,1)S(1)}, u32[]{:S(2)}, u32[]{:S(2)}) collective-permute-start(bf16[48,512]{1,0:T(8,128)(2,1)S(1)} %all_gather.10), channel_id=1, source_target_pairs={{64,128},{128,64},{192,256},{256,192},{320,384},{384,320},{448,512... | collective-permute-start | bytes 147464 | tf_op jit(solution)/shard_map/ppermute | solution.py:361
  71.8 0.7 copy-start.11
  76.2 16.4 %all-to-all-start.2 = ((bf16[32,8,512]{2,1,0:T(8,128)(2,1)}), bf16[32,8,512]{2,1,0:T(8,128)(2,1)S(1)}, u32[]{:S(2)}, u32[]{:S(2)}) async-start(bf16[32,8,512]{2,1,0:T(8,128)(2,1)} %bitcast.20), calls=%async_computation.2 | async-start | bytes 524288 | tf_op jit(solution)/shard_map/all_to_all | solution.py:339
  80.6 12.0 %copy-start.7 = (bf16[512,512]{1,0:T(8,128)(2,1)S(1)}, bf16[512,512]{1,0:T(8,128)(2,1)}, u32[]{:S(2)}) copy-start(bf16[512,512]{1,0:T(8,128)(2,1)} %src_w_ref.7) | copy-start | bytes 1572868
  94.4 5.1 %collective-permute-start.2 = (bf16[256,512]{1,0:T(8,128)(2,1)S(1)}, bf16[256,512]{1,0:T(8,128)(2,1)S(1)}, u32[]{:S(2)}, u32[]{:S(2)}) collective-permute-start(bf16[256,512]{1,0:T(8,128)(2,1)S(1)} %get-tuple-element.24), channel_id=1, source_target_pairs={{0,1},{1,0},{2,3},{3,2},{4,5},{5,4},{6,7},{7,6},{8,9},{9,8},{10,11... | collective-permute-start | bytes 786440 | tf_op jit(solution)/shard_map/ppermute | solution.py:345
